TPU v7x, 512 devices: a whole 4x8x8 slice. The times are simulated.
512 devices in a mesh: dp: 8 (over x, core), space: 16 (over y, z_hi), mp: 4 (over z_lo).
Axes of the slice: x: 4, y: 8, z: 8 (z_hi: 2, z_lo: 4; z = z_hi * 4 + z_lo), core: 2. Of those that a mesh axis runs over, the one named last changes fastest.
Arguments:
- teacher_tokens: bfloat16 [64, 16, 16, 16, 1408], P('dp', 'space'), parts along dimension 0, may hold values from -16 to 16
- student_tokens: bfloat16 [64, 16, 16, 16, 1280], P('dp', 'space'), parts along dimension 0, may hold values from -16 to 16
- teacher_head: bfloat16 [11264, 1000], P(('dp', 'space'), 'mp'), parts along dimension 0, may hold values from -1 to 1
- student_head: bfloat16 [10240, 1000], P(('dp', 'space'), 'mp'), parts along dimension 0, may hold values from -1 to 1
- valid: int32 [64, 16, 16, 16], P('dp', 'space'), parts along dimension 0, may hold values from 0 to 1, as said below
Outputs:
- patch_kl: float32 [64, 16, 16, 16], P('dp', 'space'), parts along dimension 0
- image_loss: float32 [64], P('dp'), parts along dimension 0
There are 8 independent parts, one for each index of `dp`. A program takes and returns all parts, laid end to end along the dimension named above; each array names one. Nothing has to cross between parts.
Inputs may be any that keep to these rules, and one draw needn't show every extreme that they name: An image may have no valid patch.
All inputs are finite; a program needn't handle non-finite values.
Results may differ from a plain program's by a relative error of at most 0.0003.
Values may be sent and summed in bfloat16 or wider, within the bound.
No kernel may reach another device: no remote copies, remote signals or barrier semaphores. Data moves between devices by JAX's collectives and lax.ppermute only.
A program may use at most 64 MiB of HBM per device.

v0:
```python
import math

import jax
import jax.numpy as jnp
from jax import lax
from jax.sharding import PartitionSpec as P


def shifted(block, axis, distance):
    devices = range(lax.axis_size(axis))
    route = [(i - distance, i) for i in devices if i - distance in devices]
    return lax.ppermute(block, axis, route)


def in_order(pieces, dim):
    lengths = list(pieces.shape[1:])
    lengths[dim] *= pieces.shape[0]
    return jnp.moveaxis(pieces, 0, dim).reshape(lengths)


def from_everyone(x, axis):
    copies = jnp.broadcast_to(x, (lax.axis_size(axis), *x.shape))
    return lax.all_to_all(copies, axis, split_axis=0, concat_axis=0, tiled=True)


def collect(x, axis, dim):
    return in_order(from_everyone(x, axis), dim)


def taken_together(x, axis):
    return from_everyone(x, axis).max(axis=0)


def packed_total(arrays, axis):
    ends = [0]
    for a in arrays:
        ends.append(ends[-1] + a.size)
    running = taken_together(jnp.concatenate([a.ravel() for a in arrays]), axis)
    return tuple((running[b:e].reshape(a.shape) for a, b, e in zip(arrays, ends, ends[1:])))


def taken_together_2(x, axis):
    everything = from_everyone(x, axis)
    return jnp.sum(everything, axis=0)


def packed_total_2(arrays, axis):
    ravelled, at, done = (jnp.concatenate([a.reshape(-1) for a in arrays]), 0, [])
    running = taken_together_2(ravelled, axis)
    for a in arrays:
        done.append(running[at : at + a.size].reshape(a.shape))
        at += a.size
    return tuple(done)


def logit_move(values, offset):
    return shifted(values, "space", offset)


def extend(values, mover, side, column):
    left = mover(values[:, :, -1:, :], 1)
    left = jnp.where(column > 0, left, jnp.zeros_like(left))
    right = mover(values[:, :, :1, :], -1)
    right = jnp.where(column < side - 1, right, jnp.zeros_like(right))
    wide = jnp.concatenate([left, values, right], axis=2)
    upper = mover(wide[:, -1:, :, :], side)
    lower = mover(wide[:, :1, :, :], -side)
    return jnp.concatenate([upper, wide, lower], axis=1)


def body(teacher_tokens, student_tokens, teacher_head, student_head, valid):
    side = math.isqrt(lax.axis_size("space"))
    tile_index = lax.axis_index("space")
    tile_row = tile_index // side
    tile_column = tile_index % side
    teacher_tile = teacher_tokens[:, 0]
    student_tile = student_tokens[:, 0]
    images, edge = (teacher_tile.shape[0], teacher_tile.shape[1])
    classes_here = teacher_head.shape[1]
    source_flat = teacher_tile.reshape(-1, teacher_tile.shape[-1])
    student_flat = student_tile.reshape(-1, student_tile.shape[-1])
    teacher_logits = jnp.dot(
        source_flat, collect(teacher_head, "space", 0), preferred_element_type=jnp.float32
    )
    student_logits = jnp.dot(
        student_flat, collect(student_head, "space", 0), preferred_element_type=jnp.float32
    )
    teacher_wide = extend(
        teacher_logits.reshape(images, edge, edge, classes_here), logit_move, side, tile_column
    )
    extent = side * edge
    total = jnp.zeros((images, edge, edge, classes_here), jnp.float32)
    for shift_y in range(3):
        for shift_x in range(3):
            total = total + teacher_wide[:, shift_y : shift_y + edge, shift_x : shift_x + edge, :]
    places_y = tile_row * edge + jnp.arange(edge)
    places_x = tile_column * edge + jnp.arange(edge)
    line_y = 1.0 + (places_y > 0).astype(jnp.float32) + (places_y < extent - 1).astype(jnp.float32)
    line_x = 1.0 + (places_x > 0).astype(jnp.float32) + (places_x < extent - 1).astype(jnp.float32)
    counts = line_y[:, None] * line_x[None, :]
    smoothed = total / counts[None, :, :, None]
    student = student_logits.reshape(images, edge, edge, classes_here)
    top_t, top_s = packed_total((jnp.max(smoothed, axis=-1), jnp.max(student, axis=-1)), "mp")
    expo_t = jnp.exp(smoothed - top_t[..., None])
    sum_t, weighted, sum_s = packed_total_2(
        (
            jnp.sum(expo_t, axis=-1),
            jnp.sum(expo_t * (smoothed - student), axis=-1),
            jnp.sum(jnp.exp(student - top_s[..., None]), axis=-1),
        ),
        "mp",
    )
    divergence = weighted / sum_t - top_t - jnp.log(sum_t) + top_s + jnp.log(sum_s)
    weights = valid[:, 0].astype(jnp.float32)
    totals, numbers = packed_total_2(
        (jnp.sum(divergence * weights, axis=(1, 2)), jnp.sum(weights, axis=(1, 2))), "space"
    )
    image_loss = totals / jnp.maximum(numbers, 1.0)
    return (divergence[:, None], image_loss)


def solution(mesh):
    in_specs = (
        P("dp", "space", None, None, None),
        P("dp", "space", None, None, None),
        P(("dp", "space"), "mp"),
        P(("dp", "space"), "mp"),
        P("dp", "space", None, None),
    )
    out_specs = (P("dp", "space", None, None), P("dp"))
    return jax.shard_map(body, mesh=mesh, in_specs=in_specs, out_specs=out_specs, check_vma=False)
```

profile of v0, /device:TPU:6, one launch (start us, length us, event | category | flops | bytes accessed | tf_op | source)
XLA Modules:
  0.0 154.9 jit_solution(3335413444702096625)
XLA Ops:
  0.6 1.7 %broadcast_in_dim.19 = bf16[16,88,250]{2,1,0:T(8,128)(2,1)} broadcast(bf16[88,250]{1,0:T(8,128)(2,1)} %param.7), dimensions={1,2} | broadcast | bytes 748000 | tf_op jit(solution)/shard_map/broadcast_in_dim | solution.py:22
  2.3 15.6 %all-to-all-start = ((bf16[16,88,250]{2,1,0:T(8,128)(2,1)}), bf16[16,88,250]{2,1,0:T(8,128)(2,1)S(1)}, u32[]{:S(2)}, u32[]{:S(2)}) async-start(bf16[16,88,250]{2,1,0:T(8,128)(2,1)} %broadcast_in_dim.19), calls=%async_computation | async-start | bytes 1441792 | tf_op jit(solution)/shard_map/all_to_all | solution.py:23
  18.0 27.1 %all-to-all-done = bf16[16,88,250]{2,1,0:T(8,128)(2,1)S(1)} async-done(((bf16[16,88,250]{2,1,0:T(8,128)(2,1)}), bf16[16,88,250]{2,1,0:T(8,128)(2,1)S(1)}, u32[]{:S(2)}, u32[]{:S(2)}) %all-to-all-start) | async-done | bytes 704032 | tf_op jit(solution)/shard_map/all_to_all | solution.py:23
  45.1 0.9 broadcast_in_dim.20
  46.0 8.1 %all-to-all-start.1 = ((bf16[16,80,250]{2,1,0:T(8,128)(2,1)}), bf16[16,80,250]{2,1,0:T(8,128)(2,1)S(1)}, u32[]{:S(2)}, u32[]{:S(2)}) async-start(bf16[16,80,250]{2,1,0:T(8,128)(2,1)} %broadcast_in_dim.20), calls=%async_computation.1 | async-start | bytes 1310720 | tf_op jit(solution)/shard_map/all_to_all | solution.py:23
  54.1 4.5 %fusion = f32[8,16,16,250]{3,2,1,0:T(8,128)S(1)} fusion(bf16[1408,250,1,1]{1,0,3,2:T(8,128)(2,1)S(1)} %bitcast.25, bf16[8,1,16,16,1408]{4,3,2,1,0:T(8,128)(2,1)} %param.5), kind=kOutput, calls=%fused_computation | convolution fusion | flops 1441792000 | bytes 8519168 | tf_op jit(solution)/shard_map/dot_general | solution.py:82
  58.6 0.2 fusion.16
  58.8 1.3 collective-permute-start.1
  60.1 0.1 broadcast_multiply_fusion
  60.2 8.5 %collective-permute-start = (f32[8,16,1,250]{3,2,1,0:T(1,128)S(1)}, f32[8,16,1,250]{3,2,1,0:T(1,128)S(1)}, u32[]{:S(2)}, u32[]{:S(2)}) collective-permute-start(f32[8,16,1,250]{3,2,1,0:T(1,128)S(1)} %get-tuple-element.13), channel_id=1, source_target_pairs={{0,4},{4,8},{8,12},{12,16},{16,20},{20,24},{24,28},{28,32},{32,36}... | collective-permute-start | bytes 384008 | tf_op jit(solution)/shard_map/ppermute | solution.py:12
  68.6 14.2 %collective-permute-done.1 = f32[8,16,1,250]{3,2,1,0:T(1,128)S(1)} collective-permute-done((f32[8,16,1,250]{3,2,1,0:T(1,128)S(1)}, f32[8,16,1,250]{3,2,1,0:T(1,128)S(1)}, u32[]{:S(2)}, u32[]{:S(2)}) %collective-permute-start.1) | collective-permute-done | bytes 128032 | tf_op jit(solution)/shard_map/ppermute | solution.py:12
  82.9 0.1 broadcast_select_fusion
  83.0 0.0 collective-permute-done
  83.0 0.1 broadcast_select_fusion.1
  83.1 0.8 pad_maximum_fusion.5
  83.9 8.1 %collective-permute-start.2 = (f32[8,1,18,250]{3,2,1,0:T(8,128)}, f32[8,1,18,250]{3,2,1,0:T(8,128)S(1)}, u32[]{:S(2)}, u32[]{:S(2)}) collective-permute-start(f32[8,1,18,250]{3,2,1,0:T(8,128)} %get-tuple-element.11), channel_id=1, source_target_pairs={{0,16},{4,20},{8,24},{12,28},{16,32},{20,36},{24,40},{28,44},{32,4... | collective-permute-start | bytes 432008 | tf_op jit(solution)/shard_map/ppermute | solution.py:12
  92.0 1.3 collective-permute-start.3
  93.3 0.0 all-to-all-done.1
  93.3 5.4 %fusion.18 = (f32[8,16,16]{2,1,0:T(8,128)S(1)}, f32[8,16,16,250]{3,2,1,0:T(8,128)}) fusion(bf16[1280,250,1,1]{1,0,3,2:T(8,128)(2,1)S(1)} %bitcast.26, bf16[8,1,16,16,1280]{4,3,2,1,0:T(8,128)(2,1)} %param.6), kind=kOutput, calls=%fused_computation.49 | convolution fusion | flops 1311229952 | bytes 7939072 | tf_op jit(solution)/shard_map/dot_general | solution.py:85
  98.7 0.1 reshape.261
  98.8 7.4 %collective-permute-done.3 = f32[8,1,18,250]{3,2,1,0:T(8,128)} collective-permute-done((f32[8,1,18,250]{3,2,1,0:T(8,128)S(1)}, f32[8,1,18,250]{3,2,1,0:T(8,128)}, u32[]{:S(2)}, u32[]{:S(2)}) %collective-permute-start.3) | collective-permute-done | bytes 144032 | tf_op jit(solution)/shard_map/ppermute | solution.py:12
  106.1 2.2 %maximum_maximum_fusion = (f32[8,17,18,250]{3,2,1,0:T(8,128)S(1)}, f32[8,17,18,250]{3,2,1,0:T(8,128)S(1)}) fusion(f32[8,16,1,250]{3,2,1,0:T(1,128)S(1)} %broadcast_select_fusion, f32[8,16,16,250]{3,2,1,0:T(8,128)S(1)} %fusion, f32[8,16,1,250]{3,2,1,0:T(1,128)S(1)} %broadcast_select_fusion.1, f32[8,1,18,250]{3,2,1,0:T(8,128)S(1)} %collective-permute-done.2, ...), kind=kLoop, calls=%fused_computation.4 | loop fusion | flops 3672000 | bytes 7488000 | tf_op jit(solution)/shard_map/concatenate | solution.py:68
  108.4 3.1 %fusion.14 = (f32[8,16,16]{2,1,0:T(8,128)S(1)}, f32[8,16,16,250]{3,2,1,0:T(8,128)}) fusion(f32[16,16]{1,0:T(8,128)S(1)} %broadcast_multiply_fusion, f32[8,17,18,250]{3,2,1,0:T(8,128)S(1)} %get-tuple-element.10, f32[8,16,1,250]{3,2,1,0:T(1,128)S(1)} %broadcast_select_fusion, f32[8,16,16,250]{3,2,1,0:T(8,128)S(1)} %fusion, ...), kind=kLoop, calls=%fused_computation.46 | loop fusion | flops 6141952 | bytes 16649216 | tf_op jit(solution)/shard_map/reduce_max | solution.py:103
  111.4 0.1 reshape.259
  111.6 8.1 %all_to_all.28 = f32[4,1,4096]{2,1,0:T(1,128)S(1)} all-to-all(f32[4,1,4096]{2,1,0:T(1,128)S(1)} %broadcast_in_dim.21), channel_id=1, replica_groups=mesh['dp'=8,'space'=16,'mp'=4] {'mp'}, dimensions={0} | all-to-all | bytes 131072 | tf_op jit(solution)/shard_map/all_to_all | solution.py:23
  119.7 0.1 reduce_max.29
  119.7 0.1 sub.54
  119.8 0.1 sub.58
  119.9 0.0 copy-start
  119.9 3.4 %fusion.8 = (f32[8,16,16]{2,1,0:T(8,128)S(1)}, f32[8,16,16]{2,1,0:T(8,128)S(1)}, f32[8,16,16]{2,1,0:T(8,128)S(1)}) fusion(f32[8,16,16,250]{3,2,1,0:T(8,128)} %get-tuple-element.8, f32[8,16,16]{2,1,0:T(8,128)S(1)} %sub.54, f32[8,16,16,250]{3,2,1,0:T(8,128)} %get-tuple-element.20, f32[8,16,16]{2,1,0:T(8,128)S(1)} %sub.58), kind=kLoop, calls=%fused_computation.20 | loop fusion | flops 3577856 | bytes 4136960 | tf_op jit(solution)/shard_map/reduce_sum | solution.py:107
  123.3 0.1 reshape.262
  123.4 0.1 reshape.263
  123.5 0.1 reshape.264
  123.6 0.7 broadcast_in_dim.22
  124.3 3.3 %all-to-all-start.3 = ((f32[4,1,6144]{2,1,0:T(1,128)}), f32[4,1,6144]{2,1,0:T(1,128)S(1)}, u32[]{:S(2)}, u32[]{:S(2)}) async-start(f32[4,1,6144]{2,1,0:T(1,128)} %broadcast_in_dim.22), calls=%async_computation.3 | async-start | bytes 196608 | tf_op jit(solution)/shard_map/all_to_all | solution.py:23
  127.6 0.1 convert_reduce_fusion
  127.7 5.6 %all-to-all-done.3 = f32[4,1,6144]{2,1,0:T(1,128)S(1)} async-done(((f32[4,1,6144]{2,1,0:T(1,128)}), f32[4,1,6144]{2,1,0:T(1,128)S(1)}, u32[]{:S(2)}, u32[]{:S(2)}) %all-to-all-start.3) | async-done | bytes 98336 | tf_op jit(solution)/shard_map/all_to_all | solution.py:23
  133.4 0.1 reduce_sum.66
  133.5 0.1 div.39
  133.6 0.1 log.33
  133.6 0.1 log.34
  133.7 0.2 fusion.9
  133.9 0.1 pad_maximum_fusion.8
  134.0 0.6 broadcast_in_dim.23
  134.6 7.3 %all-to-all-start.4 = ((f32[16,1,16]{2,1,0:T(1,128)}), f32[16,1,16]{2,1,0:T(1,128)S(1)}, u32[]{:S(2)}, u32[]{:S(2)}) async-start(f32[16,1,16]{2,1,0:T(1,128)} %broadcast_in_dim.23), calls=%async_computation.4 | async-start | bytes 16384 | tf_op jit(solution)/shard_map/all_to_all | solution.py:23
  141.9 0.7 reshape.265
  142.6 11.7 %all-to-all-done.4 = f32[16,1,16]{2,1,0:T(1,128)S(1)} async-done(((f32[16,1,16]{2,1,0:T(1,128)}), f32[16,1,16]{2,1,0:T(1,128)S(1)}, u32[]{:S(2)}, u32[]{:S(2)}) %all-to-all-start.4) | async-done | bytes 1056 | tf_op jit(solution)/shard_map/all_to_all | solution.py:23
  154.3 0.6 maximum_divide_fusion
  (11 shorter events, 0.1 us)
Async XLA Ops:
  0.6 44.5 %copy-start.1 = (bf16[80,250]{1,0:T(8,128)(2,1)S(1)}, bf16[80,250]{1,0:T(8,128)(2,1)}, u32[]{:S(2)}) copy-start(bf16[80,250]{1,0:T(8,128)(2,1)} %param.8) | copy-start | bytes 120004
  2.3 42.8 %all-to-all-start = ((bf16[16,88,250]{2,1,0:T(8,128)(2,1)}), bf16[16,88,250]{2,1,0:T(8,128)(2,1)S(1)}, u32[]{:S(2)}, u32[]{:S(2)}) async-start(bf16[16,88,250]{2,1,0:T(8,128)(2,1)} %broadcast_in_dim.19), calls=%async_computation | async-start | bytes 1441792 | tf_op jit(solution)/shard_map/all_to_all | solution.py:23
  46.0 47.3 %all-to-all-start.1 = ((bf16[16,80,250]{2,1,0:T(8,128)(2,1)}), bf16[16,80,250]{2,1,0:T(8,128)(2,1)S(1)}, u32[]{:S(2)}, u32[]{:S(2)}) async-start(bf16[16,80,250]{2,1,0:T(8,128)(2,1)} %broadcast_in_dim.20), calls=%async_computation.1 | async-start | bytes 1310720 | tf_op jit(solution)/shard_map/all_to_all | solution.py:23
  58.8 24.0 %collective-permute-start.1 = (f32[8,16,1,250]{3,2,1,0:T(1,128)S(1)}, f32[8,16,1,250]{3,2,1,0:T(1,128)S(1)}, u32[]{:S(2)}, u32[]{:S(2)}) collective-permute-start(f32[8,16,1,250]{3,2,1,0:T(1,128)S(1)} %get-tuple-element.14), channel_id=1, source_target_pairs={{4,0},{8,4},{12,8},{16,12},{20,16},{24,20},{28,24},{32,28},{36,32}... | collective-permute-start | bytes 384008 | tf_op jit(solution)/shard_map/ppermute | solution.py:12
  60.2 22.8 %collective-permute-start = (f32[8,16,1,250]{3,2,1,0:T(1,128)S(1)}, f32[8,16,1,250]{3,2,1,0:T(1,128)S(1)}, u32[]{:S(2)}, u32[]{:S(2)}) collective-permute-start(f32[8,16,1,250]{3,2,1,0:T(1,128)S(1)} %get-tuple-element.13), channel_id=1, source_target_pairs={{0,4},{4,8},{8,12},{12,16},{16,20},{20,24},{24,28},{28,32},{32,36}... | collective-permute-start | bytes 384008 | tf_op jit(solution)/shard_map/ppermute | solution.py:12
  83.9 14.9 %collective-permute-start.2 = (f32[8,1,18,250]{3,2,1,0:T(8,128)}, f32[8,1,18,250]{3,2,1,0:T(8,128)S(1)}, u32[]{:S(2)}, u32[]{:S(2)}) collective-permute-start(f32[8,1,18,250]{3,2,1,0:T(8,128)} %get-tuple-element.11), channel_id=1, source_target_pairs={{0,16},{4,20},{8,24},{12,28},{16,32},{20,36},{24,40},{28,44},{32,4... | collective-permute-start | bytes 432008 | tf_op jit(solution)/shard_map/ppermute | solution.py:12
  92.0 14.2 %collective-permute-start.3 = (f32[8,1,18,250]{3,2,1,0:T(8,128)S(1)}, f32[8,1,18,250]{3,2,1,0:T(8,128)}, u32[]{:S(2)}, u32[]{:S(2)}) collective-permute-start(f32[8,1,18,250]{3,2,1,0:T(8,128)S(1)} %get-tuple-element.12), channel_id=1, source_target_pairs={{16,0},{20,4},{24,8},{28,12},{32,16},{36,20},{40,24},{44,28},{48,3... | collective-permute-start | bytes 432008 | tf_op jit(solution)/shard_map/ppermute | solution.py:12
  119.9 7.7 %copy-start = (s32[8,1,16,16]{3,2,1,0:T(8,128)S(1)}, s32[8,1,16,16]{3,2,1,0:T(8,128)}, u32[]{:S(2)}) copy-start(s32[8,1,16,16]{3,2,1,0:T(8,128)} %param.9) | copy-start | bytes 24580
  124.3 9.1 %all-to-all-start.3 = ((f32[4,1,6144]{2,1,0:T(1,128)}), f32[4,1,6144]{2,1,0:T(1,128)S(1)}, u32[]{:S(2)}, u32[]{:S(2)}) async-start(f32[4,1,6144]{2,1,0:T(1,128)} %broadcast_in_dim.22), calls=%async_computation.3 | async-start | bytes 196608 | tf_op jit(solution)/shard_map/all_to_all | solution.py:23
  134.6 19.7 %all-to-all-start.4 = ((f32[16,1,16]{2,1,0:T(1,128)}), f32[16,1,16]{2,1,0:T(1,128)S(1)}, u32[]{:S(2)}, u32[]{:S(2)}) async-start(f32[16,1,16]{2,1,0:T(1,128)} %broadcast_in_dim.23), calls=%async_computation.4 | async-start | bytes 16384 | tf_op jit(solution)/shard_map/all_to_all | solution.py:23
where the time goes:
time: 156 us; the launch traced here: 155 us
  waiting for transfers between devices  66 us (42%)
  starting transfers between devices  53.4 us (34%)
  other arithmetic  10.9 us (7%)
  matrix products  9.87 us (6%)
  blocking collectives  8.11 us (5%)
  local copies, waits for them, and re-layouts  5.64 us (4%)
    all_to_all x4, waiting for transfers between devices, from_everyone(): return lax.all_to_all(copies, axis, split_axis=0, concat_axis=0, tiled=True)  44.4 us
    all_to_all x4, starting transfers between devices, from_everyone(): return lax.all_to_all(copies, axis, split_axis=0, concat_axis=0, tiled=True)  34.3 us
    ppermute x4, waiting for transfers between devices, shifted(): return lax.ppermute(block, axis, route)  21.6 us
    ppermute x4, starting transfers between devices, shifted(): return lax.ppermute(block, axis, route)  19.1 us
    all_to_all x1, blocking collectives, from_everyone(): return lax.all_to_all(copies, axis, split_axis=0, concat_axis=0, tiled=True)  8.11 us
    dot_general x1, matrix products, body(): jnp.dot(student_flat, collect(student_head, 'space', 0), preferred_elemen...  5.38 us
    dot_general x1, matrix products, body(): jnp.dot(source_flat, collect(teacher_head, 'space', 0), preferred_element...  4.49 us
    broadcast_in_dim x5, local copies, waits for them, and re-layouts, from_everyone(): copies = jnp.broadcast_to(x, (lax.axis_size(axis), *x.shape))  3.89 us
  transfers between devices with their start and end apart: 8, of which 5 were waited for; matrix products, arithmetic and copies ran while one was open for 8% of the time, Pallas kernels for 0%

commit v1 on v0

v1 whole, which is shorter than its diff:
```python
import math

import jax
import jax.numpy as jnp
from jax import lax
from jax.experimental import pallas as pl
from jax.experimental.pallas import tpu as pltpu
from jax.sharding import PartitionSpec as P

F32 = jnp.float32


def copies(x, count):
    return jnp.broadcast_to(x, (count, *x.shape))


def exchange(x, axis):
    return lax.all_to_all(x, axis, split_axis=0, concat_axis=0, tiled=True)


def gathered_rows(x, axis):
    everyone = exchange(copies(x, lax.axis_size(axis)), axis)
    return everyone.reshape(-1, x.shape[-1])


def shifted(block, axis, distance):
    devices = range(lax.axis_size(axis))
    route = [(i - distance, i) for i in devices if i - distance in devices]
    return lax.ppermute(block, axis, route)


def column_route(distance, side):
    route = []
    for i in range(side * side):
        if 0 <= i % side + distance < side:
            route.append((i, i + distance))
    return route


def teacher_kernel(edge, tokens_ref, head_ref, logits_ref, first_ref, last_ref, left_ref, right_ref):
    tokens = tokens_ref[0, 0].reshape(edge * edge, tokens_ref.shape[-1])
    logits = jnp.dot(tokens, head_ref[...], preferred_element_type=F32)
    logits_ref[0] = logits
    first_ref[0] = logits[:edge]
    last_ref[0] = logits[-edge:]
    cube = logits.reshape(edge, edge, logits.shape[-1])
    left_ref[0] = cube[:, 0, :]
    right_ref[0] = cube[:, edge - 1, :]


def teacher_logits(tokens, head):
    images, _, edge, _, width = tokens.shape
    classes = head.shape[1]
    line = pl.BlockSpec((1, edge, classes), lambda i: (i, 0, 0))
    border = jax.ShapeDtypeStruct((images, edge, classes), F32)
    patches = edge * edge
    return pl.pallas_call(
        lambda *refs: teacher_kernel(edge, *refs),
        grid=(images,),
        in_specs=[
            pl.BlockSpec((1, 1, edge, edge, width), lambda i: (i, 0, 0, 0, 0)),
            pl.BlockSpec((width, classes), lambda i: (0, 0)),
        ],
        out_specs=[pl.BlockSpec((1, patches, classes), lambda i: (i, 0, 0))] + [line] * 4,
        out_shape=[jax.ShapeDtypeStruct((images, patches, classes), F32)] + [border] * 4,
        compiler_params=pltpu.CompilerParams(vmem_limit_bytes=16 * 2**20),
        cost_estimate=pl.CostEstimate(
            flops=2 * images * patches * width * classes,
            bytes_accessed=tokens.size * 2 + head.size * 2 + images * patches * classes * 4,
            transcendentals=0,
        ),
        name="teacher_logits",
    )(tokens, head)


def stats_kernel(
    edge, parts, images, place_ref, tokens_ref, head_ref, logits_ref, up_ref, down_ref, left_ref, right_ref, out_ref
):
    image = pl.program_id(0)
    patches = edge * edge
    classes = head_ref.shape[1]
    tokens = tokens_ref[0, 0].reshape(patches, tokens_ref.shape[-1])
    student = jnp.dot(tokens, head_ref[...], preferred_element_type=F32)

    cube = logits_ref[0].reshape(edge, edge, classes)
    above = jnp.concatenate([up_ref[...], cube[:-1]], axis=0)
    below = jnp.concatenate([cube[1:], down_ref[...]], axis=0)
    columns = above + cube + below
    flat = columns.reshape(patches, classes)
    shape = (edge, edge, classes)
    x = lax.broadcasted_iota(jnp.int32, shape, 1)
    to_left = jnp.broadcast_to(left_ref[0][:, None, :], shape)
    to_right = jnp.broadcast_to(right_ref[0][:, None, :], shape)
    before = jnp.where(x == 0, to_left, pltpu.roll(flat, 1, 0).reshape(shape))
    after = jnp.where(x == edge - 1, to_right, pltpu.roll(flat, patches - 1, 0).reshape(shape))
    total = columns + before + after

    extent = place_ref[2]
    place_y = place_ref[0] + lax.broadcasted_iota(jnp.int32, (edge, edge, 1), 0)
    place_x = place_ref[1] + lax.broadcasted_iota(jnp.int32, (edge, edge, 1), 1)

    def line(place):
        return 1.0 + (place > 0).astype(F32) + (place < extent - 1).astype(F32)

    share = 1.0 / (line(place_y) * line(place_x))
    smoothed = (total * share).reshape(patches, classes)

    top_t = jnp.max(smoothed, axis=-1, keepdims=True)
    expo_t = jnp.exp(smoothed - top_t)
    sum_t = jnp.sum(expo_t, axis=-1, keepdims=True)
    gap = jnp.sum(expo_t * (smoothed - student), axis=-1, keepdims=True)
    top_s = jnp.max(student, axis=-1, keepdims=True)
    sum_s = jnp.sum(jnp.exp(student - top_s), axis=-1, keepdims=True)

    lane = lax.broadcasted_iota(jnp.int32, (patches, 128), 1)
    packed = jnp.where(lane == 0, top_t, jnp.where(lane == 1, sum_t, gap))
    packed = jnp.where(lane == 3, top_s, jnp.where(lane == 4, sum_s, packed))
    rows = packed.T
    top_t, sum_t, gap, top_s, sum_s = (rows[k : k + 1] for k in range(5))
    stats = (top_t + jnp.log(sum_t), gap / sum_t, top_s + jnp.log(sum_s))
    for k, stat in enumerate(stats):
        for c in range(parts):
            out_ref[c, pl.ds(k * images + image, 1), :] = stat


def patch_stats(place, tokens, head, logits, up, down, left, right, parts):
    images, _, edge, _, width = tokens.shape
    classes = head.shape[1]
    patches = edge * edge
    line = pl.BlockSpec((1, edge, classes), lambda i: (i, 0, 0))
    return pl.pallas_call(
        lambda *refs: stats_kernel(edge, parts, images, *refs),
        grid=(images,),
        in_specs=[
            pl.BlockSpec(memory_space=pltpu.SMEM),
            pl.BlockSpec((1, 1, edge, edge, width), lambda i: (i, 0, 0, 0, 0)),
            pl.BlockSpec((width, classes), lambda i: (0, 0)),
            pl.BlockSpec((1, patches, classes), lambda i: (i, 0, 0)),
            line,
            line,
            line,
            line,
        ],
        out_specs=pl.BlockSpec((parts, 3 * images, patches), lambda i: (0, 0, 0)),
        out_shape=jax.ShapeDtypeStruct((parts, 3 * images, patches), F32),
        compiler_params=pltpu.CompilerParams(vmem_limit_bytes=24 * 2**20),
        cost_estimate=pl.CostEstimate(
            flops=2 * images * patches * width * classes,
            bytes_accessed=tokens.size * 2 + head.size * 2 + images * patches * classes * 4,
            transcendentals=2 * images * patches * classes,
        ),
        name="patch_stats",
    )(place, tokens, head, logits, up, down, left, right)


def divergence_kernel(images, tiles, stats_ref, valid_ref, divergence_ref, totals_ref):
    lse_t = stats_ref[:, :images, :]
    gap = stats_ref[:, images : 2 * images, :]
    lse_s = stats_ref[:, 2 * images :, :]
    top_t = jnp.max(lse_t, axis=0)
    top_s = jnp.max(lse_s, axis=0)
    share = jnp.exp(lse_t - top_t[None])
    sum_t = jnp.sum(share, axis=0)
    sum_s = jnp.sum(jnp.exp(lse_s - top_s[None]), axis=0)
    mean_gap = jnp.sum(share * gap, axis=0) / sum_t
    divergence = mean_gap - top_t - jnp.log(sum_t) + top_s + jnp.log(sum_s)
    divergence_ref[...] = divergence
    weights = valid_ref[...].astype(F32)
    total = jnp.sum(divergence * weights, axis=1, keepdims=True)
    number = jnp.sum(weights, axis=1, keepdims=True)
    shape = (images, 128)
    lane = lax.broadcasted_iota(jnp.int32, shape, 1)
    row = lax.broadcasted_iota(jnp.int32, shape, 0)
    both = jnp.where(lane == row, total, jnp.where(lane == row + images, number, 0.0))
    line = jnp.sum(both, axis=0, keepdims=True)
    totals_ref[...] = jnp.broadcast_to(line[None], totals_ref.shape)


def patch_divergence(stats, valid, tiles):
    images, patches = valid.shape
    whole = pl.BlockSpec(memory_space=pltpu.VMEM)
    return pl.pallas_call(
        lambda *refs: divergence_kernel(images, tiles, *refs),
        in_specs=[whole, whole],
        out_specs=[whole, whole],
        out_shape=[
            jax.ShapeDtypeStruct((images, patches), F32),
            jax.ShapeDtypeStruct((tiles, 1, 128), F32),
        ],
        compiler_params=pltpu.CompilerParams(vmem_limit_bytes=8 * 2**20),
        name="patch_divergence",
    )(stats, valid)


def summed_columns(column, above, below):
    tall = jnp.concatenate([above, column, below], axis=1)
    return tall[:, :-2] + tall[:, 1:-1] + tall[:, 2:]


def body(teacher_tokens, student_tokens, teacher_head, student_head, valid):
    tiles = lax.axis_size("space")
    parts = lax.axis_size("mp")
    side = math.isqrt(tiles)
    tile_index = lax.axis_index("space")
    images, _, edge, _, _ = teacher_tokens.shape
    place = jnp.stack([tile_index // side * edge, tile_index % side * edge, side * edge]).astype(jnp.int32)
    flags = valid.reshape(images, edge * edge)

    head_t = gathered_rows(teacher_head, "space")
    head_s = gathered_rows(student_head, "space")
    logits, first, last, left_edge, right_edge = teacher_logits(teacher_tokens, head_t)
    up = shifted(last, "space", side)
    down = shifted(first, "space", -side)
    left_edge = summed_columns(left_edge, up[:, :1], down[:, :1])
    right_edge = summed_columns(right_edge, up[:, -1:], down[:, -1:])
    left = lax.ppermute(right_edge, "space", column_route(1, side))
    right = lax.ppermute(left_edge, "space", column_route(-1, side))
    stats = patch_stats(place, student_tokens, head_s, logits, up, down, left, right, parts)
    stats = exchange(stats, "mp")
    divergence, totals = patch_divergence(stats, flags, tiles)
    totals = jnp.sum(exchange(totals, "space"), axis=(0, 1))
    image_loss = totals[:images] / jnp.maximum(totals[images : 2 * images], 1.0)
    return (divergence.reshape(images, 1, edge, edge), image_loss)


def solution(mesh):
    in_specs = (
        P("dp", "space", None, None, None),
        P("dp", "space", None, None, None),
        P(("dp", "space"), "mp"),
        P(("dp", "space"), "mp"),
        P("dp", "space", None, None),
    )
    out_specs = (P("dp", "space", None, None), P("dp"))
    return jax.shard_map(body, mesh=mesh, in_specs=in_specs, out_specs=out_specs, check_vma=False)
```

time: 156 us -> 135 us (0.87)
  blocking collectives: 8.11 us -> 41.6 us
  waiting for transfers between devices: 66 us -> 34.5 us
  starting transfers between devices: 53.4 us -> 37.3 us
  Pallas kernels: 0 us -> 10 us
  matrix products: 9.87 us -> 0 us
  other arithmetic: 10.9 us -> 1.46 us
  local copies, waits for them, and re-layouts: 5.64 us -> 8.45 us
    all_to_all x1, blocking collectives: 8.11 us -> 41.6 us  [exchange(): return lax.all_to_all(x, axis, split_axis=0, concat_axis=0, tiled=True)]
    all_to_all x4 -> x3, waiting for transfers between devices: 44.4 us -> 17.4 us  [exchange(): return lax.all_to_all(x, axis, split_axis=0, concat_axis=0, tiled=True)]
    ppermute x4 -> x2, starting transfers between devices: 19.1 us -> 6.16 us  [shifted(): return lax.ppermute(block, axis, route)]
    all_to_all x4 -> x3, starting transfers between devices: 34.3 us -> 21.4 us  [exchange(): return lax.all_to_all(x, axis, split_axis=0, concat_axis=0, tiled=True)]
    ppermute x4 -> x2, waiting for transfers between devices: 21.6 us -> 10.4 us  [shifted(): return lax.ppermute(block, axis, route)]
    pallas_call x0 -> x3, Pallas kernels: none -> 10 us  [the longest x1 6.32 us: patch_stats(): pl.pallas_call(lambda *refs: stats_kernel(edge, parts, images, *refs), gr...]
    dot_general x2 -> x0, matrix products: 9.87 us -> none  [the longest x1 5.38 us: body(): jnp.dot(student_flat, collect(student_head, 'space', 0), preferred_elemen...]
    ppermute x0 -> x2, starting transfers between devices: none -> 9.74 us  [the longest x1 8.45 us: body(): left = lax.ppermute(right_edge, 'space', column_route(1, side))]
  transfers between devices with their start and end apart: 8 -> 7, of which waited for: 5 -> 6; matrix products, arithmetic and copies ran while one was open for 8% -> 1% of each run, Pallas kernels for 0% -> 2%
where the time goes in v1:
time: 135 us; the launch traced here: 134 us
  blocking collectives  41.6 us (31%)
  starting transfers between devices  37.3 us (28%)
  waiting for transfers between devices  34.5 us (26%)
  Pallas kernels  10 us (7%)
  local copies, waits for them, and re-layouts  8.45 us (6%)
  other arithmetic  1.46 us (1%)
    all_to_all x1, blocking collectives, exchange(): return lax.all_to_all(x, axis, split_axis=0, concat_axis=0, tiled=True)  41.6 us
    all_to_all x3, starting transfers between devices, exchange(): return lax.all_to_all(x, axis, split_axis=0, concat_axis=0, tiled=True)  21.4 us
    all_to_all x3, waiting for transfers between devices, exchange(): return lax.all_to_all(x, axis, split_axis=0, concat_axis=0, tiled=True)  17.4 us
    ppermute x2, waiting for transfers between devices, shifted(): return lax.ppermute(block, axis, route)  10.4 us
    ppermute x1, starting transfers between devices, body(): left = lax.ppermute(right_edge, 'space', column_route(1, side))  8.45 us
    pallas_call x1, Pallas kernels, patch_stats(): pl.pallas_call(lambda *refs: stats_kernel(edge, parts, images, *refs), gr...  6.32 us
    ppermute x1, waiting for transfers between devices, body(): left = lax.ppermute(right_edge, 'space', column_route(1, side))  6.29 us
    ppermute x2, starting transfers between devices, shifted(): return lax.ppermute(block, axis, route)  6.16 us
  transfers between devices with their start and end apart: 7, of which 6 were waited for; matrix products, arithmetic and copies ran while one was open for 1% of the time, Pallas kernels for 2%

profile of v1, /device:TPU:6, one launch (start us, length us, event | category | flops | bytes accessed | tf_op | source)
XLA Modules:
  0.0 134.1 jit_solution(9982254827047856643)
XLA Ops:
  0.6 0.8 broadcast_in_dim.7
  1.5 41.6 %all_to_all.20 = bf16[16,88,250]{2,1,0:T(8,128)(2,1)S(1)} all-to-all(bf16[16,88,250]{2,1,0:T(8,128)(2,1)S(1)} %broadcast_in_dim.7), channel_id=1, replica_groups=mesh['dp'=8,'space'=16,'mp'=4] {'space'}, dimensions={0} | all-to-all | bytes 1408000 | tf_op jit(solution)/shard_map/all_to_all | solution.py:18
  43.1 1.7 %broadcast_in_dim.6 = bf16[16,80,250]{2,1,0:T(8,128)(2,1)} broadcast(bf16[80,250]{1,0:T(8,128)(2,1)} %param.8), dimensions={1,2} | broadcast | bytes 680000 | tf_op jit(solution)/shard_map/broadcast_in_dim | solution.py:14
  44.7 5.0 %all-to-all-start = ((bf16[16,80,250]{2,1,0:T(8,128)(2,1)}), bf16[16,80,250]{2,1,0:T(8,128)(2,1)S(1)}, u32[]{:S(2)}, u32[]{:S(2)}) async-start(bf16[16,80,250]{2,1,0:T(8,128)(2,1)} %broadcast_in_dim.6), calls=%async_computation | async-start | bytes 1310720 | tf_op jit(solution)/shard_map/all_to_all | solution.py:18
  49.8 0.0 copy-start
  49.8 2.6 %copy-done = bf16[8,1,16,16,1408]{4,3,2,1,0:T(8,128)(2,1)S(1)} copy-done((bf16[8,1,16,16,1408]{4,3,2,1,0:T(8,128)(2,1)S(1)}, bf16[8,1,16,16,1408]{4,3,2,1,0:T(8,128)(2,1)}, u32[]{:S(2)}) %copy-start) | copy-done | bytes 5767192
  52.4 3.0 %teacher_logits.1 = (f32[8,256,250]{2,1,0:T(8,128)S(1)}, f32[8,16,250]{2,1,0:T(8,128)S(1)}, f32[8,16,250]{2,1,0:T(8,128)S(1)}, f32[8,16,250]{2,1,0:T(8,128)S(1)}, f32[8,16,250]{2,1,0:T(8,128)S(1)}) custom-call(bf16[8,1,16,16,1408]{4,3,2,1,0:T(8,128)(2,1)S(1)} %copy-done, bf16[1408,250]{1,0:T(8,128)(2,1)S(1)} %bitcast.7), custom_call_target="tpu_custom_call" | custom-call | flops 1441792000 | bytes 8519168 | tf_op jit(solution)/shard_map/teacher_logits/pallas_call | solution.py:57
  55.4 0.0 copy-start.2
  55.4 4.9 %collective-permute-start = (f32[8,16,250]{2,1,0:T(8,128)S(1)}, f32[8,16,250]{2,1,0:T(8,128)S(1)}, u32[]{:S(2)}, u32[]{:S(2)}) collective-permute-start(f32[8,16,250]{2,1,0:T(8,128)S(1)} %get-tuple-element.10), channel_id=1, source_target_pairs={{0,16},{4,20},{8,24},{12,28},{16,32},{20,36},{24,40},{28,44},{32,4... | collective-permute-start | bytes 384008 | tf_op jit(solution)/shard_map/ppermute | solution.py:29
  60.3 1.3 collective-permute-start.1
  61.6 4.5 %collective-permute-done.refs_4_ = f32[8,16,250]{2,1,0:T(8,128)S(1)} collective-permute-done((f32[8,16,250]{2,1,0:T(8,128)S(1)}, f32[8,16,250]{2,1,0:T(8,128)S(1)}, u32[]{:S(2)}, u32[]{:S(2)}) %collective-permute-start) | collective-permute-done | bytes 128032 | tf_op jit(solution)/shard_map/ppermute | solution.py:29
  66.1 6.0 %collective-permute-done.1.refs_5_ = f32[8,16,250]{2,1,0:T(8,128)S(1)} collective-permute-done((f32[8,16,250]{2,1,0:T(8,128)S(1)}, f32[8,16,250]{2,1,0:T(8,128)S(1)}, u32[]{:S(2)}, u32[]{:S(2)}) %collective-permute-start.1) | collective-permute-done | bytes 128032 | tf_op jit(solution)/shard_map/ppermute | solution.py:29
  72.1 0.1 fusion
  72.1 1.3 collective-permute-start.3
  73.4 0.7 fusion.2
  74.1 8.4 %collective-permute-start.2 = (f32[8,16,250]{2,1,0:T(8,128)}, f32[8,16,250]{2,1,0:T(8,128)S(1)}, u32[]{:S(2)}, u32[]{:S(2)}) collective-permute-start(f32[8,16,250]{2,1,0:T(8,128)} %fusion.2), channel_id=1, source_target_pairs={{0,4},{4,8},{8,12},{16,20},{20,24},{24,28},{32,36},{36,40},{40,44}... | collective-permute-start | bytes 384008 | tf_op jit(solution)/shard_map/ppermute | solution.py:216
  82.6 0.1 pad_add_fusion.refs_0_
  82.7 0.0 all-to-all-done
  82.7 0.3 collective-permute-done.3.refs_7_
  83.0 6.3 %collective-permute-done.2.refs_6_ = f32[8,16,250]{2,1,0:T(8,128)S(1)} collective-permute-done((f32[8,16,250]{2,1,0:T(8,128)}, f32[8,16,250]{2,1,0:T(8,128)S(1)}, u32[]{:S(2)}, u32[]{:S(2)}) %collective-permute-start.2) | collective-permute-done | bytes 128032 | tf_op jit(solution)/shard_map/ppermute | solution.py:216
  89.3 0.0 copy-start.1
  89.3 2.5 %copy-done.1 = bf16[8,1,16,16,1280]{4,3,2,1,0:T(8,128)(2,1)S(1)} copy-done((bf16[8,1,16,16,1280]{4,3,2,1,0:T(8,128)(2,1)S(1)}, bf16[8,1,16,16,1280]{4,3,2,1,0:T(8,128)(2,1)}, u32[]{:S(2)}) %copy-start.1) | copy-done | bytes 5242904
  91.8 6.3 %patch_stats.1 = f32[4,24,256]{2,1,0:T(8,128)} custom-call(s32[3]{0:T(128)S(1)} %pad_add_fusion.refs_0_, bf16[8,1,16,16,1280]{4,3,2,1,0:T(8,128)(2,1)S(1)} %copy-done.1, bf16[1280,250]{1,0:T(8,128)(2,1)S(1)} %bitcast.8, f32[8,256,250]{2,1,0:T(8,128)S(1)} %get-tuple-element.9.refs_3_, f32[8,16,250]{2,1,0:T(8,128)S(1)} %collective-permute-done.refs_4_, ...), custom_call_target="tpu_custom_call" | custom-call | flops 1310720000 | bytes 7930880 | tf_op jit(solution)/shard_map/patch_stats/pallas_call | solution.py:131
  98.1 5.6 %all-to-all-start.2 = ((f32[4,24,256]{2,1,0:T(8,128)}), f32[4,24,256]{2,1,0:T(8,128)S(1)}, u32[]{:S(2)}, u32[]{:S(2)}) async-start(f32[4,24,256]{2,1,0:T(8,128)} %patch_stats.1), calls=%async_computation.2 | async-start | bytes 196608 | tf_op jit(solution)/shard_map/all_to_all | solution.py:18
  103.7 0.0 copy-done.2
  103.7 0.1 reshape.18.refs_1_
  103.8 5.7 %all-to-all-done.2.refs_0_ = f32[4,24,256]{2,1,0:T(8,128)S(1)} async-done(((f32[4,24,256]{2,1,0:T(8,128)}), f32[4,24,256]{2,1,0:T(8,128)S(1)}, u32[]{:S(2)}, u32[]{:S(2)}) %all-to-all-start.2) | async-done | bytes 98336 | tf_op jit(solution)/shard_map/all_to_all | solution.py:18
  109.5 0.7 patch_divergence.1
  110.2 10.8 %all-to-all-start.3 = ((f32[16,1,128]{2,1,0:T(1,128)}), f32[16,1,128]{2,1,0:T(1,128)S(1)}, u32[]{:S(2)}, u32[]{:S(2)}) async-start(f32[16,1,128]{2,1,0:T(1,128)} %get-tuple-element.15), calls=%async_computation.3 | async-start | bytes 16384 | tf_op jit(solution)/shard_map/all_to_all | solution.py:18
  121.1 0.7 reshape.19
  121.8 11.7 %all-to-all-done.3 = f32[16,1,128]{2,1,0:T(1,128)S(1)} async-done(((f32[16,1,128]{2,1,0:T(1,128)}), f32[16,1,128]{2,1,0:T(1,128)S(1)}, u32[]{:S(2)}, u32[]{:S(2)}) %all-to-all-start.3) | async-done | bytes 8224 | tf_op jit(solution)/shard_map/all_to_all | solution.py:18
  133.5 0.6 maximum_divide_fusion
  (3 shorter events, 0.1 us)
Async XLA Ops:
  44.7 38.0 %all-to-all-start = ((bf16[16,80,250]{2,1,0:T(8,128)(2,1)}), bf16[16,80,250]{2,1,0:T(8,128)(2,1)S(1)}, u32[]{:S(2)}, u32[]{:S(2)}) async-start(bf16[16,80,250]{2,1,0:T(8,128)(2,1)} %broadcast_in_dim.6), calls=%async_computation | async-start | bytes 1310720 | tf_op jit(solution)/shard_map/all_to_all | solution.py:18
  49.8 2.6 %copy-start = (bf16[8,1,16,16,1408]{4,3,2,1,0:T(8,128)(2,1)S(1)}, bf16[8,1,16,16,1408]{4,3,2,1,0:T(8,128)(2,1)}, u32[]{:S(2)}) copy-start(bf16[8,1,16,16,1408]{4,3,2,1,0:T(8,128)(2,1)} %refs_0_.1) | copy-start | bytes 17301508
  55.4 48.3 %copy-start.2 = (s32[8,1,16,16]{3,2,1,0:T(8,128)S(1)}, s32[8,1,16,16]{3,2,1,0:T(8,128)}, u32[]{:S(2)}) copy-start(s32[8,1,16,16]{3,2,1,0:T(8,128)} %param.9) | copy-start | bytes 24580
  55.4 10.6 %collective-permute-start = (f32[8,16,250]{2,1,0:T(8,128)S(1)}, f32[8,16,250]{2,1,0:T(8,128)S(1)}, u32[]{:S(2)}, u32[]{:S(2)}) collective-permute-start(f32[8,16,250]{2,1,0:T(8,128)S(1)} %get-tuple-element.10), channel_id=1, source_target_pairs={{0,16},{4,20},{8,24},{12,28},{16,32},{20,36},{24,40},{28,44},{32,4... | collective-permute-start | bytes 384008 | tf_op jit(solution)/shard_map/ppermute | solution.py:29
  60.3 11.8 %collective-permute-start.1 = (f32[8,16,250]{2,1,0:T(8,128)S(1)}, f32[8,16,250]{2,1,0:T(8,128)S(1)}, u32[]{:S(2)}, u32[]{:S(2)}) collective-permute-start(f32[8,16,250]{2,1,0:T(8,128)S(1)} %get-tuple-element.11), channel_id=1, source_target_pairs={{16,0},{20,4},{24,8},{28,12},{32,16},{36,20},{40,24},{44,28},{48,3... | collective-permute-start | bytes 384008 | tf_op jit(solution)/shard_map/ppermute | solution.py:29
  72.1 10.9 %collective-permute-start.3 = (f32[8,16,250]{2,1,0:T(8,128)S(1)}, f32[8,16,250]{2,1,0:T(8,128)S(1)}, u32[]{:S(2)}, u32[]{:S(2)}) collective-permute-start(f32[8,16,250]{2,1,0:T(8,128)S(1)} %fusion), channel_id=1, source_target_pairs={{4,0},{8,4},{12,8},{20,16},{24,20},{28,24},{36,32},{40,36},{44,40}... | collective-permute-start | bytes 384008 | tf_op jit(solution)/shard_map/ppermute | solution.py:217
  74.1 15.2 %collective-permute-start.2 = (f32[8,16,250]{2,1,0:T(8,128)}, f32[8,16,250]{2,1,0:T(8,128)S(1)}, u32[]{:S(2)}, u32[]{:S(2)}) collective-permute-start(f32[8,16,250]{2,1,0:T(8,128)} %fusion.2), channel_id=1, source_target_pairs={{0,4},{4,8},{8,12},{16,20},{20,24},{24,28},{32,36},{36,40},{40,44}... | collective-permute-start | bytes 384008 | tf_op jit(solution)/shard_map/ppermute | solution.py:216
  89.3 2.5 %copy-start.1 = (bf16[8,1,16,16,1280]{4,3,2,1,0:T(8,128)(2,1)S(1)}, bf16[8,1,16,16,1280]{4,3,2,1,0:T(8,128)(2,1)}, u32[]{:S(2)}) copy-start(bf16[8,1,16,16,1280]{4,3,2,1,0:T(8,128)(2,1)} %refs_1_.1) | copy-start | bytes 15728644
  98.1 11.4 %all-to-all-start.2 = ((f32[4,24,256]{2,1,0:T(8,128)}), f32[4,24,256]{2,1,0:T(8,128)S(1)}, u32[]{:S(2)}, u32[]{:S(2)}) async-start(f32[4,24,256]{2,1,0:T(8,128)} %patch_stats.1), calls=%async_computation.2 | async-start | bytes 196608 | tf_op jit(solution)/shard_map/all_to_all | solution.py:18
  110.2 23.2 %all-to-all-start.3 = ((f32[16,1,128]{2,1,0:T(1,128)}), f32[16,1,128]{2,1,0:T(1,128)S(1)}, u32[]{:S(2)}, u32[]{:S(2)}) async-start(f32[16,1,128]{2,1,0:T(1,128)} %get-tuple-element.15), calls=%async_computation.3 | async-start | bytes 16384 | tf_op jit(solution)/shard_map/all_to_all | solution.py:18

commit v2 on v1

v2 whole, which is shorter than its diff:
```python
import math

import jax
import jax.numpy as jnp
from jax import lax
from jax.experimental import pallas as pl
from jax.experimental.pallas import tpu as pltpu
from jax.sharding import PartitionSpec as P

F32 = jnp.float32
LANES = 256


def copies(x, count):
    return jnp.broadcast_to(x, (count, *x.shape))


def exchange(x, axis):
    return lax.all_to_all(x, axis, split_axis=0, concat_axis=0, tiled=True)


def gathered_heads(teacher_head, student_head, tiles):
    classes = teacher_head.shape[1]
    own = jnp.concatenate([teacher_head, student_head])
    own = jnp.pad(own, ((0, 0), (0, LANES - classes)))
    other = lax.ppermute(own, "space", [(t, t ^ 1) for t in range(tiles)])
    first = lax.axis_index("space") % 2 == 0
    even, odd = jnp.where(first, own, other), jnp.where(first, other, own)
    cut = teacher_head.shape[0]
    pair = jnp.concatenate([even[:cut], odd[:cut], even[cut:], odd[cut:]])
    groups = [list(range(z, tiles, 2)) for z in range(2)]
    return lax.all_gather(pair, "space", axis_index_groups=groups)


def swapped(block, pairs, parts, shift):
    route = []
    for a, b in pairs:
        for m in range(parts):
            n = (m + shift) % parts
            route += [(a * parts + m, b * parts + n), (b * parts + n, a * parts + m)]
    return lax.ppermute(block, ("space", "mp"), route)


def pairs_of(side, start, down, right):
    pairs = []
    for row in range(side):
        for column in range(side):
            place = row * down + column * right
            if place % 2 == start and place + 1 < side:
                here = row * side + column
                pairs.append((here, here + down * side + right))
    return pairs


def border_tokens(tokens, side, row, column, parts):
    images, edge, _, width = tokens.shape
    row_even, column_even = row % 2 == 0, column % 2 == 0
    last, none = edge - 1, 0

    def near(even):
        return jnp.where(even, last, none), jnp.where(even, none, last)

    rows = [
        swapped(lax.dynamic_index_in_dim(tokens, y, 1, keepdims=False), pairs_of(side, k, 1, 0), parts, 0)
        for k, y in enumerate(near(row_even))
    ]
    columns = []
    for k, x in enumerate(near(column_even)):
        own = lax.dynamic_index_in_dim(tokens, x, 2, keepdims=False)
        ends = [lax.dynamic_index_in_dim(r, x, 1, keepdims=False) for r in rows]
        top, bottom = jnp.where(row_even, ends[1], ends[0]), jnp.where(row_even, ends[0], ends[1])
        line = jnp.concatenate([own.reshape(images * edge, width), top, bottom])
        columns.append(swapped(line, pairs_of(side, k, 0, 1), parts, parts // 2))
    return [r.reshape(images * edge, width) for r in rows] + columns


def in_lanes(columns):
    height = columns[0].shape[0]
    lane = lax.broadcasted_iota(jnp.int32, (height, 128), 1)
    packed = jnp.broadcast_to(columns[-1], (height, 128))
    for k, column in enumerate(columns[:-1]):
        packed = jnp.where(lane == k, column, packed)
    rows = packed.T
    return [rows[k : k + 1] for k in range(len(columns))]


def stats_kernel(
    edge,
    classes,
    parts,
    images,
    place_ref,
    teacher_ref,
    student_ref,
    heads_ref,
    row_refs,
    column_refs,
    out_ref,
    teacher_head,
    student_head,
    rows_out,
    columns_out,
):
    image = pl.program_id(0)
    patches = edge * edge
    shape = (edge, edge, LANES)

    @pl.when(image == 0)
    def _():
        pairs = heads_ref.shape[0]
        cut = teacher_head.shape[0] // pairs
        rest = student_head.shape[0] // pairs
        for k in range(pairs):
            teacher_head[k * cut : (k + 1) * cut, :] = heads_ref[k, :cut, :]
            student_head[k * rest : (k + 1) * rest, :] = heads_ref[k, cut:, :]
        for refs, out, even in ((row_refs, rows_out, place_ref[3]), (column_refs, columns_out, place_ref[4])):
            for k, ref in enumerate(refs):
                after = even if k == 0 else 1 - even
                out[after] = jnp.dot(ref[...], teacher_head[...], preferred_element_type=F32)

    tokens = teacher_ref[0, 0].reshape(patches, teacher_ref.shape[-1])
    teacher = jnp.dot(tokens, teacher_head[...], preferred_element_type=F32)
    tokens = student_ref[0, 0].reshape(patches, student_ref.shape[-1])
    student = jnp.dot(tokens, student_head[...], preferred_element_type=F32)

    here = pl.ds(pl.multiple_of(image * edge, edge), edge)
    cube = teacher.reshape(shape)
    above = jnp.concatenate([rows_out[0, here, :][None], cube[:-1]], axis=0)
    below = jnp.concatenate([cube[1:], rows_out[1, here, :][None]], axis=0)
    columns = above + cube + below
    flat = columns.reshape(patches, LANES)

    y = lax.broadcasted_iota(jnp.int32, (edge, LANES), 0)

    def side_column(side):
        line = columns_out[side, here, :]
        top = columns_out[side, pl.ds(images * edge + image, 1), :]
        bottom = columns_out[side, pl.ds(images * edge + images + image, 1), :]
        over = jnp.where(y == 0, top, pltpu.roll(line, 1, 0))
        under = jnp.where(y == edge - 1, bottom, pltpu.roll(line, edge - 1, 0))
        return jnp.broadcast_to((line + over + under)[:, None, :], shape)

    x = lax.broadcasted_iota(jnp.int32, shape, 1)
    before = jnp.where(x == 0, side_column(0), pltpu.roll(flat, 1, 0).reshape(shape))
    after = jnp.where(x == edge - 1, side_column(1), pltpu.roll(flat, patches - 1, 0).reshape(shape))
    total = columns + before + after

    extent = place_ref[2]
    place_y = place_ref[0] + lax.broadcasted_iota(jnp.int32, (edge, edge, 1), 0)
    place_x = place_ref[1] + lax.broadcasted_iota(jnp.int32, (edge, edge, 1), 1)

    def line(place):
        return 1.0 + (place > 0).astype(F32) + (place < extent - 1).astype(F32)

    share = 1.0 / (line(place_y) * line(place_x))
    smoothed = (total * share).reshape(patches, LANES)[:, :classes]
    student = student[:, :classes]

    top_t = jnp.max(smoothed, axis=-1, keepdims=True)
    expo_t = jnp.exp(smoothed - top_t)
    sum_t = jnp.sum(expo_t, axis=-1, keepdims=True)
    gap = jnp.sum(expo_t * (smoothed - student), axis=-1, keepdims=True)
    top_s = jnp.max(student, axis=-1, keepdims=True)
    sum_s = jnp.sum(jnp.exp(student - top_s), axis=-1, keepdims=True)
    top_t, sum_t, gap, top_s, sum_s = in_lanes([top_t, sum_t, gap, top_s, sum_s])
    stats = (top_t + jnp.log(sum_t), gap / sum_t, top_s + jnp.log(sum_s))
    for k, stat in enumerate(stats):
        for c in range(parts):
            out_ref[c, pl.ds(k * images + image, 1), :] = stat


def patch_stats(place, teacher, student, heads, borders, classes, parts):
    images, _, edge, _, width_t = teacher.shape
    width_s = student.shape[-1]
    patches = edge * edge

    def kernel(place_ref, teacher_ref, student_ref, heads_ref, a, b, c, d, out_ref, *scratch):
        stats_kernel(
            edge, classes, parts, images, place_ref, teacher_ref, student_ref, heads_ref, (a, b), (c, d), out_ref, *scratch
        )

    def tile(width):
        return pl.BlockSpec((1, 1, edge, edge, width), lambda i: (i, 0, 0, 0, 0))

    def whole(x):
        return pl.BlockSpec(x.shape, lambda i: (0,) * x.ndim)

    return pl.pallas_call(
        kernel,
        grid=(images,),
        in_specs=[
            pl.BlockSpec(memory_space=pltpu.SMEM),
            tile(width_t),
            tile(width_s),
            whole(heads),
            *[whole(b) for b in borders],
        ],
        out_specs=pl.BlockSpec((parts, 3 * images, patches), lambda i: (0, 0, 0)),
        out_shape=jax.ShapeDtypeStruct((parts, 3 * images, patches), F32),
        scratch_shapes=[
            pltpu.VMEM((width_t, LANES), heads.dtype),
            pltpu.VMEM((width_s, LANES), heads.dtype),
            pltpu.VMEM((2, borders[0].shape[0], LANES), F32),
            pltpu.VMEM((2, borders[2].shape[0], LANES), F32),
        ],
        compiler_params=pltpu.CompilerParams(vmem_limit_bytes=24 * 2**20),
        cost_estimate=pl.CostEstimate(
            flops=2 * images * patches * (width_t + width_s) * LANES,
            bytes_accessed=(teacher.size + student.size + heads.size) * 2,
            transcendentals=2 * images * patches * LANES,
        ),
        name="patch_stats",
    )(place, teacher, student, heads, *borders)


def divergence_kernel(images, tiles, stats_ref, valid_ref, divergence_ref, totals_ref):
    lse_t = stats_ref[:, :images, :]
    gap = stats_ref[:, images : 2 * images, :]
    lse_s = stats_ref[:, 2 * images :, :]
    top_t = jnp.max(lse_t, axis=0)
    top_s = jnp.max(lse_s, axis=0)
    share = jnp.exp(lse_t - top_t[None])
    sum_t = jnp.sum(share, axis=0)
    sum_s = jnp.sum(jnp.exp(lse_s - top_s[None]), axis=0)
    mean_gap = jnp.sum(share * gap, axis=0) / sum_t
    divergence = mean_gap - top_t - jnp.log(sum_t) + top_s + jnp.log(sum_s)
    divergence_ref[...] = divergence
    weights = valid_ref[...].astype(F32)
    total = jnp.sum(divergence * weights, axis=1, keepdims=True)
    number = jnp.sum(weights, axis=1, keepdims=True)
    shape = (images, 128)
    lane = lax.broadcasted_iota(jnp.int32, shape, 1)
    row = lax.broadcasted_iota(jnp.int32, shape, 0)
    both = jnp.where(lane == row, total, jnp.where(lane == row + images, number, 0.0))
    line = jnp.sum(both, axis=0, keepdims=True)
    totals_ref[...] = jnp.broadcast_to(line[None], totals_ref.shape)


def patch_divergence(stats, valid, tiles):
    images, patches = valid.shape
    whole = pl.BlockSpec(memory_space=pltpu.VMEM)
    return pl.pallas_call(
        lambda *refs: divergence_kernel(images, tiles, *refs),
        in_specs=[whole, whole],
        out_specs=[whole, whole],
        out_shape=[
            jax.ShapeDtypeStruct((images, patches), F32),
            jax.ShapeDtypeStruct((tiles, 1, 128), F32),
        ],
        compiler_params=pltpu.CompilerParams(vmem_limit_bytes=8 * 2**20),
        name="patch_divergence",
    )(stats, valid)


def everywhere_sum(x, tiles, parts):
    groups = []
    for start in range(parts):
        groups.append([t * parts + (start + t % 2 * (parts // 2)) % parts for t in range(tiles)])
    everyone = lax.all_to_all(
        x, ("space", "mp"), split_axis=0, concat_axis=0, tiled=True, axis_index_groups=groups
    )
    return jnp.sum(everyone, axis=(0, 1))


def body(teacher_tokens, student_tokens, teacher_head, student_head, valid):
    tiles = lax.axis_size("space")
    parts = lax.axis_size("mp")
    side = math.isqrt(tiles)
    tile_index = lax.axis_index("space")
    row, column = tile_index // side, tile_index % side
    images, _, edge, _, _ = teacher_tokens.shape
    flags = valid.reshape(images, edge * edge)
    place = jnp.stack([row * edge, column * edge, side * edge, 1 - row % 2, 1 - column % 2]).astype(jnp.int32)

    heads = gathered_heads(teacher_head, student_head, tiles)
    borders = border_tokens(teacher_tokens[:, 0], side, row, column, parts)
    stats = patch_stats(place, teacher_tokens, student_tokens, heads, borders, teacher_head.shape[1], parts)
    stats = exchange(stats, "mp")
    divergence, totals = patch_divergence(stats, flags, tiles)
    totals = everywhere_sum(totals, tiles, parts)
    image_loss = totals[:images] / jnp.maximum(totals[images : 2 * images], 1.0)
    return (divergence.reshape(images, 1, edge, edge), image_loss)


def solution(mesh):
    in_specs = (
        P("dp", "space", None, None, None),
        P("dp", "space", None, None, None),
        P(("dp", "space"), "mp"),
        P(("dp", "space"), "mp"),
        P("dp", "space", None, None),
    )
    out_specs = (P("dp", "space", None, None), P("dp"))
    return jax.shard_map(body, mesh=mesh, in_specs=in_specs, out_specs=out_specs, check_vma=False)
```

time: 135 us -> 147 us (1.089)
  blocking collectives: 41.6 us -> 0 us
  waiting for transfers between devices: 34.5 us -> 60.3 us
  between operations: 0.75 us -> 14.3 us
  starting transfers between devices: 37.3 us -> 46.4 us
  local copies, waits for them, and re-layouts: 8.45 us -> 13 us
  other arithmetic: 1.46 us -> 3.08 us
    all_to_all x1 -> x0, blocking collectives: 41.6 us -> none  [exchange(): return lax.all_to_all(x, axis, split_axis=0, concat_axis=0, tiled=True)]
    ppermute x4 -> x5, waiting for transfers between devices: 17.1 us -> 44.6 us  [the longest x4 40.9 us: swapped(): return lax.ppermute(block, ('space', 'mp'), route)]
    all_to_all x3 -> x1, starting transfers between devices: 21.4 us -> 3.3 us  [exchange(): return lax.all_to_all(x, axis, split_axis=0, concat_axis=0, tiled=True)]
    ppermute x4 -> x5, starting transfers between devices: 15.9 us -> 29.6 us  [the longest x4 18.7 us: swapped(): return lax.ppermute(block, ('space', 'mp'), route)]
    all_to_all x0 -> x1, starting transfers between devices: none -> 13.4 us  [everywhere_sum(): lax.all_to_all(x, ('space', 'mp'), split_axis=0, concat_axis=0, tiled=Tru...]
    all_to_all x3 -> x1, waiting for transfers between devices: 17.4 us -> 5.8 us  [exchange(): return lax.all_to_all(x, axis, split_axis=0, concat_axis=0, tiled=True)]
    all_to_all x0 -> x1, waiting for transfers between devices: none -> 9.9 us  [everywhere_sum(): lax.all_to_all(x, ('space', 'mp'), split_axis=0, concat_axis=0, tiled=Tru...]
    dynamic_slice x0 -> x4, local copies, waits for them, and re-layouts: none -> 5.47 us  [the longest x1 4.18 us: border_tokens(): own = lax.dynamic_index_in_dim(tokens, x, 2, keepdims=False)]
  transfers between devices with their start and end apart: 7 -> 8, of which waited for: 6 -> 5; matrix products, arithmetic and copies ran while one was open for 1% -> 5% of each run, Pallas kernels for 2% -> 0%
where the time goes in v2:
time: 147 us
  waiting for transfers between devices  60.3 us (41%)
  starting transfers between devices  46.4 us (32%)
  between operations  14.3 us (10%)
  local copies, waits for them, and re-layouts  13 us (9%)
  Pallas kernels  9.55 us (6%)
  other arithmetic  3.08 us (2%)
    ppermute x4, waiting for transfers between devices, swapped(): return lax.ppermute(block, ('space', 'mp'), route)  40.9 us
    ppermute x4, starting transfers between devices, swapped(): return lax.ppermute(block, ('space', 'mp'), route)  18.7 us
    all_to_all x1, starting transfers between devices, everywhere_sum(): lax.all_to_all(x, ('space', 'mp'), split_axis=0, concat_axis=0, tiled=Tru...  13.4 us
    ppermute x1, starting transfers between devices, gathered_heads(): other = lax.ppermute(own, 'space', [(t, t ^ 1) for t in range(tiles)])  10.9 us
    all_to_all x1, waiting for transfers between devices, everywhere_sum(): lax.all_to_all(x, ('space', 'mp'), split_axis=0, concat_axis=0, tiled=Tru...  9.9 us
    pallas_call x1, Pallas kernels, patch_stats(): pl.pallas_call(kernel, grid=(images,), in_specs=[pl.BlockSpec(memory_spac...  8.84 us
    unnamed x10, local copies, waits for them, and re-layouts  6.55 us
    all_to_all x1, waiting for transfers between devices, exchange(): return lax.all_to_all(x, axis, split_axis=0, concat_axis=0, tiled=True)  5.8 us
  transfers between devices with their start and end apart: 8, of which 5 were waited for; matrix products, arithmetic and copies ran while one was open for 5% of the time, Pallas kernels for 0%

profile of v2, /device:TPU:6, one launch (start us, length us, event | category | flops | bytes accessed | tf_op | source)
XLA Modules:
  0.0 146.7 jit_solution(16868558847643032779)
XLA Ops:
  7.2 0.0 all-gather.3.cloned.1.call-start
  7.2 0.8 fusion.2
  8.0 10.9 %collective-permute-start = (bf16[168,256]{1,0:T(8,128)(2,1)S(1)}, bf16[168,256]{1,0:T(8,128)(2,1)S(1)}, u32[]{:S(2)}, u32[]{:S(2)}) collective-permute-start(bf16[168,256]{1,0:T(8,128)(2,1)S(1)} %fusion.2), channel_id=1, source_target_pairs={{0,4},{4,0},{8,12},{12,8},{16,20},{20,16},{24,28},{28,24},{32,36},... | collective-permute-start | bytes 258056 | tf_op jit(solution)/shard_map/ppermute | solution.py:26
  19.0 3.7 %collective-permute-done = bf16[168,256]{1,0:T(8,128)(2,1)S(1)} collective-permute-done((bf16[168,256]{1,0:T(8,128)(2,1)S(1)}, bf16[168,256]{1,0:T(8,128)(2,1)S(1)}, u32[]{:S(2)}, u32[]{:S(2)}) %collective-permute-start) | collective-permute-done | bytes 86048 | tf_op jit(solution)/shard_map/ppermute | solution.py:26
  22.7 0.9 broadcast_select_fusion.1
  23.6 0.7 pad_maximum_fusion.2
  24.3 0.0 all-gather.3.cloned.1.call-update
  24.4 1.2 constant_dynamic-slice_fusion.2
  25.5 0.1 copy.22
  25.6 4.5 %collective-permute-start.1 = (bf16[8,16,1408]{2,0,1:T(8,128)(2,1)S(1)}, bf16[8,16,1408]{2,0,1:T(8,128)(2,1)S(1)}, u32[]{:S(2)}, u32[]{:S(2)}) collective-permute-start(bf16[8,16,1408]{2,0,1:T(8,128)(2,1)S(1)} %bitcast.31), channel_id=1, source_target_pairs={{0,16},{16,0},{1,17},{17,1},{2,18},{18,2},{3,19},{19,3},{4,20},{20... | collective-permute-start | bytes 1081352 | tf_op jit(solution)/shard_map/ppermute | solution.py:41
  30.1 0.1 copy.21
  30.2 0.7 collective-permute-start.2
  30.9 4.2 %constant_dynamic-slice_fusion = (bf16[8,1,16,1,1408]{4,3,2,1,0:T(2,128)(2,1)S(1)}, bf16[8,1,16,1,1408]{4,3,2,1,0:T(2,128)(2,1)S(1)}) fusion(bf16[8,1,16,16,1408]{4,3,2,1,0:T(8,128)(2,1)} %teacher_ref.1, s32[]{:T(128)S(6)} %select_n.111, s32[]{:T(128)S(6)} %select_n.105), kind=kLoop, calls=%fused_computation.15 | loop fusion | bytes 1441800 | tf_op jit(solution)/shard_map/jit(dynamic_index_in_dim)/dynamic_slice | solution.py:69
  35.2 11.1 %collective-permute-done.1 = bf16[8,16,1408]{2,0,1:T(8,128)(2,1)S(1)} collective-permute-done((bf16[8,16,1408]{2,0,1:T(8,128)(2,1)S(1)}, bf16[8,16,1408]{2,0,1:T(8,128)(2,1)S(1)}, u32[]{:S(2)}, u32[]{:S(2)}) %collective-permute-start.1) | collective-permute-done | bytes 360480 | tf_op jit(solution)/shard_map/ppermute | solution.py:41
  46.4 0.0 collective-permute-done.2
  46.4 0.7 collective-permute-start.4
  47.1 12.8 %collective-permute-start.3 = (bf16[144,1408]{1,0:T(8,128)(2,1)S(1)}, bf16[144,1408]{1,0:T(8,128)(2,1)S(1)}, u32[]{:S(2)}, u32[]{:S(2)}) collective-permute-start(bf16[144,1408]{1,0:T(8,128)(2,1)S(1)} %pad_maximum_fusion), channel_id=1, source_target_pairs={{0,6},{6,0},{1,7},{7,1},{2,4},{4,2},{3,5},{5,3},{8,14},{14,8},{9,1... | collective-permute-start | bytes 1216520 | tf_op jit(solution)/shard_map/ppermute | solution.py:41
  60.0 0.1 stack.19.place_ref
  60.2 0.0 collective-permute-done.4.d
  60.2 29.7 %collective-permute-done.3.c = bf16[144,1408]{1,0:T(8,128)(2,1)S(1)} collective-permute-done((bf16[144,1408]{1,0:T(8,128)(2,1)S(1)}, bf16[144,1408]{1,0:T(8,128)(2,1)S(1)}, u32[]{:S(2)}, u32[]{:S(2)}) %collective-permute-start.3) | collective-permute-done | bytes 405536 | tf_op jit(solution)/shard_map/ppermute | solution.py:41
  89.9 0.0 all-gather.3.cloned.1.call-done
  89.9 0.0 copy-start
  89.9 2.6 %copy-done = bf16[8,1,16,16,1408]{4,3,2,1,0:T(8,128)(2,1)S(1)} copy-done((bf16[8,1,16,16,1408]{4,3,2,1,0:T(8,128)(2,1)S(1)}, bf16[8,1,16,16,1408]{4,3,2,1,0:T(8,128)(2,1)}, u32[]{:S(2)}) %copy-start) | copy-done | bytes 5767192
  92.5 0.0 copy-start.1
  92.5 2.5 %copy-done.1 = bf16[8,1,16,16,1280]{4,3,2,1,0:T(8,128)(2,1)S(1)} copy-done((bf16[8,1,16,16,1280]{4,3,2,1,0:T(8,128)(2,1)S(1)}, bf16[8,1,16,16,1280]{4,3,2,1,0:T(8,128)(2,1)}, u32[]{:S(2)}) %copy-start.1) | copy-done | bytes 5242904
  95.0 0.0 copy-start.2
  95.0 1.3 copy-done.2
  96.4 0.0 copy-start.3
  96.4 8.8 %patch_stats.1 = f32[4,24,256]{2,1,0:T(8,128)} custom-call(s32[5]{0:T(128)S(1)} %stack.19.place_ref, bf16[8,1,16,16,1408]{4,3,2,1,0:T(8,128)(2,1)S(1)} %copy-done, bf16[8,1,16,16,1280]{4,3,2,1,0:T(8,128)(2,1)S(1)} %copy-done.1, bf16[8,336,256]{2,1,0:T(8,128)(2,1)S(1)} %bitcast.28, bf16[128,1408]{1,0:T(8,128)(2,1)S(1)} %bitcast.26, ...), custom_call_target="tpu_custom_call" | custom-call | flops 2818572288 | bytes 12386304 | tf_op jit(solution)/shard_map/patch_stats/pallas_call | solution.py:188
  105.2 3.3 %all-to-all-start = ((f32[4,24,256]{2,1,0:T(8,128)}), f32[4,24,256]{2,1,0:T(8,128)S(1)}, u32[]{:S(2)}, u32[]{:S(2)}) async-start(f32[4,24,256]{2,1,0:T(8,128)} %patch_stats.1), calls=%async_computation | async-start | bytes 196608 | tf_op jit(solution)/shard_map/all_to_all | solution.py:19
  108.5 0.0 copy-done.3
  108.5 0.1 reshape.44.refs_1_
  108.6 5.8 %all-to-all-done.refs_0_ = f32[4,24,256]{2,1,0:T(8,128)S(1)} async-done(((f32[4,24,256]{2,1,0:T(8,128)}), f32[4,24,256]{2,1,0:T(8,128)S(1)}, u32[]{:S(2)}, u32[]{:S(2)}) %all-to-all-start) | async-done | bytes 98336 | tf_op jit(solution)/shard_map/all_to_all | solution.py:19
  114.4 0.7 patch_divergence.1
  115.1 13.4 %all-to-all-start.1 = ((f32[16,1,128]{2,1,0:T(1,128)}), f32[16,1,128]{2,1,0:T(1,128)S(1)}, u32[]{:S(2)}, u32[]{:S(2)}) async-start(f32[16,1,128]{2,1,0:T(1,128)} %get-tuple-element.5), calls=%async_computation.1 | async-start | bytes 16384 | tf_op jit(solution)/shard_map/all_to_all | solution.py:259
  128.6 0.7 reshape.45
  129.3 9.9 %all-to-all-done.1 = f32[16,1,128]{2,1,0:T(1,128)S(1)} async-done(((f32[16,1,128]{2,1,0:T(1,128)}), f32[16,1,128]{2,1,0:T(1,128)S(1)}, u32[]{:S(2)}, u32[]{:S(2)}) %all-to-all-start.1) | async-done | bytes 8224 | tf_op jit(solution)/shard_map/all_to_all | solution.py:259
  139.2 0.6 maximum_divide_fusion
  (12 shorter events, 0.3 us)
Async XLA Ops:
  7.2 82.7 %all-gather.3.cloned.1.call-start = ((), (), s32[]{:S(2)}) async-start(), calls=%async_computation.2 | async-start | bytes 1548288 | tf_op jit(solution)/shard_map/all_gather | solution.py:32
  8.0 14.7 %collective-permute-start = (bf16[168,256]{1,0:T(8,128)(2,1)S(1)}, bf16[168,256]{1,0:T(8,128)(2,1)S(1)}, u32[]{:S(2)}, u32[]{:S(2)}) collective-permute-start(bf16[168,256]{1,0:T(8,128)(2,1)S(1)} %fusion.2), channel_id=1, source_target_pairs={{0,4},{4,0},{8,12},{12,8},{16,20},{20,16},{24,28},{28,24},{32,36},... | collective-permute-start | bytes 258056 | tf_op jit(solution)/shard_map/ppermute | solution.py:26
  25.6 20.7 %collective-permute-start.1 = (bf16[8,16,1408]{2,0,1:T(8,128)(2,1)S(1)}, bf16[8,16,1408]{2,0,1:T(8,128)(2,1)S(1)}, u32[]{:S(2)}, u32[]{:S(2)}) collective-permute-start(bf16[8,16,1408]{2,0,1:T(8,128)(2,1)S(1)} %bitcast.31), channel_id=1, source_target_pairs={{0,16},{16,0},{1,17},{17,1},{2,18},{18,2},{3,19},{19,3},{4,20},{20... | collective-permute-start | bytes 1081352 | tf_op jit(solution)/shard_map/ppermute | solution.py:41
  30.2 16.2 %collective-permute-start.2 = (bf16[8,16,1408]{2,0,1:T(8,128)(2,1)S(1)}, bf16[8,16,1408]{2,0,1:T(8,128)(2,1)S(1)}, u32[]{:S(2)}, u32[]{:S(2)}) collective-permute-start(bf16[8,16,1408]{2,0,1:T(8,128)(2,1)S(1)} %bitcast.32), channel_id=1, source_target_pairs={{16,32},{32,16},{17,33},{33,17},{18,34},{34,18},{19,35},{35,19},{2... | collective-permute-start | bytes 1081352 | tf_op jit(solution)/shard_map/ppermute | solution.py:41
  46.4 13.8 %collective-permute-start.4 = (bf16[144,1408]{1,0:T(8,128)(2,1)S(1)}, bf16[144,1408]{1,0:T(8,128)(2,1)S(1)}, u32[]{:S(2)}, u32[]{:S(2)}) collective-permute-start(bf16[144,1408]{1,0:T(8,128)(2,1)S(1)} %pad_maximum_fusion.1), channel_id=1, source_target_pairs={{4,10},{10,4},{5,11},{11,5},{6,8},{8,6},{7,9},{9,7},{20,26},{26,20... | collective-permute-start | bytes 1216520 | tf_op jit(solution)/shard_map/ppermute | solution.py:41
  47.1 42.8 %collective-permute-start.3 = (bf16[144,1408]{1,0:T(8,128)(2,1)S(1)}, bf16[144,1408]{1,0:T(8,128)(2,1)S(1)}, u32[]{:S(2)}, u32[]{:S(2)}) collective-permute-start(bf16[144,1408]{1,0:T(8,128)(2,1)S(1)} %pad_maximum_fusion), channel_id=1, source_target_pairs={{0,6},{6,0},{1,7},{7,1},{2,4},{4,2},{3,5},{5,3},{8,14},{14,8},{9,1... | collective-permute-start | bytes 1216520 | tf_op jit(solution)/shard_map/ppermute | solution.py:41
  89.9 2.6 %copy-start = (bf16[8,1,16,16,1408]{4,3,2,1,0:T(8,128)(2,1)S(1)}, bf16[8,1,16,16,1408]{4,3,2,1,0:T(8,128)(2,1)}, u32[]{:S(2)}) copy-start(bf16[8,1,16,16,1408]{4,3,2,1,0:T(8,128)(2,1)} %teacher_ref.1) | copy-start | bytes 17301508
  92.5 2.5 %copy-start.1 = (bf16[8,1,16,16,1280]{4,3,2,1,0:T(8,128)(2,1)S(1)}, bf16[8,1,16,16,1280]{4,3,2,1,0:T(8,128)(2,1)}, u32[]{:S(2)}) copy-start(bf16[8,1,16,16,1280]{4,3,2,1,0:T(8,128)(2,1)} %student_ref.1) | copy-start | bytes 15728644
  95.0 1.3 copy-start.2
  96.4 12.2 %copy-start.3 = (s32[8,1,16,16]{3,2,1,0:T(8,128)S(1)}, s32[8,1,16,16]{3,2,1,0:T(8,128)}, u32[]{:S(2)}) copy-start(s32[8,1,16,16]{3,2,1,0:T(8,128)} %param.9) | copy-start | bytes 24580
  105.2 9.2 %all-to-all-start = ((f32[4,24,256]{2,1,0:T(8,128)}), f32[4,24,256]{2,1,0:T(8,128)S(1)}, u32[]{:S(2)}, u32[]{:S(2)}) async-start(f32[4,24,256]{2,1,0:T(8,128)} %patch_stats.1), calls=%async_computation | async-start | bytes 196608 | tf_op jit(solution)/shard_map/all_to_all | solution.py:19
  115.1 24.0 %all-to-all-start.1 = ((f32[16,1,128]{2,1,0:T(1,128)}), f32[16,1,128]{2,1,0:T(1,128)S(1)}, u32[]{:S(2)}, u32[]{:S(2)}) async-start(f32[16,1,128]{2,1,0:T(1,128)} %get-tuple-element.5), calls=%async_computation.1 | async-start | bytes 16384 | tf_op jit(solution)/shard_map/all_to_all | solution.py:259
Sparse Core Ops, SparseCore 0:
  24.5 47.5 all-gather.2

commit v3 on v2

v3 whole, which is shorter than its diff:
```python
import math

import jax
import jax.numpy as jnp
from jax import lax
from jax.experimental import pallas as pl
from jax.experimental.pallas import tpu as pltpu
from jax.sharding import PartitionSpec as P

F32 = jnp.float32
LANES = 256


def copies(x, count):
    return jnp.broadcast_to(x, (count, *x.shape))


def exchange(x, axis):
    return lax.all_to_all(x, axis, split_axis=0, concat_axis=0, tiled=True)


def gathered_heads(teacher_head, student_head, tiles):
    classes = teacher_head.shape[1]
    own = jnp.concatenate([teacher_head, student_head])
    own = jnp.pad(own, ((0, 0), (0, LANES - classes)))
    other = lax.ppermute(own, "space", [(t, t ^ 1) for t in range(tiles)])
    first = lax.axis_index("space") % 2 == 0
    even, odd = jnp.where(first, own, other), jnp.where(first, other, own)
    cut = teacher_head.shape[0]
    pair = jnp.concatenate([even[:cut], odd[:cut], even[cut:], odd[cut:]])
    groups = [list(range(z, tiles, 2)) for z in range(2)]
    return lax.all_gather(pair, "space", axis_index_groups=groups)


def swapped(block, pairs, parts, shift):
    route = []
    for a, b in pairs:
        for m in range(parts):
            n = (m + shift) % parts
            route += [(a * parts + m, b * parts + n), (b * parts + n, a * parts + m)]
    return lax.ppermute(block, ("space", "mp"), route)


def pairs_of(side, start, down, right):
    pairs = []
    for row in range(side):
        for column in range(side):
            place = row * down + column * right
            if place % 2 == start and place + 1 < side:
                here = row * side + column
                pairs.append((here, here + down * side + right))
    return pairs


def neighbour(block, side, down, right):
    route = []
    for row in range(side):
        for column in range(side):
            if 0 <= row + down < side and 0 <= column + right < side:
                route.append(((row + down) * side + column + right, row * side + column))
    return lax.ppermute(block, "space", route)


def in_lanes(columns):
    height = columns[0].shape[0]
    lane = lax.broadcasted_iota(jnp.int32, (height, 128), 1)
    packed = jnp.broadcast_to(columns[-1], (height, 128))
    for k, column in enumerate(columns[:-1]):
        packed = jnp.where(lane == k, column, packed)
    rows = packed.T
    return [rows[k : k + 1] for k in range(len(columns))]


def tile_spec(edge, width):
    return pl.BlockSpec((1, 1, edge, edge, width), lambda i: (i, 0, 0, 0, 0))


def whole_spec(shape):
    return pl.BlockSpec(shape, lambda i: (0,) * len(shape))


def image_spec(rows):
    return pl.BlockSpec((1, rows, LANES), lambda i: (i, 0, 0))


def teacher_kernel(
    edge, place_ref, tokens_ref, corner_ref, heads_ref, logits_ref, row_a, row_b, column_a, column_b, corners_ref, head_ref
):
    patches = edge * edge

    @pl.when(pl.program_id(0) == 0)
    def _():
        pairs = heads_ref.shape[0]
        cut = head_ref.shape[0] // pairs
        for k in range(pairs):
            head_ref[k * cut : (k + 1) * cut, :] = heads_ref[k, :cut, :]
        corners_ref[...] = jnp.dot(corner_ref[...], head_ref[...], preferred_element_type=F32)

    tokens = tokens_ref[0, 0].reshape(patches, tokens_ref.shape[-1])
    logits = jnp.dot(tokens, head_ref[...], preferred_element_type=F32)
    logits_ref[0] = logits
    cube = logits.reshape(edge, edge, LANES)
    row_even, column_even = place_ref[3] == 1, place_ref[4] == 1
    first, last = cube[0], cube[edge - 1]
    row_a[0] = jnp.where(row_even, last, first)
    row_b[0] = jnp.where(row_even, first, last)
    left, right = cube[:, 0, :], cube[:, edge - 1, :]
    column_a[0] = jnp.where(column_even, right, left)
    column_b[0] = jnp.where(column_even, left, right)


def teacher_logits(place, tokens, corner_tokens, heads):
    images, _, edge, _, width = tokens.shape
    corners = corner_tokens.shape[0]
    patches = edge * edge
    border = jax.ShapeDtypeStruct((images, edge, LANES), F32)
    return pl.pallas_call(
        lambda *refs: teacher_kernel(edge, *refs),
        grid=(images,),
        in_specs=[
            pl.BlockSpec(memory_space=pltpu.SMEM),
            tile_spec(edge, width),
            whole_spec(corner_tokens.shape),
            whole_spec(heads.shape),
        ],
        out_specs=[image_spec(patches)] + [image_spec(edge)] * 4 + [whole_spec((corners, LANES))],
        out_shape=[jax.ShapeDtypeStruct((images, patches, LANES), F32)]
        + [border] * 4
        + [jax.ShapeDtypeStruct((corners, LANES), F32)],
        scratch_shapes=[pltpu.VMEM((width, LANES), heads.dtype)],
        compiler_params=pltpu.CompilerParams(vmem_limit_bytes=16 * 2**20),
        cost_estimate=pl.CostEstimate(
            flops=2 * images * patches * width * LANES,
            bytes_accessed=tokens.size * 2 + heads.size * 2 + images * patches * LANES * 4,
            transcendentals=0,
        ),
        name="teacher_logits",
    )(place, tokens, corner_tokens, heads)


def student_kernel(edge, classes, tokens_ref, heads_ref, logits_ref, lse_ref, head_ref):
    @pl.when(pl.program_id(0) == 0)
    def _():
        pairs = heads_ref.shape[0]
        rest = head_ref.shape[0] // pairs
        cut = heads_ref.shape[1] - rest
        for k in range(pairs):
            head_ref[k * rest : (k + 1) * rest, :] = heads_ref[k, cut:, :]

    tokens = tokens_ref[0, 0].reshape(edge * edge, tokens_ref.shape[-1])
    logits = jnp.dot(tokens, head_ref[...], preferred_element_type=F32)
    logits_ref[0] = logits
    logits = logits[:, :classes]
    top = jnp.max(logits, axis=-1, keepdims=True)
    total = jnp.sum(jnp.exp(logits - top), axis=-1, keepdims=True)
    top, total = in_lanes([top, total])
    lse_ref[pl.ds(pl.program_id(0), 1), :] = top + jnp.log(total)


def student_logits(tokens, heads, classes):
    images, _, edge, _, width = tokens.shape
    patches = edge * edge
    return pl.pallas_call(
        lambda *refs: student_kernel(edge, classes, *refs),
        grid=(images,),
        in_specs=[tile_spec(edge, width), whole_spec(heads.shape)],
        out_specs=[image_spec(patches), whole_spec((images, patches))],
        out_shape=[
            jax.ShapeDtypeStruct((images, patches, LANES), F32),
            jax.ShapeDtypeStruct((images, patches), F32),
        ],
        scratch_shapes=[pltpu.VMEM((width, LANES), heads.dtype)],
        compiler_params=pltpu.CompilerParams(vmem_limit_bytes=16 * 2**20),
        cost_estimate=pl.CostEstimate(
            flops=2 * images * patches * width * LANES,
            bytes_accessed=tokens.size * 2 + heads.size * 2 + images * patches * LANES * 4,
            transcendentals=images * patches * LANES,
        ),
        name="student_logits",
    )(tokens, heads)


def stats_kernel(
    edge,
    classes,
    parts,
    images,
    place_ref,
    student_ref,
    lse_ref,
    logits_ref,
    row_a,
    row_b,
    column_a,
    column_b,
    corners_ref,
    out_ref,
):
    image = pl.program_id(0)
    patches = edge * edge
    shape = (edge, edge, LANES)
    row_even, column_even = place_ref[3] == 1, place_ref[4] == 1

    up = jnp.where(row_even, row_b[0], row_a[0])
    down = jnp.where(row_even, row_a[0], row_b[0])
    cube = logits_ref[0].reshape(shape)
    above = jnp.concatenate([up[None], cube[:-1]], axis=0)
    below = jnp.concatenate([cube[1:], down[None]], axis=0)
    columns = above + cube + below
    flat = columns.reshape(patches, LANES)

    y = lax.broadcasted_iota(jnp.int32, (edge, LANES), 0)

    def corner(k):
        return corners_ref[pl.ds(k * images + image, 1), :]

    def side_column(line, top, bottom):
        over = jnp.where(y == 0, top, pltpu.roll(line, 1, 0))
        under = jnp.where(y == edge - 1, bottom, pltpu.roll(line, edge - 1, 0))
        return jnp.broadcast_to((line + over + under)[:, None, :], shape)

    x = lax.broadcasted_iota(jnp.int32, shape, 1)
    to_left = side_column(jnp.where(column_even, column_b[0], column_a[0]), corner(0), corner(2))
    to_right = side_column(jnp.where(column_even, column_a[0], column_b[0]), corner(1), corner(3))
    before = jnp.where(x == 0, to_left, pltpu.roll(flat, 1, 0).reshape(shape))
    after = jnp.where(x == edge - 1, to_right, pltpu.roll(flat, patches - 1, 0).reshape(shape))
    total = columns + before + after

    extent = place_ref[2]
    place_y = place_ref[0] + lax.broadcasted_iota(jnp.int32, (edge, edge, 1), 0)
    place_x = place_ref[1] + lax.broadcasted_iota(jnp.int32, (edge, edge, 1), 1)

    def line(place):
        return 1.0 + (place > 0).astype(F32) + (place < extent - 1).astype(F32)

    share = 1.0 / (line(place_y) * line(place_x))
    smoothed = (total * share).reshape(patches, LANES)[:, :classes]
    student = student_ref[0][:, :classes]

    top_t = jnp.max(smoothed, axis=-1, keepdims=True)
    expo_t = jnp.exp(smoothed - top_t)
    sum_t = jnp.sum(expo_t, axis=-1, keepdims=True)
    gap = jnp.sum(expo_t * (smoothed - student), axis=-1, keepdims=True)
    top_t, sum_t, gap = in_lanes([top_t, sum_t, gap])
    lse_s = lse_ref[pl.ds(image, 1), :]
    for k, stat in enumerate((top_t + jnp.log(sum_t), gap / sum_t, lse_s)):
        for c in range(parts):
            out_ref[c, pl.ds(k * images + image, 1), :] = stat


def patch_stats(place, student, lse_s, logits, borders, corners, classes, parts):
    images, patches, _ = logits.shape
    edge = borders[0].shape[1]
    return pl.pallas_call(
        lambda *refs: stats_kernel(edge, classes, parts, images, *refs),
        grid=(images,),
        in_specs=[
            pl.BlockSpec(memory_space=pltpu.SMEM),
            image_spec(patches),
            whole_spec((images, patches)),
            image_spec(patches),
            *[image_spec(edge)] * 4,
            whole_spec(corners.shape),
        ],
        out_specs=whole_spec((parts, 3 * images, patches)),
        out_shape=jax.ShapeDtypeStruct((parts, 3 * images, patches), F32),
        compiler_params=pltpu.CompilerParams(vmem_limit_bytes=16 * 2**20),
        cost_estimate=pl.CostEstimate(
            flops=30 * images * patches * LANES,
            bytes_accessed=2 * images * patches * LANES * 4,
            transcendentals=images * patches * LANES,
        ),
        name="patch_stats",
    )(place, student, lse_s, logits, *borders, corners)


def divergence_kernel(images, tiles, stats_ref, valid_ref, divergence_ref, totals_ref):
    lse_t = stats_ref[:, :images, :]
    gap = stats_ref[:, images : 2 * images, :]
    lse_s = stats_ref[:, 2 * images :, :]
    top_t = jnp.max(lse_t, axis=0)
    top_s = jnp.max(lse_s, axis=0)
    share = jnp.exp(lse_t - top_t[None])
    sum_t = jnp.sum(share, axis=0)
    sum_s = jnp.sum(jnp.exp(lse_s - top_s[None]), axis=0)
    mean_gap = jnp.sum(share * gap, axis=0) / sum_t
    divergence = mean_gap - top_t - jnp.log(sum_t) + top_s + jnp.log(sum_s)
    divergence_ref[...] = divergence
    weights = valid_ref[...].astype(F32)
    total = jnp.sum(divergence * weights, axis=1, keepdims=True)
    number = jnp.sum(weights, axis=1, keepdims=True)
    shape = (images, 128)
    lane = lax.broadcasted_iota(jnp.int32, shape, 1)
    row = lax.broadcasted_iota(jnp.int32, shape, 0)
    both = jnp.where(lane == row, total, jnp.where(lane == row + images, number, 0.0))
    line = jnp.sum(both, axis=0, keepdims=True)
    totals_ref[...] = jnp.broadcast_to(line[None], totals_ref.shape)


def patch_divergence(stats, valid, tiles):
    images, patches = valid.shape
    whole = pl.BlockSpec(memory_space=pltpu.VMEM)
    return pl.pallas_call(
        lambda *refs: divergence_kernel(images, tiles, *refs),
        in_specs=[whole, whole],
        out_specs=[whole, whole],
        out_shape=[
            jax.ShapeDtypeStruct((images, patches), F32),
            jax.ShapeDtypeStruct((tiles, 1, 128), F32),
        ],
        compiler_params=pltpu.CompilerParams(vmem_limit_bytes=8 * 2**20),
        name="patch_divergence",
    )(stats, valid)


def everywhere_sum(x, tiles, parts):
    groups = []
    for start in range(parts):
        groups.append([t * parts + (start + t % 2 * (parts // 2)) % parts for t in range(tiles)])
    everyone = lax.all_to_all(
        x, ("space", "mp"), split_axis=0, concat_axis=0, tiled=True, axis_index_groups=groups
    )
    return jnp.sum(everyone, axis=(0, 1))


def body(teacher_tokens, student_tokens, teacher_head, student_head, valid):
    tiles = lax.axis_size("space")
    parts = lax.axis_size("mp")
    side = math.isqrt(tiles)
    tile_index = lax.axis_index("space")
    row, column = tile_index // side, tile_index % side
    images, _, edge, _, _ = teacher_tokens.shape
    classes = teacher_head.shape[1]
    flags = valid.reshape(images, edge * edge)
    place = jnp.stack([row * edge, column * edge, side * edge, 1 - row % 2, 1 - column % 2]).astype(jnp.int32)

    heads = gathered_heads(teacher_head, student_head, tiles)
    around = ((-1, -1, -1, -1), (-1, 1, -1, 0), (1, -1, 0, -1), (1, 1, 0, 0))
    corner_tokens = jnp.concatenate(
        [neighbour(teacher_tokens[:, 0, y, x], side, down, right) for down, right, y, x in around]
    )
    logits, row_a, row_b, column_a, column_b, corners = teacher_logits(place, teacher_tokens, corner_tokens, heads)
    borders = [
        swapped(row_a, pairs_of(side, 0, 1, 0), parts, 0),
        swapped(row_b, pairs_of(side, 1, 1, 0), parts, 0),
        swapped(column_a, pairs_of(side, 0, 0, 1), parts, 0),
        swapped(column_b, pairs_of(side, 1, 0, 1), parts, 0),
    ]
    student, lse_s = student_logits(student_tokens, heads, classes)
    stats = patch_stats(place, student, lse_s, logits, borders, corners, classes, parts)
    stats = exchange(stats, "mp")
    divergence, totals = patch_divergence(stats, flags, tiles)
    totals = everywhere_sum(totals, tiles, parts)
    image_loss = totals[:images] / jnp.maximum(totals[images : 2 * images], 1.0)
    return (divergence.reshape(images, 1, edge, edge), image_loss)


def solution(mesh):
    in_specs = (
        P("dp", "space", None, None, None),
        P("dp", "space", None, None, None),
        P(("dp", "space"), "mp"),
        P(("dp", "space"), "mp"),
        P("dp", "space", None, None),
    )
    out_specs = (P("dp", "space", None, None), P("dp"))
    return jax.shard_map(body, mesh=mesh, in_specs=in_specs, out_specs=out_specs, check_vma=False)
```

time: 147 us -> 141 us (0.959)
  waiting for transfers between devices: 60.3 us -> 49.2 us
  starting transfers between devices: 46.4 us -> 54.2 us
  local copies, waits for them, and re-layouts: 13 us -> 6.25 us
  Pallas kernels: 9.55 us -> 13.9 us
    ppermute x4, waiting for transfers between devices: 40.9 us -> 0.02 us  [swapped(): return lax.ppermute(block, ('space', 'mp'), route)]
    ppermute x0 -> x4, waiting for transfers between devices: none -> 14.9 us  [neighbour(): return lax.ppermute(block, 'space', route)]
    all_gather x1, waiting for transfers between devices: 0.01 us -> 14.8 us  [gathered_heads(): return lax.all_gather(pair, 'space', axis_index_groups=groups)]
    ppermute x0 -> x4, starting transfers between devices: none -> 12.9 us  [neighbour(): return lax.ppermute(block, 'space', route)]
    ppermute x4, starting transfers between devices: 18.7 us -> 13 us  [swapped(): return lax.ppermute(block, ('space', 'mp'), route)]
    dynamic_slice x4 -> x0, local copies, waits for them, and re-layouts: 5.47 us -> none  [the longest x1 4.18 us: border_tokens(): own = lax.dynamic_index_in_dim(tokens, x, 2, keepdims=False)]
    pallas_call x1 -> x3, Pallas kernels: 8.84 us -> 13.2 us  [the longest x1 4.73 us: patch_stats(): pl.pallas_call(lambda *refs: stats_kernel(edge, classes, parts, images, *...]
    unnamed x10 -> x14, local copies, waits for them, and re-layouts: 6.55 us -> 4.01 us
  transfers between devices with their start and end apart: 8 -> 12, of which waited for: 5 -> 5; matrix products, arithmetic and copies ran while one was open for 5% -> 2% of each run, Pallas kernels for 0% -> 3%
where the time goes in v3:
time: 141 us
  starting transfers between devices  54.2 us (38%)
  waiting for transfers between devices  49.2 us (35%)
  between operations  14.3 us (10%)
  Pallas kernels  13.9 us (10%)
  local copies, waits for them, and re-layouts  6.25 us (4%)
  other arithmetic  2.99 us (2%)
    ppermute x4, waiting for transfers between devices, neighbour(): return lax.ppermute(block, 'space', route)  14.9 us
    all_gather x1, waiting for transfers between devices, gathered_heads(): return lax.all_gather(pair, 'space', axis_index_groups=groups)  14.8 us
    all_to_all x1, starting transfers between devices, everywhere_sum(): lax.all_to_all(x, ('space', 'mp'), split_axis=0, concat_axis=0, tiled=Tru...  13.2 us
    ppermute x4, starting transfers between devices, swapped(): return lax.ppermute(block, ('space', 'mp'), route)  13 us
    ppermute x4, starting transfers between devices, neighbour(): return lax.ppermute(block, 'space', route)  12.9 us
    ppermute x1, starting transfers between devices, gathered_heads(): other = lax.ppermute(own, 'space', [(t, t ^ 1) for t in range(tiles)])  10.9 us
    all_to_all x1, waiting for transfers between devices, everywhere_sum(): lax.all_to_all(x, ('space', 'mp'), split_axis=0, concat_axis=0, tiled=Tru...  9.9 us
    all_to_all x1, waiting for transfers between devices, exchange(): return lax.all_to_all(x, axis, split_axis=0, concat_axis=0, tiled=True)  5.74 us
  transfers between devices with their start and end apart: 12, of which 5 were waited for; matrix products, arithmetic and copies ran while one was open for 2% of the time, Pallas kernels for 3%

profile of v3, /device:TPU:6, one launch (start us, length us, event | category | flops | bytes accessed | tf_op | source)
XLA Modules:
  0.0 140.8 jit_solution(16312817258762052282)
XLA Ops:
  7.2 0.0 all-gather.3.cloned.1.call-start
  7.2 0.8 fusion.2
  8.0 10.9 %collective-permute-start = (bf16[168,256]{1,0:T(8,128)(2,1)S(1)}, bf16[168,256]{1,0:T(8,128)(2,1)S(1)}, u32[]{:S(2)}, u32[]{:S(2)}) collective-permute-start(bf16[168,256]{1,0:T(8,128)(2,1)S(1)} %fusion.2), channel_id=1, source_target_pairs={{0,4},{4,0},{8,12},{12,8},{16,20},{20,16},{24,28},{28,24},{32,36},... | collective-permute-start | bytes 258056 | tf_op jit(solution)/shard_map/ppermute | solution.py:26
  19.0 3.7 %collective-permute-done = bf16[168,256]{1,0:T(8,128)(2,1)S(1)} collective-permute-done((bf16[168,256]{1,0:T(8,128)(2,1)S(1)}, bf16[168,256]{1,0:T(8,128)(2,1)S(1)}, u32[]{:S(2)}, u32[]{:S(2)}) %collective-permute-start) | collective-permute-done | bytes 86048 | tf_op jit(solution)/shard_map/ppermute | solution.py:26
  22.7 0.9 broadcast_select_fusion.1
  23.6 0.7 pad_maximum_fusion
  24.3 0.0 all-gather.3.cloned.1.call-update
  24.3 1.3 fusion.3
  25.7 10.3 %collective-permute-start.1 = (bf16[8,1408]{1,0:T(8,128)(2,1)S(1)}, bf16[8,1408]{1,0:T(8,128)(2,1)S(1)}, u32[]{:S(2)}, u32[]{:S(2)}) collective-permute-start(bf16[8,1408]{1,0:T(8,128)(2,1)S(1)} %bitcast.23), channel_id=1, source_target_pairs={{0,20},{4,24},{8,28},{16,36},{20,40},{24,44},{32,52},{36,56},{40,6... | collective-permute-start | bytes 67592 | tf_op jit(solution)/shard_map/ppermute | solution.py:61
  36.0 0.7 collective-permute-start.2
  36.7 0.7 collective-permute-start.3
  37.4 1.3 collective-permute-start.4
  38.7 0.1 stack.19.refs_0_
  38.8 0.0 collective-permute-done.1
  38.8 0.0 collective-permute-done.2
  38.8 0.0 collective-permute-done.3
  38.8 14.9 %collective-permute-done.4 = bf16[8,1408]{1,0:T(8,128)(2,1)S(1)} collective-permute-done((bf16[8,1408]{1,0:T(8,128)(2,1)S(1)}, bf16[8,1408]{1,0:T(8,128)(2,1)S(1)}, u32[]{:S(2)}, u32[]{:S(2)}) %collective-permute-start.4) | collective-permute-done | bytes 22560 | tf_op jit(solution)/shard_map/ppermute | solution.py:61
  53.7 14.8 %all-gather.3.cloned.1.call-done = bf16[2688,256]{1,0:T(8,128)(2,1)} async-done(((bf16[336,256]{1,0:T(8,128)(2,1)}), bf16[2688,256]{1,0:T(8,128)(2,1)}) %all-gather.3.cloned.1.call-update) | async-done | bytes 1376272 | tf_op jit(solution)/shard_map/all_gather | solution.py:32
  68.5 0.0 copy-start
  68.6 2.6 %copy-done = bf16[8,1,16,16,1408]{4,3,2,1,0:T(8,128)(2,1)S(1)} copy-done((bf16[8,1,16,16,1408]{4,3,2,1,0:T(8,128)(2,1)S(1)}, bf16[8,1,16,16,1408]{4,3,2,1,0:T(8,128)(2,1)}, u32[]{:S(2)}) %copy-start) | copy-done | bytes 5767192
  71.2 0.0 copy-start.1
  71.2 1.3 copy-done.1
  72.5 0.0 copy-start.2
  72.5 0.0 copy-start.3
  72.5 4.0 %teacher_logits.1 = (f32[8,256,256]{2,1,0:T(8,128)S(1)}, f32[8,16,256]{2,1,0:T(8,128)S(1)}, f32[8,16,256]{2,1,0:T(8,128)S(1)}, f32[8,16,256]{2,1,0:T(8,128)S(1)}...) custom-call(s32[5]{0:T(128)S(1)} %stack.19.refs_0_, bf16[8,1,16,16,1408]{4,3,2,1,0:T(8,128)(2,1)S(1)} %copy-done, ...), custom_call_target="tpu_custom_call" | custom-call | flops 1476395008 | bytes 9240576 | tf_op jit(solution)/shard_map/teacher_logits/pallas_call | solution.py:117
  76.5 3.8 %collective-permute-start.5 = (f32[8,16,256]{2,1,0:T(8,128)S(1)}, f32[8,16,256]{2,1,0:T(8,128)S(1)}, u32[]{:S(2)}, u32[]{:S(2)}) collective-permute-start(f32[8,16,256]{2,1,0:T(8,128)S(1)} %get-tuple-element.15), channel_id=1, source_target_pairs={{0,16},{16,0},{1,17},{17,1},{2,18},{18,2},{3,19},{19,3},{4,20},{20... | collective-permute-start | bytes 393224 | tf_op jit(solution)/shard_map/ppermute | solution.py:41
  80.3 0.7 collective-permute-start.6
  81.0 7.7 %collective-permute-start.7 = (f32[8,16,256]{2,1,0:T(8,128)S(1)}, f32[8,16,256]{2,1,0:T(8,128)S(1)}, u32[]{:S(2)}, u32[]{:S(2)}) collective-permute-start(f32[8,16,256]{2,1,0:T(8,128)S(1)} %get-tuple-element.17), channel_id=1, source_target_pairs={{0,4},{4,0},{1,5},{5,1},{2,6},{6,2},{3,7},{7,3},{8,12},{12,8},{9,1... | collective-permute-start | bytes 393224 | tf_op jit(solution)/shard_map/ppermute | solution.py:41
  88.8 0.0 copy-start.4
  88.8 0.8 collective-permute-start.8
  89.6 0.0 copy-done.2
  89.6 0.0 copy-done.3
  89.6 4.5 %student_logits.1 = (f32[8,256,256]{2,1,0:T(8,128)S(1)}, f32[8,256]{1,0:T(8,128)S(1)}) custom-call(bf16[8,1,16,16,1280]{4,3,2,1,0:T(8,128)(2,1)S(1)} %copy-done.3, bf16[8,336,256]{2,1,0:T(8,128)(2,1)S(1)} %bitcast.21), custom_call_target="tpu_custom_call" | custom-call | flops 1342177280 | bytes 8716288 | tf_op jit(solution)/shard_map/student_logits/pallas_call | solution.py:163
  94.1 0.0 collective-permute-done.5.refs_4_
  94.1 0.0 collective-permute-done.6.refs_5_
  94.1 0.0 collective-permute-done.7.refs_6_
  94.1 0.0 collective-permute-done.8.refs_7_
  94.1 4.7 %patch_stats.1 = f32[4,24,256]{2,1,0:T(8,128)} custom-call(s32[5]{0:T(128)S(1)} %stack.19.refs_0_, f32[8,256,256]{2,1,0:T(8,128)S(1)} %get-tuple-element.12.refs_1_, f32[8,256]{1,0:T(8,128)S(1)} %get-tuple-element.13.refs_2_, f32[8,256,256]{2,1,0:T(8,128)S(1)} %get-tuple-element.14.refs_3_, f32[8,16,256]{2,1,0:T(8,128)S(1)} %collective-permute-done.5.refs_4_, ...), custom_call_target="tpu_custom_call" | custom-call | flops 15728640 | bytes 4194304 | tf_op jit(solution)/shard_map/patch_stats/pallas_call | solution.py:254
  98.9 4.1 %all-to-all-start = ((f32[4,24,256]{2,1,0:T(8,128)}), f32[4,24,256]{2,1,0:T(8,128)S(1)}, u32[]{:S(2)}, u32[]{:S(2)}) async-start(f32[4,24,256]{2,1,0:T(8,128)} %patch_stats.1), calls=%async_computation | async-start | bytes 196608 | tf_op jit(solution)/shard_map/all_to_all | solution.py:19
  103.0 0.0 copy-done.4
  103.0 0.1 reshape.10.refs_1_
  103.0 5.7 %all-to-all-done.refs_0_ = f32[4,24,256]{2,1,0:T(8,128)S(1)} async-done(((f32[4,24,256]{2,1,0:T(8,128)}), f32[4,24,256]{2,1,0:T(8,128)S(1)}, u32[]{:S(2)}, u32[]{:S(2)}) %all-to-all-start) | async-done | bytes 98336 | tf_op jit(solution)/shard_map/all_to_all | solution.py:19
  108.8 0.7 patch_divergence.1
  109.5 13.2 %all-to-all-start.1 = ((f32[16,1,128]{2,1,0:T(1,128)}), f32[16,1,128]{2,1,0:T(1,128)S(1)}, u32[]{:S(2)}, u32[]{:S(2)}) async-start(f32[16,1,128]{2,1,0:T(1,128)} %get-tuple-element.21), calls=%async_computation.1 | async-start | bytes 16384 | tf_op jit(solution)/shard_map/all_to_all | solution.py:320
  122.7 0.7 reshape.11
  123.4 9.9 %all-to-all-done.1 = f32[16,1,128]{2,1,0:T(1,128)S(1)} async-done(((f32[16,1,128]{2,1,0:T(1,128)}), f32[16,1,128]{2,1,0:T(1,128)S(1)}, u32[]{:S(2)}, u32[]{:S(2)}) %all-to-all-start.1) | async-done | bytes 8224 | tf_op jit(solution)/shard_map/all_to_all | solution.py:320
  133.3 0.6 maximum_divide_fusion
  (10 shorter events, 0.1 us)
Async XLA Ops:
  7.2 61.4 %all-gather.3.cloned.1.call-start = ((), (), s32[]{:S(2)}) async-start(), calls=%async_computation.2 | async-start | bytes 1548288 | tf_op jit(solution)/shard_map/all_gather | solution.py:32
  8.0 14.7 %collective-permute-start = (bf16[168,256]{1,0:T(8,128)(2,1)S(1)}, bf16[168,256]{1,0:T(8,128)(2,1)S(1)}, u32[]{:S(2)}, u32[]{:S(2)}) collective-permute-start(bf16[168,256]{1,0:T(8,128)(2,1)S(1)} %fusion.2), channel_id=1, source_target_pairs={{0,4},{4,0},{8,12},{12,8},{16,20},{20,16},{24,28},{28,24},{32,36},... | collective-permute-start | bytes 258056 | tf_op jit(solution)/shard_map/ppermute | solution.py:26
  25.7 13.1 %collective-permute-start.1 = (bf16[8,1408]{1,0:T(8,128)(2,1)S(1)}, bf16[8,1408]{1,0:T(8,128)(2,1)S(1)}, u32[]{:S(2)}, u32[]{:S(2)}) collective-permute-start(bf16[8,1408]{1,0:T(8,128)(2,1)S(1)} %bitcast.23), channel_id=1, source_target_pairs={{0,20},{4,24},{8,28},{16,36},{20,40},{24,44},{32,52},{36,56},{40,6... | collective-permute-start | bytes 67592 | tf_op jit(solution)/shard_map/ppermute | solution.py:61
  36.0 2.8 %collective-permute-start.2 = (bf16[8,1408]{1,0:T(8,128)(2,1)S(1)}, bf16[8,1408]{1,0:T(8,128)(2,1)S(1)}, u32[]{:S(2)}, u32[]{:S(2)}) collective-permute-start(bf16[8,1408]{1,0:T(8,128)(2,1)S(1)} %bitcast.24), channel_id=1, source_target_pairs={{4,16},{8,20},{12,24},{20,32},{24,36},{28,40},{36,48},{40,52},{44,... | collective-permute-start | bytes 67592 | tf_op jit(solution)/shard_map/ppermute | solution.py:61
  36.7 2.1 %collective-permute-start.3 = (bf16[8,1408]{1,0:T(8,128)(2,1)S(1)}, bf16[8,1408]{1,0:T(8,128)(2,1)S(1)}, u32[]{:S(2)}, u32[]{:S(2)}) collective-permute-start(bf16[8,1408]{1,0:T(8,128)(2,1)S(1)} %bitcast.25), channel_id=1, source_target_pairs={{16,4},{20,8},{24,12},{32,20},{36,24},{40,28},{48,36},{52,40},{56,... | collective-permute-start | bytes 67592 | tf_op jit(solution)/shard_map/ppermute | solution.py:61
  37.4 16.4 %collective-permute-start.4 = (bf16[8,1408]{1,0:T(8,128)(2,1)S(1)}, bf16[8,1408]{1,0:T(8,128)(2,1)S(1)}, u32[]{:S(2)}, u32[]{:S(2)}) collective-permute-start(bf16[8,1408]{1,0:T(8,128)(2,1)S(1)} %bitcast.26), channel_id=1, source_target_pairs={{20,0},{24,4},{28,8},{36,16},{40,20},{44,24},{52,32},{56,36},{60,4... | collective-permute-start | bytes 67592 | tf_op jit(solution)/shard_map/ppermute | solution.py:61
  68.5 2.6 %copy-start = (bf16[8,1,16,16,1408]{4,3,2,1,0:T(8,128)(2,1)S(1)}, bf16[8,1,16,16,1408]{4,3,2,1,0:T(8,128)(2,1)}, u32[]{:S(2)}) copy-start(bf16[8,1,16,16,1408]{4,3,2,1,0:T(8,128)(2,1)} %refs_1_.1) | copy-start | bytes 17301508
  71.2 1.3 copy-start.1
  72.5 17.1 %copy-start.2 = (bf16[2688,256]{1,0:T(8,128)(2,1)S(1)}, bf16[2688,256]{1,0:T(8,128)(2,1)}, u32[]{:S(2)}) copy-start(bf16[2688,256]{1,0:T(8,128)(2,1)} %all-gather.3.cloned.1.call-done) | copy-start | bytes 4128772
  72.5 17.1 %copy-start.3 = (bf16[8,1,16,16,1280]{4,3,2,1,0:T(8,128)(2,1)S(1)}, bf16[8,1,16,16,1280]{4,3,2,1,0:T(8,128)(2,1)}, u32[]{:S(2)}) copy-start(bf16[8,1,16,16,1280]{4,3,2,1,0:T(8,128)(2,1)} %refs_0_.1) | copy-start | bytes 15728644
  76.5 17.6 %collective-permute-start.5 = (f32[8,16,256]{2,1,0:T(8,128)S(1)}, f32[8,16,256]{2,1,0:T(8,128)S(1)}, u32[]{:S(2)}, u32[]{:S(2)}) collective-permute-start(f32[8,16,256]{2,1,0:T(8,128)S(1)} %get-tuple-element.15), channel_id=1, source_target_pairs={{0,16},{16,0},{1,17},{17,1},{2,18},{18,2},{3,19},{19,3},{4,20},{20... | collective-permute-start | bytes 393224 | tf_op jit(solution)/shard_map/ppermute | solution.py:41
  80.3 13.8 %collective-permute-start.6 = (f32[8,16,256]{2,1,0:T(8,128)S(1)}, f32[8,16,256]{2,1,0:T(8,128)S(1)}, u32[]{:S(2)}, u32[]{:S(2)}) collective-permute-start(f32[8,16,256]{2,1,0:T(8,128)S(1)} %get-tuple-element.16), channel_id=1, source_target_pairs={{16,32},{32,16},{17,33},{33,17},{18,34},{34,18},{19,35},{35,19},{2... | collective-permute-start | bytes 393224 | tf_op jit(solution)/shard_map/ppermute | solution.py:41
  81.0 13.1 %collective-permute-start.7 = (f32[8,16,256]{2,1,0:T(8,128)S(1)}, f32[8,16,256]{2,1,0:T(8,128)S(1)}, u32[]{:S(2)}, u32[]{:S(2)}) collective-permute-start(f32[8,16,256]{2,1,0:T(8,128)S(1)} %get-tuple-element.17), channel_id=1, source_target_pairs={{0,4},{4,0},{1,5},{5,1},{2,6},{6,2},{3,7},{7,3},{8,12},{12,8},{9,1... | collective-permute-start | bytes 393224 | tf_op jit(solution)/shard_map/ppermute | solution.py:41
  88.8 14.2 %copy-start.4 = (s32[8,1,16,16]{3,2,1,0:T(8,128)S(1)}, s32[8,1,16,16]{3,2,1,0:T(8,128)}, u32[]{:S(2)}) copy-start(s32[8,1,16,16]{3,2,1,0:T(8,128)} %param.9) | copy-start | bytes 24580
  88.8 5.4 %collective-permute-start.8 = (f32[8,16,256]{2,1,0:T(8,128)S(1)}, f32[8,16,256]{2,1,0:T(8,128)S(1)}, u32[]{:S(2)}, u32[]{:S(2)}) collective-permute-start(f32[8,16,256]{2,1,0:T(8,128)S(1)} %get-tuple-element.18), channel_id=1, source_target_pairs={{4,8},{8,4},{5,9},{9,5},{6,10},{10,6},{7,11},{11,7},{20,24},{24,20... | collective-permute-start | bytes 393224 | tf_op jit(solution)/shard_map/ppermute | solution.py:41
  98.9 9.9 %all-to-all-start = ((f32[4,24,256]{2,1,0:T(8,128)}), f32[4,24,256]{2,1,0:T(8,128)S(1)}, u32[]{:S(2)}, u32[]{:S(2)}) async-start(f32[4,24,256]{2,1,0:T(8,128)} %patch_stats.1), calls=%async_computation | async-start | bytes 196608 | tf_op jit(solution)/shard_map/all_to_all | solution.py:19
  109.5 23.8 %all-to-all-start.1 = ((f32[16,1,128]{2,1,0:T(1,128)}), f32[16,1,128]{2,1,0:T(1,128)S(1)}, u32[]{:S(2)}, u32[]{:S(2)}) async-start(f32[16,1,128]{2,1,0:T(1,128)} %get-tuple-element.21), calls=%async_computation.1 | async-start | bytes 16384 | tf_op jit(solution)/shard_map/all_to_all | solution.py:320
Sparse Core Ops, SparseCore 0:
  24.5 44.0 all-gather.2

commit v4 on v3

--- a/solution.py
+++ b/solution.py
@@ -20,16 +20,11 @@
 
 
 def gathered_heads(teacher_head, student_head, tiles):
-    classes = teacher_head.shape[1]
+    cut, classes = teacher_head.shape
     own = jnp.concatenate([teacher_head, student_head])
     own = jnp.pad(own, ((0, 0), (0, LANES - classes)))
-    other = lax.ppermute(own, "space", [(t, t ^ 1) for t in range(tiles)])
-    first = lax.axis_index("space") % 2 == 0
-    even, odd = jnp.where(first, own, other), jnp.where(first, other, own)
-    cut = teacher_head.shape[0]
-    pair = jnp.concatenate([even[:cut], odd[:cut], even[cut:], odd[cut:]])
-    groups = [list(range(z, tiles, 2)) for z in range(2)]
-    return lax.all_gather(pair, "space", axis_index_groups=groups)
+    everyone = exchange(copies(own, tiles), "space")
+    return everyone[:, :cut].reshape(-1, LANES), everyone[:, cut:].reshape(-1, LANES)
 
 
 def swapped(block, pairs, parts, shift):
@@ -71,10 +66,6 @@
     return [rows[k : k + 1] for k in range(len(columns))]
 
 
-def tile_spec(edge, width):
-    return pl.BlockSpec((1, 1, edge, edge, width), lambda i: (i, 0, 0, 0, 0))
-
-
 def whole_spec(shape):
     return pl.BlockSpec(shape, lambda i: (0,) * len(shape))
 
@@ -84,70 +75,70 @@
 
 
 def teacher_kernel(
-    edge, place_ref, tokens_ref, corner_ref, heads_ref, logits_ref, row_a, row_b, column_a, column_b, corners_ref, head_ref
+    place_ref,
+    source,
+    corner_ref,
+    head_ref,
+    logits_ref,
+    row_a,
+    row_b,
+    column_a,
+    column_b,
+    corners_ref,
+    tokens_ref,
+    semaphores,
 ):
-    patches = edge * edge
-
-    @pl.when(pl.program_id(0) == 0)
-    def _():
-        pairs = heads_ref.shape[0]
-        cut = head_ref.shape[0] // pairs
-        for k in range(pairs):
-            head_ref[k * cut : (k + 1) * cut, :] = heads_ref[k, :cut, :]
-        corners_ref[...] = jnp.dot(corner_ref[...], head_ref[...], preferred_element_type=F32)
-
-    tokens = tokens_ref[0, 0].reshape(patches, tokens_ref.shape[-1])
-    logits = jnp.dot(tokens, head_ref[...], preferred_element_type=F32)
-    logits_ref[0] = logits
-    cube = logits.reshape(edge, edge, LANES)
+    images, edge, _, width = tokens_ref.shape
+    moves = [pltpu.make_async_copy(source.at[i, 0], tokens_ref.at[i], semaphores.at[i]) for i in range(images)]
+    for move in moves:
+        move.start()
     row_even, column_even = place_ref[3] == 1, place_ref[4] == 1
-    first, last = cube[0], cube[edge - 1]
-    row_a[0] = jnp.where(row_even, last, first)
-    row_b[0] = jnp.where(row_even, first, last)
-    left, right = cube[:, 0, :], cube[:, edge - 1, :]
-    column_a[0] = jnp.where(column_even, right, left)
-    column_b[0] = jnp.where(column_even, left, right)
-
-
-def teacher_logits(place, tokens, corner_tokens, heads):
+    corners_ref[...] = jnp.dot(corner_ref[...], head_ref[...], preferred_element_type=F32)
+    for i, move in enumerate(moves):
+        move.wait()
+        tokens = tokens_ref[i].reshape(edge * edge, width)
+        logits = jnp.dot(tokens, head_ref[...], preferred_element_type=F32)
+        logits_ref[i] = logits
+        cube = logits.reshape(edge, edge, LANES)
+        first, last = cube[0], cube[edge - 1]
+        row_a[i] = jnp.where(row_even, last, first)
+        row_b[i] = jnp.where(row_even, first, last)
+        left, right = cube[:, 0, :], cube[:, edge - 1, :]
+        column_a[i] = jnp.where(column_even, right, left)
+        column_b[i] = jnp.where(column_even, left, right)
+
+
+def teacher_logits(place, tokens, corner_tokens, head):
     images, _, edge, _, width = tokens.shape
     corners = corner_tokens.shape[0]
     patches = edge * edge
     border = jax.ShapeDtypeStruct((images, edge, LANES), F32)
+    whole = pl.BlockSpec(memory_space=pltpu.VMEM)
     return pl.pallas_call(
-        lambda *refs: teacher_kernel(edge, *refs),
-        grid=(images,),
+        teacher_kernel,
         in_specs=[
             pl.BlockSpec(memory_space=pltpu.SMEM),
-            tile_spec(edge, width),
-            whole_spec(corner_tokens.shape),
-            whole_spec(heads.shape),
+            pl.BlockSpec(memory_space=pltpu.HBM),
+            whole,
+            whole,
         ],
-        out_specs=[image_spec(patches)] + [image_spec(edge)] * 4 + [whole_spec((corners, LANES))],
+        out_specs=[whole] * 6,
         out_shape=[jax.ShapeDtypeStruct((images, patches, LANES), F32)]
         + [border] * 4
         + [jax.ShapeDtypeStruct((corners, LANES), F32)],
-        scratch_shapes=[pltpu.VMEM((width, LANES), heads.dtype)],
-        compiler_params=pltpu.CompilerParams(vmem_limit_bytes=16 * 2**20),
+        scratch_shapes=[pltpu.VMEM((images, edge, edge, width), tokens.dtype), pltpu.SemaphoreType.DMA((images,))],
+        compiler_params=pltpu.CompilerParams(vmem_limit_bytes=50 * 2**20),
         cost_estimate=pl.CostEstimate(
             flops=2 * images * patches * width * LANES,
-            bytes_accessed=tokens.size * 2 + heads.size * 2 + images * patches * LANES * 4,
+            bytes_accessed=tokens.size * 2 + head.size * 2 + images * patches * LANES * 4,
             transcendentals=0,
         ),
         name="teacher_logits",
-    )(place, tokens, corner_tokens, heads)
-
-
-def student_kernel(edge, classes, tokens_ref, heads_ref, logits_ref, lse_ref, head_ref):
-    @pl.when(pl.program_id(0) == 0)
-    def _():
-        pairs = heads_ref.shape[0]
-        rest = head_ref.shape[0] // pairs
-        cut = heads_ref.shape[1] - rest
-        for k in range(pairs):
-            head_ref[k * rest : (k + 1) * rest, :] = heads_ref[k, cut:, :]
-
-    tokens = tokens_ref[0, 0].reshape(edge * edge, tokens_ref.shape[-1])
+    )(place, tokens, corner_tokens, head)
+
+
+def student_kernel(edge, classes, tokens_ref, head_ref, logits_ref, lse_ref):
+    tokens = tokens_ref[pl.program_id(0), 0].reshape(edge * edge, tokens_ref.shape[-1])
     logits = jnp.dot(tokens, head_ref[...], preferred_element_type=F32)
     logits_ref[0] = logits
     logits = logits[:, :classes]
@@ -157,27 +148,26 @@
     lse_ref[pl.ds(pl.program_id(0), 1), :] = top + jnp.log(total)
 
 
-def student_logits(tokens, heads, classes):
+def student_logits(tokens, head, classes):
     images, _, edge, _, width = tokens.shape
     patches = edge * edge
     return pl.pallas_call(
         lambda *refs: student_kernel(edge, classes, *refs),
         grid=(images,),
-        in_specs=[tile_spec(edge, width), whole_spec(heads.shape)],
+        in_specs=[pl.BlockSpec(memory_space=pltpu.VMEM), whole_spec(head.shape)],
         out_specs=[image_spec(patches), whole_spec((images, patches))],
         out_shape=[
             jax.ShapeDtypeStruct((images, patches, LANES), F32),
             jax.ShapeDtypeStruct((images, patches), F32),
         ],
-        scratch_shapes=[pltpu.VMEM((width, LANES), heads.dtype)],
         compiler_params=pltpu.CompilerParams(vmem_limit_bytes=16 * 2**20),
         cost_estimate=pl.CostEstimate(
             flops=2 * images * patches * width * LANES,
-            bytes_accessed=tokens.size * 2 + heads.size * 2 + images * patches * LANES * 4,
+            bytes_accessed=tokens.size * 2 + head.size * 2 + images * patches * LANES * 4,
             transcendentals=images * patches * LANES,
         ),
         name="student_logits",
-    )(tokens, heads)
+    )(tokens, head)
 
 
 def stats_kernel(
@@ -334,19 +324,20 @@
     flags = valid.reshape(images, edge * edge)
     place = jnp.stack([row * edge, column * edge, side * edge, 1 - row % 2, 1 - column % 2]).astype(jnp.int32)
 
-    heads = gathered_heads(teacher_head, student_head, tiles)
+    head_t, head_s = gathered_heads(teacher_head, student_head, tiles)
     around = ((-1, -1, -1, -1), (-1, 1, -1, 0), (1, -1, 0, -1), (1, 1, 0, 0))
     corner_tokens = jnp.concatenate(
         [neighbour(teacher_tokens[:, 0, y, x], side, down, right) for down, right, y, x in around]
     )
-    logits, row_a, row_b, column_a, column_b, corners = teacher_logits(place, teacher_tokens, corner_tokens, heads)
-    borders = [
-        swapped(row_a, pairs_of(side, 0, 1, 0), parts, 0),
-        swapped(row_b, pairs_of(side, 1, 1, 0), parts, 0),
-        swapped(column_a, pairs_of(side, 0, 0, 1), parts, 0),
-        swapped(column_b, pairs_of(side, 1, 0, 1), parts, 0),
-    ]
-    student, lse_s = student_logits(student_tokens, heads, classes)
+    logits, row_a, row_b, column_a, column_b, corners = teacher_logits(
+        place, teacher_tokens, corner_tokens, head_t
+    )
+    column_a = swapped(column_a, pairs_of(side, 0, 0, 1), parts, 0)
+    column_b = swapped(column_b, pairs_of(side, 1, 0, 1), parts, 0)
+    row_a = swapped(row_a, pairs_of(side, 0, 1, 0), parts, 0)
+    row_b = swapped(row_b, pairs_of(side, 1, 1, 0), parts, 0)
+    borders = [row_a, row_b, column_a, column_b]
+    student, lse_s = student_logits(student_tokens, head_s, classes)
     stats = patch_stats(place, student, lse_s, logits, borders, corners, classes, parts)
     stats = exchange(stats, "mp")
     divergence, totals = patch_divergence(stats, flags, tiles)

time: 141 us -> 136 us (0.965)
  between operations: 14.3 us -> 0.9 us
  waiting for transfers between devices: 49.2 us -> 55.7 us
  starting transfers between devices: 54.2 us -> 57.6 us
  local copies, waits for them, and re-layouts: 6.25 us -> 3.53 us
  Pallas kernels: 13.9 us -> 16.3 us
  other arithmetic: 2.99 us -> 1.47 us
    ppermute x4, waiting for transfers between devices: 14.9 us -> 34.8 us  [neighbour(): return lax.ppermute(block, 'space', route)]
    all_to_all x1 -> x2, starting transfers between devices: 4.09 us -> 19 us  [exchange(): return lax.all_to_all(x, axis, split_axis=0, concat_axis=0, tiled=True)]
    all_gather x1 -> x0, waiting for transfers between devices: 14.8 us -> none  [gathered_heads(): return lax.all_gather(pair, 'space', axis_index_groups=groups)]
    ppermute x1 -> x0, starting transfers between devices: 10.9 us -> none  [gathered_heads(): other = lax.ppermute(own, 'space', [(t, t ^ 1) for t in range(tiles)])]
    ppermute x4, waiting for transfers between devices: 0.02 us -> 5.25 us  [swapped(): return lax.ppermute(block, ('space', 'mp'), route)]
    unnamed x14 -> x10, local copies, waits for them, and re-layouts: 4.01 us -> 0.04 us
    ppermute x1 -> x0, waiting for transfers between devices: 3.75 us -> none  [gathered_heads(): other = lax.ppermute(own, 'space', [(t, t ^ 1) for t in range(tiles)])]
    all_to_all x1, starting transfers between devices: 13.2 us -> 15.7 us  [everywhere_sum(): lax.all_to_all(x, ('space', 'mp'), split_axis=0, concat_axis=0, tiled=Tru...]
  transfers between devices with their start and end apart: 12 -> 11, of which waited for: 5 -> 5; matrix products, arithmetic and copies ran while one was open for 2% -> 2% of each run, Pallas kernels for 3% -> 3%
where the time goes in v4:
time: 136 us; the launch traced here: 135 us
  starting transfers between devices  57.6 us (42%)
  waiting for transfers between devices  55.7 us (41%)
  Pallas kernels  16.3 us (12%)
  local copies, waits for them, and re-layouts  3.53 us (3%)
  other arithmetic  1.47 us (1%)
    ppermute x4, waiting for transfers between devices, neighbour(): return lax.ppermute(block, 'space', route)  34.8 us
    all_to_all x2, starting transfers between devices, exchange(): return lax.all_to_all(x, axis, split_axis=0, concat_axis=0, tiled=True)  19 us
    all_to_all x1, starting transfers between devices, everywhere_sum(): lax.all_to_all(x, ('space', 'mp'), split_axis=0, concat_axis=0, tiled=Tru...  15.7 us
    ppermute x4, starting transfers between devices, neighbour(): return lax.ppermute(block, 'space', route)  12.1 us
    ppermute x4, starting transfers between devices, swapped(): return lax.ppermute(block, ('space', 'mp'), route)  10.8 us
    all_to_all x1, waiting for transfers between devices, everywhere_sum(): lax.all_to_all(x, ('space', 'mp'), split_axis=0, concat_axis=0, tiled=Tru...  9.9 us
    pallas_call x1, Pallas kernels, teacher_logits(): pl.pallas_call(teacher_kernel, in_specs=[pl.BlockSpec(memory_space=pltpu....  6.45 us
    all_to_all x2, waiting for transfers between devices, exchange(): return lax.all_to_all(x, axis, split_axis=0, concat_axis=0, tiled=True)  5.7 us
  transfers between devices with their start and end apart: 11, of which 5 were waited for; matrix products, arithmetic and copies ran while one was open for 2% of the time, Pallas kernels for 3%

profile of v4, /device:TPU:6, one launch (start us, length us, event | category | flops | bytes accessed | tf_op | source)
XLA Modules:
  0.0 135.5 jit_solution(17377976069728333575)
XLA Ops:
  0.6 0.8 fusion.2
  1.5 1.2 broadcast_in_dim.3
  2.6 15.6 %all-to-all-start = ((bf16[16,168,256]{2,1,0:T(8,128)(2,1)}), bf16[16,168,256]{2,1,0:T(8,128)(2,1)S(1)}, u32[]{:S(2)}, u32[]{:S(2)}) async-start(bf16[16,168,256]{2,1,0:T(8,128)(2,1)} %broadcast_in_dim.3), calls=%async_computation | async-start | bytes 2752512 | tf_op jit(solution)/shard_map/all_to_all | solution.py:19
  18.3 1.3 fusion.3
  19.7 9.5 %collective-permute-start = (bf16[8,1408]{1,0:T(8,128)(2,1)S(1)}, bf16[8,1408]{1,0:T(8,128)(2,1)S(1)}, u32[]{:S(2)}, u32[]{:S(2)}) collective-permute-start(bf16[8,1408]{1,0:T(8,128)(2,1)S(1)} %bitcast.26), channel_id=1, source_target_pairs={{0,20},{4,24},{8,28},{16,36},{20,40},{24,44},{32,52},{36,56},{40,6... | collective-permute-start | bytes 67592 | tf_op jit(solution)/shard_map/ppermute | solution.py:56
  29.2 0.7 collective-permute-start.1
  29.9 0.7 collective-permute-start.2
  30.6 1.3 collective-permute-start.3
  31.9 0.1 stack.19.place_ref.refs_0_
  32.0 16.4 %collective-permute-done = bf16[8,1408]{1,0:T(8,128)(2,1)S(1)} collective-permute-done((bf16[8,1408]{1,0:T(8,128)(2,1)S(1)}, bf16[8,1408]{1,0:T(8,128)(2,1)S(1)}, u32[]{:S(2)}, u32[]{:S(2)}) %collective-permute-start) | collective-permute-done | bytes 22560 | tf_op jit(solution)/shard_map/ppermute | solution.py:56
  48.4 0.0 collective-permute-done.1
  48.4 0.0 collective-permute-done.2
  48.4 18.4 %collective-permute-done.3 = bf16[8,1408]{1,0:T(8,128)(2,1)S(1)} collective-permute-done((bf16[8,1408]{1,0:T(8,128)(2,1)S(1)}, bf16[8,1408]{1,0:T(8,128)(2,1)S(1)}, u32[]{:S(2)}, u32[]{:S(2)}) %collective-permute-start.3) | collective-permute-done | bytes 22560 | tf_op jit(solution)/shard_map/ppermute | solution.py:56
  66.9 0.0 slice-start
  66.9 0.0 all-to-all-done
  66.9 0.0 slice-start.1
  67.0 6.5 %teacher_logits.1 = (f32[8,256,256]{2,1,0:T(8,128)S(1)}, f32[8,16,256]{2,1,0:T(8,128)S(1)}, f32[8,16,256]{2,1,0:T(8,128)S(1)}, f32[8,16,256]{2,1,0:T(8,128)S(1)}...) custom-call(s32[5]{0:T(128)S(1)} %stack.19.place_ref.refs_0_, bf16[8,1,16,16,1408]{4,3,2,1,0:T(8,128)(2,1)} %source.1, ...), custom_call_target="tpu_custom_call" | custom-call | flops 1476395008 | bytes 8585216 | tf_op jit(solution)/shard_map/teacher_logits/pallas_call | solution.py:117
  73.4 7.5 %collective-permute-start.4 = (f32[8,16,256]{2,1,0:T(8,128)S(1)}, f32[8,16,256]{2,1,0:T(8,128)S(1)}, u32[]{:S(2)}, u32[]{:S(2)}) collective-permute-start(f32[8,16,256]{2,1,0:T(8,128)S(1)} %get-tuple-element.15), channel_id=1, source_target_pairs={{0,16},{16,0},{1,17},{17,1},{2,18},{18,2},{3,19},{19,3},{4,20},{20... | collective-permute-start | bytes 393224 | tf_op jit(solution)/shard_map/ppermute | solution.py:36
  80.9 0.7 collective-permute-start.5
  81.6 1.9 %collective-permute-start.6 = (f32[8,16,256]{2,1,0:T(8,128)S(1)}, f32[8,16,256]{2,1,0:T(8,128)S(1)}, u32[]{:S(2)}, u32[]{:S(2)}) collective-permute-start(f32[8,16,256]{2,1,0:T(8,128)S(1)} %get-tuple-element.17), channel_id=1, source_target_pairs={{0,4},{4,0},{1,5},{5,1},{2,6},{6,2},{3,7},{7,3},{8,12},{12,8},{9,1... | collective-permute-start | bytes 393224 | tf_op jit(solution)/shard_map/ppermute | solution.py:36
  83.5 0.7 collective-permute-start.7
  84.3 0.0 slice-done
  84.3 0.0 slice-done.1
  84.3 4.4 %student_logits.1 = (f32[8,256,256]{2,1,0:T(8,128)S(1)}, f32[8,256]{1,0:T(8,128)S(1)}) custom-call(bf16[8,1,16,16,1280]{4,3,2,1,0:T(8,128)(2,1)S(1)} %bitcast.22, bf16[1280,256]{1,0:T(8,128)(2,1)S(1)} %bitcast.24), custom_call_target="tpu_custom_call" | custom-call | flops 1342177280 | bytes 7995392 | tf_op jit(solution)/shard_map/student_logits/pallas_call | solution.py:154
  88.7 0.0 collective-permute-done.4.refs_4_
  88.7 0.0 collective-permute-done.5.refs_5_
  88.8 5.2 %collective-permute-done.6.refs_6_ = f32[8,16,256]{2,1,0:T(8,128)S(1)} collective-permute-done((f32[8,16,256]{2,1,0:T(8,128)S(1)}, f32[8,16,256]{2,1,0:T(8,128)S(1)}, u32[]{:S(2)}, u32[]{:S(2)}) %collective-permute-start.6) | collective-permute-done | bytes 131104 | tf_op jit(solution)/shard_map/ppermute | solution.py:36
  94.0 0.0 collective-permute-done.7.refs_7_
  94.0 0.0 copy-start
  94.0 4.7 %patch_stats.1 = f32[4,24,256]{2,1,0:T(8,128)} custom-call(s32[5]{0:T(128)S(1)} %stack.19.place_ref.refs_0_, f32[8,256,256]{2,1,0:T(8,128)S(1)} %get-tuple-element.12.refs_1_, f32[8,256]{1,0:T(8,128)S(1)} %get-tuple-element.13.refs_2_, f32[8,256,256]{2,1,0:T(8,128)S(1)} %get-tuple-element.14.refs_3_, f32[8,16,256]{2,1,0:T(8,128)S(1)} %collective-permute-done.4.refs_4_, ...), custom_call_target="tpu_custom_call" | custom-call | flops 15728640 | bytes 4194304 | tf_op jit(solution)/shard_map/patch_stats/pallas_call | solution.py:244
  98.7 3.3 %all-to-all-start.1 = ((f32[4,24,256]{2,1,0:T(8,128)}), f32[4,24,256]{2,1,0:T(8,128)S(1)}, u32[]{:S(2)}, u32[]{:S(2)}) async-start(f32[4,24,256]{2,1,0:T(8,128)} %patch_stats.1), calls=%async_computation.1 | async-start | bytes 196608 | tf_op jit(solution)/shard_map/all_to_all | solution.py:19
  102.0 0.0 copy-done
  102.0 0.1 reshape.18.refs_1_
  102.1 5.7 %all-to-all-done.1.refs_0_ = f32[4,24,256]{2,1,0:T(8,128)S(1)} async-done(((f32[4,24,256]{2,1,0:T(8,128)}), f32[4,24,256]{2,1,0:T(8,128)S(1)}, u32[]{:S(2)}, u32[]{:S(2)}) %all-to-all-start.1) | async-done | bytes 98336 | tf_op jit(solution)/shard_map/all_to_all | solution.py:19
  107.8 0.7 patch_divergence.1
  108.5 15.7 %all-to-all-start.2 = ((f32[16,1,128]{2,1,0:T(1,128)}), f32[16,1,128]{2,1,0:T(1,128)S(1)}, u32[]{:S(2)}, u32[]{:S(2)}) async-start(f32[16,1,128]{2,1,0:T(1,128)} %get-tuple-element.21), calls=%async_computation.2 | async-start | bytes 16384 | tf_op jit(solution)/shard_map/all_to_all | solution.py:310
  124.2 0.7 reshape.19
  125.0 9.9 %all-to-all-done.2 = f32[16,1,128]{2,1,0:T(1,128)S(1)} async-done(((f32[16,1,128]{2,1,0:T(1,128)}), f32[16,1,128]{2,1,0:T(1,128)S(1)}, u32[]{:S(2)}, u32[]{:S(2)}) %all-to-all-start.2) | async-done | bytes 8224 | tf_op jit(solution)/shard_map/all_to_all | solution.py:310
  134.9 0.6 maximum_divide_fusion
  (9 shorter events, 0.2 us)
Async XLA Ops:
  2.6 64.2 %all-to-all-start = ((bf16[16,168,256]{2,1,0:T(8,128)(2,1)}), bf16[16,168,256]{2,1,0:T(8,128)(2,1)S(1)}, u32[]{:S(2)}, u32[]{:S(2)}) async-start(bf16[16,168,256]{2,1,0:T(8,128)(2,1)} %broadcast_in_dim.3), calls=%async_computation | async-start | bytes 2752512 | tf_op jit(solution)/shard_map/all_to_all | solution.py:19
  19.7 28.8 %collective-permute-start = (bf16[8,1408]{1,0:T(8,128)(2,1)S(1)}, bf16[8,1408]{1,0:T(8,128)(2,1)S(1)}, u32[]{:S(2)}, u32[]{:S(2)}) collective-permute-start(bf16[8,1408]{1,0:T(8,128)(2,1)S(1)} %bitcast.26), channel_id=1, source_target_pairs={{0,20},{4,24},{8,28},{16,36},{20,40},{24,44},{32,52},{36,56},{40,6... | collective-permute-start | bytes 67592 | tf_op jit(solution)/shard_map/ppermute | solution.py:56
  29.2 19.2 %collective-permute-start.1 = (bf16[8,1408]{1,0:T(8,128)(2,1)S(1)}, bf16[8,1408]{1,0:T(8,128)(2,1)S(1)}, u32[]{:S(2)}, u32[]{:S(2)}) collective-permute-start(bf16[8,1408]{1,0:T(8,128)(2,1)S(1)} %bitcast.27), channel_id=1, source_target_pairs={{4,16},{8,20},{12,24},{20,32},{24,36},{28,40},{36,48},{40,52},{44,... | collective-permute-start | bytes 67592 | tf_op jit(solution)/shard_map/ppermute | solution.py:56
  29.9 18.5 %collective-permute-start.2 = (bf16[8,1408]{1,0:T(8,128)(2,1)S(1)}, bf16[8,1408]{1,0:T(8,128)(2,1)S(1)}, u32[]{:S(2)}, u32[]{:S(2)}) collective-permute-start(bf16[8,1408]{1,0:T(8,128)(2,1)S(1)} %bitcast.28), channel_id=1, source_target_pairs={{16,4},{20,8},{24,12},{32,20},{36,24},{40,28},{48,36},{52,40},{56,... | collective-permute-start | bytes 67592 | tf_op jit(solution)/shard_map/ppermute | solution.py:56
  30.6 36.3 %collective-permute-start.3 = (bf16[8,1408]{1,0:T(8,128)(2,1)S(1)}, bf16[8,1408]{1,0:T(8,128)(2,1)S(1)}, u32[]{:S(2)}, u32[]{:S(2)}) collective-permute-start(bf16[8,1408]{1,0:T(8,128)(2,1)S(1)} %bitcast.29), channel_id=1, source_target_pairs={{20,0},{24,4},{28,8},{36,16},{40,20},{44,24},{52,32},{56,36},{60,4... | collective-permute-start | bytes 67592 | tf_op jit(solution)/shard_map/ppermute | solution.py:56
  66.9 17.4 %slice-start = ((s8[5242880]{0:T(1024)(128)(4,1)}), s8[1048576]{0:T(1024)(128)(4,1)S(1)}, s32[]{:S(2)}) async-start(s8[5242880]{0:T(1024)(128)(4,1)} %bitcast.21), calls=%async_computation.3 | async-start | bytes 2097152
  66.9 17.3 %slice-start.1 = ((s8[5242880]{0:T(1024)(128)(4,1)}), s8[4194304]{0:T(1024)(128)(4,1)S(1)}, s32[]{:S(2)}) async-start(s8[5242880]{0:T(1024)(128)(4,1)} %bitcast.21), calls=%async_computation.4 | async-start | bytes 8388608
  73.4 15.3 %collective-permute-start.4 = (f32[8,16,256]{2,1,0:T(8,128)S(1)}, f32[8,16,256]{2,1,0:T(8,128)S(1)}, u32[]{:S(2)}, u32[]{:S(2)}) collective-permute-start(f32[8,16,256]{2,1,0:T(8,128)S(1)} %get-tuple-element.15), channel_id=1, source_target_pairs={{0,16},{16,0},{1,17},{17,1},{2,18},{18,2},{3,19},{19,3},{4,20},{20... | collective-permute-start | bytes 393224 | tf_op jit(solution)/shard_map/ppermute | solution.py:36
  80.9 7.8 %collective-permute-start.5 = (f32[8,16,256]{2,1,0:T(8,128)S(1)}, f32[8,16,256]{2,1,0:T(8,128)S(1)}, u32[]{:S(2)}, u32[]{:S(2)}) collective-permute-start(f32[8,16,256]{2,1,0:T(8,128)S(1)} %get-tuple-element.16), channel_id=1, source_target_pairs={{16,32},{32,16},{17,33},{33,17},{18,34},{34,18},{19,35},{35,19},{2... | collective-permute-start | bytes 393224 | tf_op jit(solution)/shard_map/ppermute | solution.py:36
  81.6 12.4 %collective-permute-start.6 = (f32[8,16,256]{2,1,0:T(8,128)S(1)}, f32[8,16,256]{2,1,0:T(8,128)S(1)}, u32[]{:S(2)}, u32[]{:S(2)}) collective-permute-start(f32[8,16,256]{2,1,0:T(8,128)S(1)} %get-tuple-element.17), channel_id=1, source_target_pairs={{0,4},{4,0},{1,5},{5,1},{2,6},{6,2},{3,7},{7,3},{8,12},{12,8},{9,1... | collective-permute-start | bytes 393224 | tf_op jit(solution)/shard_map/ppermute | solution.py:36
  83.5 10.5 %collective-permute-start.7 = (f32[8,16,256]{2,1,0:T(8,128)S(1)}, f32[8,16,256]{2,1,0:T(8,128)S(1)}, u32[]{:S(2)}, u32[]{:S(2)}) collective-permute-start(f32[8,16,256]{2,1,0:T(8,128)S(1)} %get-tuple-element.18), channel_id=1, source_target_pairs={{4,8},{8,4},{5,9},{9,5},{6,10},{10,6},{7,11},{11,7},{20,24},{24,20... | collective-permute-start | bytes 393224 | tf_op jit(solution)/shard_map/ppermute | solution.py:36
  94.0 8.0 %copy-start = (s32[8,1,16,16]{3,2,1,0:T(8,128)S(1)}, s32[8,1,16,16]{3,2,1,0:T(8,128)}, u32[]{:S(2)}) copy-start(s32[8,1,16,16]{3,2,1,0:T(8,128)} %param.9) | copy-start | bytes 24580
  98.7 9.1 %all-to-all-start.1 = ((f32[4,24,256]{2,1,0:T(8,128)}), f32[4,24,256]{2,1,0:T(8,128)S(1)}, u32[]{:S(2)}, u32[]{:S(2)}) async-start(f32[4,24,256]{2,1,0:T(8,128)} %patch_stats.1), calls=%async_computation.1 | async-start | bytes 196608 | tf_op jit(solution)/shard_map/all_to_all | solution.py:19
  108.5 26.3 %all-to-all-start.2 = ((f32[16,1,128]{2,1,0:T(1,128)}), f32[16,1,128]{2,1,0:T(1,128)S(1)}, u32[]{:S(2)}, u32[]{:S(2)}) async-start(f32[16,1,128]{2,1,0:T(1,128)} %get-tuple-element.21), calls=%async_computation.2 | async-start | bytes 16384 | tf_op jit(solution)/shard_map/all_to_all | solution.py:310

commit v5 on v4

--- a/solution.py
+++ b/solution.py
@@ -9,6 +9,7 @@
 
 F32 = jnp.float32
 LANES = 256
+BLOCK = 4
 
 
 def copies(x, count):
@@ -19,12 +20,20 @@
     return lax.all_to_all(x, axis, split_axis=0, concat_axis=0, tiled=True)
 
 
+def padded(head):
+    return jnp.pad(head, ((0, 0), (0, LANES - head.shape[1])))
+
+
 def gathered_heads(teacher_head, student_head, tiles):
-    cut, classes = teacher_head.shape
-    own = jnp.concatenate([teacher_head, student_head])
-    own = jnp.pad(own, ((0, 0), (0, LANES - classes)))
-    everyone = exchange(copies(own, tiles), "space")
-    return everyone[:, :cut].reshape(-1, LANES), everyone[:, cut:].reshape(-1, LANES)
+    first = exchange(copies(padded(teacher_head), tiles), "space")
+    own = padded(student_head)
+    other = lax.ppermute(own, "space", [(t, t ^ 1) for t in range(tiles)])
+    even = lax.axis_index("space") % 2 == 0
+    pair = jnp.concatenate([jnp.where(even, own, other), jnp.where(even, other, own)])
+    second, first = lax.optimization_barrier((copies(pair, tiles // 2), first))
+    groups = [list(range(z, tiles, 2)) for z in range(2)]
+    second = lax.all_to_all(second, "space", split_axis=0, concat_axis=0, tiled=True, axis_index_groups=groups)
+    return first.reshape(-1, LANES), second.reshape(-1, LANES)
 
 
 def swapped(block, pairs, parts, shift):
@@ -47,15 +56,6 @@
     return pairs
 
 
-def neighbour(block, side, down, right):
-    route = []
-    for row in range(side):
-        for column in range(side):
-            if 0 <= row + down < side and 0 <= column + right < side:
-                route.append(((row + down) * side + column + right, row * side + column))
-    return lax.ppermute(block, "space", route)
-
-
 def in_lanes(columns):
     height = columns[0].shape[0]
     lane = lax.broadcasted_iota(jnp.int32, (height, 128), 1)
@@ -74,32 +74,17 @@
     return pl.BlockSpec((1, rows, LANES), lambda i: (i, 0, 0))
 
 
-def teacher_kernel(
-    place_ref,
-    source,
-    corner_ref,
-    head_ref,
-    logits_ref,
-    row_a,
-    row_b,
-    column_a,
-    column_b,
-    corners_ref,
-    tokens_ref,
-    semaphores,
-):
-    images, edge, _, width = tokens_ref.shape
-    moves = [pltpu.make_async_copy(source.at[i, 0], tokens_ref.at[i], semaphores.at[i]) for i in range(images)]
-    for move in moves:
-        move.start()
+def teacher_kernel(place_ref, tokens_ref, head_ref, logits_ref, row_a, row_b, column_a, column_b):
+    edge, width = tokens_ref.shape[2], tokens_ref.shape[-1]
+    block, patches, _ = logits_ref.shape
+    here = pl.ds(pl.program_id(0) * block, block)
+    tokens = tokens_ref[here, 0].reshape(block * patches, width)
+    logits = jnp.dot(tokens, head_ref[...], preferred_element_type=F32)
     row_even, column_even = place_ref[3] == 1, place_ref[4] == 1
-    corners_ref[...] = jnp.dot(corner_ref[...], head_ref[...], preferred_element_type=F32)
-    for i, move in enumerate(moves):
-        move.wait()
-        tokens = tokens_ref[i].reshape(edge * edge, width)
-        logits = jnp.dot(tokens, head_ref[...], preferred_element_type=F32)
-        logits_ref[i] = logits
-        cube = logits.reshape(edge, edge, LANES)
+    for i in range(block):
+        image = logits[i * patches : (i + 1) * patches]
+        logits_ref[i] = image
+        cube = image.reshape(edge, edge, LANES)
         first, last = cube[0], cube[edge - 1]
         row_a[i] = jnp.where(row_even, last, first)
         row_b[i] = jnp.where(row_even, first, last)
@@ -108,33 +93,62 @@
         column_b[i] = jnp.where(column_even, left, right)
 
 
-def teacher_logits(place, tokens, corner_tokens, head):
+def teacher_logits(place, tokens, head):
     images, _, edge, _, width = tokens.shape
-    corners = corner_tokens.shape[0]
     patches = edge * edge
+    block = math.gcd(images, BLOCK)
     border = jax.ShapeDtypeStruct((images, edge, LANES), F32)
-    whole = pl.BlockSpec(memory_space=pltpu.VMEM)
+
+    def spec(rows):
+        return pl.BlockSpec((block, rows, LANES), lambda i: (i, 0, 0))
+
     return pl.pallas_call(
         teacher_kernel,
+        grid=(images // block,),
         in_specs=[
             pl.BlockSpec(memory_space=pltpu.SMEM),
-            pl.BlockSpec(memory_space=pltpu.HBM),
-            whole,
-            whole,
+            pl.BlockSpec(memory_space=pltpu.VMEM),
+            pl.BlockSpec(memory_space=pltpu.VMEM),
         ],
-        out_specs=[whole] * 6,
-        out_shape=[jax.ShapeDtypeStruct((images, patches, LANES), F32)]
-        + [border] * 4
-        + [jax.ShapeDtypeStruct((corners, LANES), F32)],
-        scratch_shapes=[pltpu.VMEM((images, edge, edge, width), tokens.dtype), pltpu.SemaphoreType.DMA((images,))],
-        compiler_params=pltpu.CompilerParams(vmem_limit_bytes=50 * 2**20),
+        out_specs=[spec(patches)] + [spec(edge)] * 4,
+        out_shape=[jax.ShapeDtypeStruct((images, patches, LANES), F32)] + [border] * 4,
+        compiler_params=pltpu.CompilerParams(vmem_limit_bytes=16 * 2**20),
         cost_estimate=pl.CostEstimate(
             flops=2 * images * patches * width * LANES,
             bytes_accessed=tokens.size * 2 + head.size * 2 + images * patches * LANES * 4,
             transcendentals=0,
         ),
         name="teacher_logits",
-    )(place, tokens, corner_tokens, head)
+    )(place, tokens, head)
+
+
+def row_kernel(place_ref, row_a, row_b, column_a, column_b, out_a, out_b):
+    images, edge, _ = row_a.shape
+    row_even, column_even = place_ref[3] == 1, place_ref[4] == 1
+    left = jnp.where(column_even, column_b[...], column_a[...])
+    right = jnp.where(column_even, column_a[...], column_b[...])
+    x = lax.broadcasted_iota(jnp.int32, (edge, LANES), 0)
+    for row, out, at_end in ((row_a, out_a, row_even), (row_b, out_b, ~row_even)):
+        for i in range(images):
+            line = row[i]
+            start = jnp.where(at_end, left[i, edge - 1 :], left[i, :1])
+            end = jnp.where(at_end, right[i, edge - 1 :], right[i, :1])
+            before = jnp.where(x == 0, start, pltpu.roll(line, 1, 0))
+            after = jnp.where(x == edge - 1, end, pltpu.roll(line, edge - 1, 0))
+            out[i] = line + before + after
+
+
+def row_sums(place, row_a, row_b, column_a, column_b):
+    whole = pl.BlockSpec(memory_space=pltpu.VMEM)
+    return pl.pallas_call(
+        row_kernel,
+        in_specs=[pl.BlockSpec(memory_space=pltpu.SMEM)] + [whole] * 4,
+        out_specs=[whole] * 2,
+        out_shape=[jax.ShapeDtypeStruct(row_a.shape, F32)] * 2,
+        compiler_params=pltpu.CompilerParams(vmem_limit_bytes=4 * 2**20),
+        cost_estimate=pl.CostEstimate(flops=10 * row_a.size, bytes_accessed=24 * row_a.size, transcendentals=0),
+        name="row_sums",
+    )(place, row_a, row_b, column_a, column_b)
 
 
 def student_kernel(edge, classes, tokens_ref, head_ref, logits_ref, lse_ref):
@@ -183,7 +197,6 @@
     row_b,
     column_a,
     column_b,
-    corners_ref,
     out_ref,
 ):
     image = pl.program_id(0)
@@ -191,30 +204,19 @@
     shape = (edge, edge, LANES)
     row_even, column_even = place_ref[3] == 1, place_ref[4] == 1
 
+    flat = logits_ref[0]
+    cube = flat.reshape(shape)
+    x = lax.broadcasted_iota(jnp.int32, shape, 1)
+    to_left = jnp.broadcast_to(jnp.where(column_even, column_b[0], column_a[0])[:, None, :], shape)
+    to_right = jnp.broadcast_to(jnp.where(column_even, column_a[0], column_b[0])[:, None, :], shape)
+    before = jnp.where(x == 0, to_left, pltpu.roll(flat, 1, 0).reshape(shape))
+    after = jnp.where(x == edge - 1, to_right, pltpu.roll(flat, patches - 1, 0).reshape(shape))
+    rows = cube + before + after
     up = jnp.where(row_even, row_b[0], row_a[0])
     down = jnp.where(row_even, row_a[0], row_b[0])
-    cube = logits_ref[0].reshape(shape)
-    above = jnp.concatenate([up[None], cube[:-1]], axis=0)
-    below = jnp.concatenate([cube[1:], down[None]], axis=0)
-    columns = above + cube + below
-    flat = columns.reshape(patches, LANES)
-
-    y = lax.broadcasted_iota(jnp.int32, (edge, LANES), 0)
-
-    def corner(k):
-        return corners_ref[pl.ds(k * images + image, 1), :]
-
-    def side_column(line, top, bottom):
-        over = jnp.where(y == 0, top, pltpu.roll(line, 1, 0))
-        under = jnp.where(y == edge - 1, bottom, pltpu.roll(line, edge - 1, 0))
-        return jnp.broadcast_to((line + over + under)[:, None, :], shape)
-
-    x = lax.broadcasted_iota(jnp.int32, shape, 1)
-    to_left = side_column(jnp.where(column_even, column_b[0], column_a[0]), corner(0), corner(2))
-    to_right = side_column(jnp.where(column_even, column_a[0], column_b[0]), corner(1), corner(3))
-    before = jnp.where(x == 0, to_left, pltpu.roll(flat, 1, 0).reshape(shape))
-    after = jnp.where(x == edge - 1, to_right, pltpu.roll(flat, patches - 1, 0).reshape(shape))
-    total = columns + before + after
+    above = jnp.concatenate([up[None], rows[:-1]], axis=0)
+    below = jnp.concatenate([rows[1:], down[None]], axis=0)
+    total = rows + above + below
 
     extent = place_ref[2]
     place_y = place_ref[0] + lax.broadcasted_iota(jnp.int32, (edge, edge, 1), 0)
@@ -238,7 +240,7 @@
             out_ref[c, pl.ds(k * images + image, 1), :] = stat
 
 
-def patch_stats(place, student, lse_s, logits, borders, corners, classes, parts):
+def patch_stats(place, student, lse_s, logits, borders, classes, parts):
     images, patches, _ = logits.shape
     edge = borders[0].shape[1]
     return pl.pallas_call(
@@ -250,7 +252,6 @@
             whole_spec((images, patches)),
             image_spec(patches),
             *[image_spec(edge)] * 4,
-            whole_spec(corners.shape),
         ],
         out_specs=whole_spec((parts, 3 * images, patches)),
         out_shape=jax.ShapeDtypeStruct((parts, 3 * images, patches), F32),
@@ -261,7 +262,7 @@
             transcendentals=images * patches * LANES,
         ),
         name="patch_stats",
-    )(place, student, lse_s, logits, *borders, corners)
+    )(place, student, lse_s, logits, *borders)
 
 
 def divergence_kernel(images, tiles, stats_ref, valid_ref, divergence_ref, totals_ref):
@@ -325,20 +326,14 @@
     place = jnp.stack([row * edge, column * edge, side * edge, 1 - row % 2, 1 - column % 2]).astype(jnp.int32)
 
     head_t, head_s = gathered_heads(teacher_head, student_head, tiles)
-    around = ((-1, -1, -1, -1), (-1, 1, -1, 0), (1, -1, 0, -1), (1, 1, 0, 0))
-    corner_tokens = jnp.concatenate(
-        [neighbour(teacher_tokens[:, 0, y, x], side, down, right) for down, right, y, x in around]
-    )
-    logits, row_a, row_b, column_a, column_b, corners = teacher_logits(
-        place, teacher_tokens, corner_tokens, head_t
-    )
+    logits, row_a, row_b, column_a, column_b = teacher_logits(place, teacher_tokens, head_t)
     column_a = swapped(column_a, pairs_of(side, 0, 0, 1), parts, 0)
     column_b = swapped(column_b, pairs_of(side, 1, 0, 1), parts, 0)
+    row_a, row_b = row_sums(place, row_a, row_b, column_a, column_b)
     row_a = swapped(row_a, pairs_of(side, 0, 1, 0), parts, 0)
     row_b = swapped(row_b, pairs_of(side, 1, 1, 0), parts, 0)
-    borders = [row_a, row_b, column_a, column_b]
     student, lse_s = student_logits(student_tokens, head_s, classes)
-    stats = patch_stats(place, student, lse_s, logits, borders, corners, classes, parts)
+    stats = patch_stats(place, student, lse_s, logits, [row_a, row_b, column_a, column_b], classes, parts)
     stats = exchange(stats, "mp")
     divergence, totals = patch_divergence(stats, flags, tiles)
     totals = everywhere_sum(totals, tiles, parts)

time: 136 us -> 125 us (0.919)
  waiting for transfers between devices: 55.7 us -> 40.1 us
  local copies, waits for them, and re-layouts: 3.53 us -> 9.41 us
  Pallas kernels: 16.3 us -> 13.7 us
    ppermute x4 -> x1, waiting for transfers between devices: 34.8 us -> 4.05 us  [gathered_heads(): other = lax.ppermute(own, 'space', [(t, t ^ 1) for t in range(tiles)])]
    all_to_all x2, waiting for transfers between devices: 5.7 us -> 19.8 us  [exchange(): return lax.all_to_all(x, axis, split_axis=0, concat_axis=0, tiled=True)]
    all_to_all x0 -> x1, starting transfers between devices: none -> 7.9 us  [gathered_heads(): lax.all_to_all(second, 'space', split_axis=0, concat_axis=0, tiled=True,...]
    unnamed x10 -> x6, local copies, waits for them, and re-layouts: 0.04 us -> 5.12 us
    ppermute x4 -> x1, starting transfers between devices: 12.1 us -> 7.73 us  [gathered_heads(): other = lax.ppermute(own, 'space', [(t, t ^ 1) for t in range(tiles)])]
    all_to_all x1, starting transfers between devices: 15.7 us -> 11.6 us  [everywhere_sum(): lax.all_to_all(x, ('space', 'mp'), split_axis=0, concat_axis=0, tiled=Tru...]
    pallas_call x1 -> x2, Pallas kernels: 6.45 us -> 3.8 us  [the longest x1 2.54 us: teacher_logits(): pl.pallas_call(teacher_kernel, grid=(images // block,), in_specs=[pl.Bloc...]
    pad x0 -> x2, local copies, waits for them, and re-layouts: none -> 1.59 us  [padded(): return jnp.pad(head, ((0, 0), (0, LANES - head.shape[1])))]
  transfers between devices with their start and end apart: 11 -> 9, of which waited for: 5 -> 5; matrix products, arithmetic and copies ran while one was open for 2% -> 2% of each run, Pallas kernels for 3% -> 7%
where the time goes in v5:
time: 125 us; the launch traced here: 124 us
  starting transfers between devices  58.4 us (47%)
  waiting for transfers between devices  40.1 us (32%)
  Pallas kernels  13.7 us (11%)
  local copies, waits for them, and re-layouts  9.41 us (8%)
  other arithmetic  1.43 us (1%)
    all_to_all x2, waiting for transfers between devices, exchange(): return lax.all_to_all(x, axis, split_axis=0, concat_axis=0, tiled=True)  19.8 us
    all_to_all x2, starting transfers between devices, exchange(): return lax.all_to_all(x, axis, split_axis=0, concat_axis=0, tiled=True)  19.8 us
    all_to_all x1, starting transfers between devices, everywhere_sum(): lax.all_to_all(x, ('space', 'mp'), split_axis=0, concat_axis=0, tiled=Tru...  11.6 us
    ppermute x4, starting transfers between devices, swapped(): return lax.ppermute(block, ('space', 'mp'), route)  11.4 us
    all_to_all x1, waiting for transfers between devices, everywhere_sum(): lax.all_to_all(x, ('space', 'mp'), split_axis=0, concat_axis=0, tiled=Tru...  9.9 us
    all_to_all x1, starting transfers between devices, gathered_heads(): lax.all_to_all(second, 'space', split_axis=0, concat_axis=0, tiled=True,...  7.9 us
    ppermute x1, starting transfers between devices, gathered_heads(): other = lax.ppermute(own, 'space', [(t, t ^ 1) for t in range(tiles)])  7.73 us
    ppermute x4, waiting for transfers between devices, swapped(): return lax.ppermute(block, ('space', 'mp'), route)  6.41 us
  transfers between devices with their start and end apart: 9, of which 5 were waited for; matrix products, arithmetic and copies ran while one was open for 2% of the time, Pallas kernels for 7%

profile of v5, /device:TPU:6, one launch (start us, length us, event | category | flops | bytes accessed | tf_op | source)
XLA Modules:
  0.0 123.8 jit_solution(6294901214180018936)
XLA Ops:
  0.6 0.8 pad.9
  1.4 0.9 broadcast_in_dim.7
  2.4 15.6 %all-to-all-start = ((bf16[16,88,256]{2,1,0:T(8,128)(2,1)}), bf16[16,88,256]{2,1,0:T(8,128)(2,1)S(1)}, u32[]{:S(2)}, u32[]{:S(2)}) async-start(bf16[16,88,256]{2,1,0:T(8,128)(2,1)} %broadcast_in_dim.7), calls=%async_computation | async-start | bytes 1441792 | tf_op jit(solution)/shard_map/all_to_all | solution.py:20
  18.0 0.8 pad.8
  18.8 7.7 %collective-permute-start = (bf16[80,256]{1,0:T(8,128)(2,1)S(1)}, bf16[80,256]{1,0:T(8,128)(2,1)S(1)}, u32[]{:S(2)}, u32[]{:S(2)}) collective-permute-start(bf16[80,256]{1,0:T(8,128)(2,1)S(1)} %pad.8), channel_id=1, source_target_pairs={{0,4},{4,0},{8,12},{12,8},{16,20},{20,16},{24,28},{28,24},{32,36},... | collective-permute-start | bytes 122888 | tf_op jit(solution)/shard_map/ppermute | solution.py:30
  26.6 4.1 %collective-permute-done = bf16[80,256]{1,0:T(8,128)(2,1)S(1)} collective-permute-done((bf16[80,256]{1,0:T(8,128)(2,1)S(1)}, bf16[80,256]{1,0:T(8,128)(2,1)S(1)}, u32[]{:S(2)}, u32[]{:S(2)}) %collective-permute-start) | collective-permute-done | bytes 40992 | tf_op jit(solution)/shard_map/ppermute | solution.py:30
  30.6 0.8 broadcast_select_fusion.1
  31.4 14.0 %all-to-all-done = bf16[16,88,256]{2,1,0:T(8,128)(2,1)S(1)} async-done(((bf16[16,88,256]{2,1,0:T(8,128)(2,1)}), bf16[16,88,256]{2,1,0:T(8,128)(2,1)S(1)}, u32[]{:S(2)}, u32[]{:S(2)}) %all-to-all-start) | async-done | bytes 720928 | tf_op jit(solution)/shard_map/all_to_all | solution.py:20
  45.5 0.9 broadcast_in_dim.6
  46.4 7.9 %all-to-all-start.1 = ((bf16[8,160,256]{2,1,0:T(8,128)(2,1)}), bf16[8,160,256]{2,1,0:T(8,128)(2,1)S(1)}, u32[]{:S(2)}, u32[]{:S(2)}) async-start(bf16[8,160,256]{2,1,0:T(8,128)(2,1)} %broadcast_in_dim.6), calls=%async_computation.1 | async-start | bytes 1310720 | tf_op jit(solution)/shard_map/all_to_all | solution.py:35
  54.2 0.1 stack.19.place_ref.refs_0_
  54.3 0.0 copy-start
  54.3 2.6 %copy-done = bf16[8,1,16,16,1408]{4,3,2,1,0:T(8,128)(2,1)S(1)} copy-done((bf16[8,1,16,16,1408]{4,3,2,1,0:T(8,128)(2,1)S(1)}, bf16[8,1,16,16,1408]{4,3,2,1,0:T(8,128)(2,1)}, u32[]{:S(2)}) %copy-start) | copy-done | bytes 5767192
  57.0 2.5 %teacher_logits.1 = (f32[8,256,256]{2,1,0:T(8,128)S(1)}, f32[8,16,256]{2,1,0:T(8,128)S(1)}, f32[8,16,256]{2,1,0:T(8,128)S(1)}, f32[8,16,256]{2,1,0:T(8,128)S(1)}, f32[8,16,256]{2,1,0:T(8,128)S(1)}) custom-call(s32[5]{0:T(128)S(1)} %stack.19.place_ref.refs_0_, bf16[8,1,16,16,1408]{4,3,2,1,0:T(8,128)(2,1)S(1)} %copy-done, bf16[1408,256]{1,0:T(8,128)(2,1)S(1)} %bitcast.9), custom_call_target="tpu_custom_call" | custom-call | flops 1476395008 | bytes 8585216 | tf_op jit(solution)/shard_map/teacher_logits/pallas_call | solution.py:105
  59.5 5.6 %collective-permute-start.1 = (f32[8,16,256]{2,1,0:T(8,128)S(1)}, f32[8,16,256]{2,1,0:T(8,128)S(1)}, u32[]{:S(2)}, u32[]{:S(2)}) collective-permute-start(f32[8,16,256]{2,1,0:T(8,128)S(1)} %get-tuple-element.22), channel_id=1, source_target_pairs={{0,4},{4,0},{1,5},{5,1},{2,6},{6,2},{3,7},{7,3},{8,12},{12,8},{9,1... | collective-permute-start | bytes 393224 | tf_op jit(solution)/shard_map/ppermute | solution.py:45
  65.1 0.7 collective-permute-start.2
  65.8 6.4 %collective-permute-done.1.column_a.refs_6_ = f32[8,16,256]{2,1,0:T(8,128)S(1)} collective-permute-done((f32[8,16,256]{2,1,0:T(8,128)S(1)}, f32[8,16,256]{2,1,0:T(8,128)S(1)}, u32[]{:S(2)}, u32[]{:S(2)}) %collective-permute-start.1) | collective-permute-done | bytes 131104 | tf_op jit(solution)/shard_map/ppermute | solution.py:45
  72.2 0.0 collective-permute-done.2.column_b.refs_7_
  72.2 1.3 %row_sums.1 = (f32[8,16,256]{2,1,0:T(8,128)}, f32[8,16,256]{2,1,0:T(8,128)S(1)}) custom-call(s32[5]{0:T(128)S(1)} %stack.19.place_ref.refs_0_, f32[8,16,256]{2,1,0:T(8,128)S(1)} %get-tuple-element.20.row_a, f32[8,16,256]{2,1,0:T(8,128)S(1)} %get-tuple-element.21.row_b, f32[8,16,256]{2,1,0:T(8,128)S(1)} %collective-permute-done.1.column_a.refs_6_, ...), custom_call_target="tpu_custom_call" | custom-call | flops 327680 | bytes 786432 | tf_op jit(solution)/shard_map/row_sums/pallas_call | solution.py:143
  73.4 4.5 %collective-permute-start.3 = (f32[8,16,256]{2,1,0:T(8,128)}, f32[8,16,256]{2,1,0:T(8,128)S(1)}, u32[]{:S(2)}, u32[]{:S(2)}) collective-permute-start(f32[8,16,256]{2,1,0:T(8,128)} %get-tuple-element.24), channel_id=1, source_target_pairs={{0,16},{16,0},{1,17},{17,1},{2,18},{18,2},{3,19},{19,3},{4,20},{20... | collective-permute-start | bytes 393224 | tf_op jit(solution)/shard_map/ppermute | solution.py:45
  77.9 0.7 collective-permute-start.4
  78.6 0.0 all-to-all-done.1
  78.6 0.0 copy-start.1
  78.6 2.5 %copy-done.1 = bf16[8,1,16,16,1280]{4,3,2,1,0:T(8,128)(2,1)S(1)} copy-done((bf16[8,1,16,16,1280]{4,3,2,1,0:T(8,128)(2,1)S(1)}, bf16[8,1,16,16,1280]{4,3,2,1,0:T(8,128)(2,1)}, u32[]{:S(2)}) %copy-start.1) | copy-done | bytes 5242904
  81.1 0.0 copy-start.2
  81.1 4.4 %student_logits.1 = (f32[8,256,256]{2,1,0:T(8,128)S(1)}, f32[8,256]{1,0:T(8,128)S(1)}) custom-call(bf16[8,1,16,16,1280]{4,3,2,1,0:T(8,128)(2,1)S(1)} %copy-done.1, bf16[1280,256]{1,0:T(8,128)(2,1)S(1)} %bitcast.10), custom_call_target="tpu_custom_call" | custom-call | flops 1342177280 | bytes 7995392 | tf_op jit(solution)/shard_map/student_logits/pallas_call | solution.py:168
  85.5 0.0 collective-permute-done.3.refs_4_
  85.5 0.0 collective-permute-done.4.refs_5_
  85.5 4.8 %patch_stats.1 = f32[4,24,256]{2,1,0:T(8,128)} custom-call(s32[5]{0:T(128)S(1)} %stack.19.place_ref.refs_0_, f32[8,256,256]{2,1,0:T(8,128)S(1)} %get-tuple-element.16.refs_1_, f32[8,256]{1,0:T(8,128)S(1)} %get-tuple-element.17.refs_2_, f32[8,256,256]{2,1,0:T(8,128)S(1)} %get-tuple-element.19.refs_3_, f32[8,16,256]{2,1,0:T(8,128)S(1)} %collective-permute-done.3.refs_4_, ...), custom_call_target="tpu_custom_call" | custom-call | flops 15728640 | bytes 4194304 | tf_op jit(solution)/shard_map/patch_stats/pallas_call | solution.py:246
  90.3 4.1 %all-to-all-start.2 = ((f32[4,24,256]{2,1,0:T(8,128)}), f32[4,24,256]{2,1,0:T(8,128)S(1)}, u32[]{:S(2)}, u32[]{:S(2)}) async-start(f32[4,24,256]{2,1,0:T(8,128)} %patch_stats.1), calls=%async_computation.2 | async-start | bytes 196608 | tf_op jit(solution)/shard_map/all_to_all | solution.py:20
  94.4 0.0 copy-done.2
  94.4 0.1 reshape.18.refs_1_
  94.5 5.7 %all-to-all-done.2.refs_0_ = f32[4,24,256]{2,1,0:T(8,128)S(1)} async-done(((f32[4,24,256]{2,1,0:T(8,128)}), f32[4,24,256]{2,1,0:T(8,128)S(1)}, u32[]{:S(2)}, u32[]{:S(2)}) %all-to-all-start.2) | async-done | bytes 98336 | tf_op jit(solution)/shard_map/all_to_all | solution.py:20
  100.3 0.7 patch_divergence.1
  101.0 11.6 %all-to-all-start.3 = ((f32[16,1,128]{2,1,0:T(1,128)}), f32[16,1,128]{2,1,0:T(1,128)S(1)}, u32[]{:S(2)}, u32[]{:S(2)}) async-start(f32[16,1,128]{2,1,0:T(1,128)} %get-tuple-element.27), calls=%async_computation.3 | async-start | bytes 16384 | tf_op jit(solution)/shard_map/all_to_all | solution.py:311
  112.6 0.7 reshape.19
  113.3 9.9 %all-to-all-done.3 = f32[16,1,128]{2,1,0:T(1,128)S(1)} async-done(((f32[16,1,128]{2,1,0:T(1,128)}), f32[16,1,128]{2,1,0:T(1,128)S(1)}, u32[]{:S(2)}, u32[]{:S(2)}) %all-to-all-start.3) | async-done | bytes 8224 | tf_op jit(solution)/shard_map/all_to_all | solution.py:311
  123.2 0.6 maximum_divide_fusion
  (2 shorter events, 0.0 us)
Async XLA Ops:
  2.4 43.1 %all-to-all-start = ((bf16[16,88,256]{2,1,0:T(8,128)(2,1)}), bf16[16,88,256]{2,1,0:T(8,128)(2,1)S(1)}, u32[]{:S(2)}, u32[]{:S(2)}) async-start(bf16[16,88,256]{2,1,0:T(8,128)(2,1)} %broadcast_in_dim.7), calls=%async_computation | async-start | bytes 1441792 | tf_op jit(solution)/shard_map/all_to_all | solution.py:20
  18.8 11.8 %collective-permute-start = (bf16[80,256]{1,0:T(8,128)(2,1)S(1)}, bf16[80,256]{1,0:T(8,128)(2,1)S(1)}, u32[]{:S(2)}, u32[]{:S(2)}) collective-permute-start(bf16[80,256]{1,0:T(8,128)(2,1)S(1)} %pad.8), channel_id=1, source_target_pairs={{0,4},{4,0},{8,12},{12,8},{16,20},{20,16},{24,28},{28,24},{32,36},... | collective-permute-start | bytes 122888 | tf_op jit(solution)/shard_map/ppermute | solution.py:30
  46.4 32.2 %all-to-all-start.1 = ((bf16[8,160,256]{2,1,0:T(8,128)(2,1)}), bf16[8,160,256]{2,1,0:T(8,128)(2,1)S(1)}, u32[]{:S(2)}, u32[]{:S(2)}) async-start(bf16[8,160,256]{2,1,0:T(8,128)(2,1)} %broadcast_in_dim.6), calls=%async_computation.1 | async-start | bytes 1310720 | tf_op jit(solution)/shard_map/all_to_all | solution.py:35
  54.3 2.6 %copy-start = (bf16[8,1,16,16,1408]{4,3,2,1,0:T(8,128)(2,1)S(1)}, bf16[8,1,16,16,1408]{4,3,2,1,0:T(8,128)(2,1)}, u32[]{:S(2)}) copy-start(bf16[8,1,16,16,1408]{4,3,2,1,0:T(8,128)(2,1)} %tokens_ref.1) | copy-start | bytes 17301508
  59.5 12.7 %collective-permute-start.1 = (f32[8,16,256]{2,1,0:T(8,128)S(1)}, f32[8,16,256]{2,1,0:T(8,128)S(1)}, u32[]{:S(2)}, u32[]{:S(2)}) collective-permute-start(f32[8,16,256]{2,1,0:T(8,128)S(1)} %get-tuple-element.22), channel_id=1, source_target_pairs={{0,4},{4,0},{1,5},{5,1},{2,6},{6,2},{3,7},{7,3},{8,12},{12,8},{9,1... | collective-permute-start | bytes 393224 | tf_op jit(solution)/shard_map/ppermute | solution.py:45
  65.1 7.1 %collective-permute-start.2 = (f32[8,16,256]{2,1,0:T(8,128)S(1)}, f32[8,16,256]{2,1,0:T(8,128)S(1)}, u32[]{:S(2)}, u32[]{:S(2)}) collective-permute-start(f32[8,16,256]{2,1,0:T(8,128)S(1)} %get-tuple-element.23), channel_id=1, source_target_pairs={{4,8},{8,4},{5,9},{9,5},{6,10},{10,6},{7,11},{11,7},{20,24},{24,20... | collective-permute-start | bytes 393224 | tf_op jit(solution)/shard_map/ppermute | solution.py:45
  73.4 12.1 %collective-permute-start.3 = (f32[8,16,256]{2,1,0:T(8,128)}, f32[8,16,256]{2,1,0:T(8,128)S(1)}, u32[]{:S(2)}, u32[]{:S(2)}) collective-permute-start(f32[8,16,256]{2,1,0:T(8,128)} %get-tuple-element.24), channel_id=1, source_target_pairs={{0,16},{16,0},{1,17},{17,1},{2,18},{18,2},{3,19},{19,3},{4,20},{20... | collective-permute-start | bytes 393224 | tf_op jit(solution)/shard_map/ppermute | solution.py:45
  77.9 7.6 %collective-permute-start.4 = (f32[8,16,256]{2,1,0:T(8,128)S(1)}, f32[8,16,256]{2,1,0:T(8,128)S(1)}, u32[]{:S(2)}, u32[]{:S(2)}) collective-permute-start(f32[8,16,256]{2,1,0:T(8,128)S(1)} %get-tuple-element.25), channel_id=1, source_target_pairs={{16,32},{32,16},{17,33},{33,17},{18,34},{34,18},{19,35},{35,19},{2... | collective-permute-start | bytes 393224 | tf_op jit(solution)/shard_map/ppermute | solution.py:45
  78.6 2.5 %copy-start.1 = (bf16[8,1,16,16,1280]{4,3,2,1,0:T(8,128)(2,1)S(1)}, bf16[8,1,16,16,1280]{4,3,2,1,0:T(8,128)(2,1)}, u32[]{:S(2)}) copy-start(bf16[8,1,16,16,1280]{4,3,2,1,0:T(8,128)(2,1)} %refs_0_.1) | copy-start | bytes 15728644
  81.1 13.3 %copy-start.2 = (s32[8,1,16,16]{3,2,1,0:T(8,128)S(1)}, s32[8,1,16,16]{3,2,1,0:T(8,128)}, u32[]{:S(2)}) copy-start(s32[8,1,16,16]{3,2,1,0:T(8,128)} %param.9) | copy-start | bytes 24580
  90.3 9.9 %all-to-all-start.2 = ((f32[4,24,256]{2,1,0:T(8,128)}), f32[4,24,256]{2,1,0:T(8,128)S(1)}, u32[]{:S(2)}, u32[]{:S(2)}) async-start(f32[4,24,256]{2,1,0:T(8,128)} %patch_stats.1), calls=%async_computation.2 | async-start | bytes 196608 | tf_op jit(solution)/shard_map/all_to_all | solution.py:20
  101.0 22.2 %all-to-all-start.3 = ((f32[16,1,128]{2,1,0:T(1,128)}), f32[16,1,128]{2,1,0:T(1,128)S(1)}, u32[]{:S(2)}, u32[]{:S(2)}) async-start(f32[16,1,128]{2,1,0:T(1,128)} %get-tuple-element.27), calls=%async_computation.3 | async-start | bytes 16384 | tf_op jit(solution)/shard_map/all_to_all | solution.py:311

commit v6 on v5

--- a/solution.py
+++ b/solution.py
@@ -25,14 +25,20 @@
 
 
 def gathered_heads(teacher_head, student_head, tiles):
-    first = exchange(copies(padded(teacher_head), tiles), "space")
-    own = padded(student_head)
+    cut = teacher_head.shape[0]
+    own = padded(jnp.concatenate([teacher_head, student_head]))
     other = lax.ppermute(own, "space", [(t, t ^ 1) for t in range(tiles)])
-    even = lax.axis_index("space") % 2 == 0
-    pair = jnp.concatenate([jnp.where(even, own, other), jnp.where(even, other, own)])
-    second, first = lax.optimization_barrier((copies(pair, tiles // 2), first))
+    is_even = lax.axis_index("space") % 2 == 0
+    even, odd = jnp.where(is_even, own, other), jnp.where(is_even, other, own)
     groups = [list(range(z, tiles, 2)) for z in range(2)]
-    second = lax.all_to_all(second, "space", split_axis=0, concat_axis=0, tiled=True, axis_index_groups=groups)
+
+    def along_y(pair):
+        return lax.all_to_all(pair, "space", split_axis=0, concat_axis=0, tiled=True, axis_index_groups=groups)
+
+    first = along_y(copies(jnp.concatenate([even[:cut], odd[:cut]]), tiles // 2))
+    second = copies(jnp.concatenate([even[cut:], odd[cut:]]), tiles // 2)
+    second, first = lax.optimization_barrier((second, first))
+    second = along_y(second)
     return first.reshape(-1, LANES), second.reshape(-1, LANES)
 
 
@@ -152,24 +158,29 @@
 
 
 def student_kernel(edge, classes, tokens_ref, head_ref, logits_ref, lse_ref):
-    tokens = tokens_ref[pl.program_id(0), 0].reshape(edge * edge, tokens_ref.shape[-1])
+    block, patches, _ = logits_ref.shape
+    start = pl.program_id(0) * block
+    tokens = tokens_ref[pl.ds(start, block), 0].reshape(block * patches, tokens_ref.shape[-1])
     logits = jnp.dot(tokens, head_ref[...], preferred_element_type=F32)
-    logits_ref[0] = logits
-    logits = logits[:, :classes]
-    top = jnp.max(logits, axis=-1, keepdims=True)
-    total = jnp.sum(jnp.exp(logits - top), axis=-1, keepdims=True)
-    top, total = in_lanes([top, total])
-    lse_ref[pl.ds(pl.program_id(0), 1), :] = top + jnp.log(total)
+    for i in range(block):
+        image = logits[i * patches : (i + 1) * patches]
+        logits_ref[i] = image
+        image = image[:, :classes]
+        top = jnp.max(image, axis=-1, keepdims=True)
+        total = jnp.sum(jnp.exp(image - top), axis=-1, keepdims=True)
+        top, total = in_lanes([top, total])
+        lse_ref[pl.ds(start + i, 1), :] = top + jnp.log(total)
 
 
 def student_logits(tokens, head, classes):
     images, _, edge, _, width = tokens.shape
     patches = edge * edge
+    block = math.gcd(images, BLOCK)
     return pl.pallas_call(
         lambda *refs: student_kernel(edge, classes, *refs),
-        grid=(images,),
-        in_specs=[pl.BlockSpec(memory_space=pltpu.VMEM), whole_spec(head.shape)],
-        out_specs=[image_spec(patches), whole_spec((images, patches))],
+        grid=(images // block,),
+        in_specs=[pl.BlockSpec(memory_space=pltpu.VMEM), pl.BlockSpec(memory_space=pltpu.VMEM)],
+        out_specs=[pl.BlockSpec((block, patches, LANES), lambda i: (i, 0, 0)), whole_spec((images, patches))],
         out_shape=[
             jax.ShapeDtypeStruct((images, patches, LANES), F32),
             jax.ShapeDtypeStruct((images, patches), F32),

time: 125 us -> 123 us (0.984)
  waiting for transfers between devices: 40.1 us -> 46.2 us
  starting transfers between devices: 58.4 us -> 53.6 us
  Pallas kernels: 13.7 us -> 11.7 us
  local copies, waits for them, and re-layouts: 9.41 us -> 7.84 us
    all_to_all x1 -> x2, waiting for transfers between devices: 0.01 us -> 19.9 us  [along_y(): lax.all_to_all(pair, 'space', split_axis=0, concat_axis=0, tiled=True, ax...]
    all_to_all x2 -> x1, waiting for transfers between devices: 19.8 us -> 5.74 us  [exchange(): return lax.all_to_all(x, axis, split_axis=0, concat_axis=0, tiled=True)]
    all_to_all x2 -> x1, starting transfers between devices: 19.8 us -> 6.44 us  [exchange(): return lax.all_to_all(x, axis, split_axis=0, concat_axis=0, tiled=True)]
    ppermute x1, starting transfers between devices: 7.73 us -> 10.9 us  [gathered_heads(): other = lax.ppermute(own, 'space', [(t, t ^ 1) for t in range(tiles)])]
    all_to_all x1 -> x2, starting transfers between devices: 7.9 us -> 10.6 us  [along_y(): lax.all_to_all(pair, 'space', split_axis=0, concat_axis=0, tiled=True, ax...]
    pallas_call x1, Pallas kernels: 4.43 us -> 2.39 us  [student_logits(): pl.pallas_call(lambda *refs: student_kernel(edge, classes, *refs), grid=(...]
    ppermute x4, starting transfers between devices: 11.4 us -> 13.2 us  [swapped(): return lax.ppermute(block, ('space', 'mp'), route)]
    pad x2 -> x0, local copies, waits for them, and re-layouts: 1.59 us -> none  [padded(): return jnp.pad(head, ((0, 0), (0, LANES - head.shape[1])))]
  transfers between devices with their start and end apart: 9 -> 9, of which waited for: 5 -> 5; matrix products, arithmetic and copies ran while one was open for 2% -> 1% of each run, Pallas kernels for 7% -> 5%
where the time goes in v6:
time: 123 us; the launch traced here: 122 us
  starting transfers between devices  53.6 us (44%)
  waiting for transfers between devices  46.2 us (38%)
  Pallas kernels  11.7 us (10%)
  local copies, waits for them, and re-layouts  7.84 us (6%)
  other arithmetic  2.33 us (2%)
    all_to_all x2, waiting for transfers between devices, along_y(): lax.all_to_all(pair, 'space', split_axis=0, concat_axis=0, tiled=True, ax...  19.9 us
    ppermute x4, starting transfers between devices, swapped(): return lax.ppermute(block, ('space', 'mp'), route)  13.2 us
    all_to_all x1, starting transfers between devices, everywhere_sum(): lax.all_to_all(x, ('space', 'mp'), split_axis=0, concat_axis=0, tiled=Tru...  12.4 us
    ppermute x1, starting transfers between devices, gathered_heads(): other = lax.ppermute(own, 'space', [(t, t ^ 1) for t in range(tiles)])  10.9 us
    all_to_all x2, starting transfers between devices, along_y(): lax.all_to_all(pair, 'space', split_axis=0, concat_axis=0, tiled=True, ax...  10.6 us
    all_to_all x1, waiting for transfers between devices, everywhere_sum(): lax.all_to_all(x, ('space', 'mp'), split_axis=0, concat_axis=0, tiled=Tru...  9.9 us
    ppermute x4, waiting for transfers between devices, swapped(): return lax.ppermute(block, ('space', 'mp'), route)  6.87 us
    all_to_all x1, starting transfers between devices, exchange(): return lax.all_to_all(x, axis, split_axis=0, concat_axis=0, tiled=True)  6.44 us
  transfers between devices with their start and end apart: 9, of which 5 were waited for; matrix products, arithmetic and copies ran while one was open for 1% of the time, Pallas kernels for 5%

profile of v6, /device:TPU:6, one launch (start us, length us, event | category | flops | bytes accessed | tf_op | source)
XLA Modules:
  0.0 122.5 jit_solution(7704860969515035565)
XLA Ops:
  0.6 0.8 fusion.2
  1.5 10.9 %collective-permute-start = (bf16[168,256]{1,0:T(8,128)(2,1)S(1)}, bf16[168,256]{1,0:T(8,128)(2,1)S(1)}, u32[]{:S(2)}, u32[]{:S(2)}) collective-permute-start(bf16[168,256]{1,0:T(8,128)(2,1)S(1)} %fusion.2), channel_id=1, source_target_pairs={{0,4},{4,0},{8,12},{12,8},{16,20},{20,16},{24,28},{28,24},{32,36},... | collective-permute-start | bytes 258056 | tf_op jit(solution)/shard_map/ppermute | solution.py:30
  12.4 3.7 %collective-permute-done = bf16[168,256]{1,0:T(8,128)(2,1)S(1)} collective-permute-done((bf16[168,256]{1,0:T(8,128)(2,1)S(1)}, bf16[168,256]{1,0:T(8,128)(2,1)S(1)}, u32[]{:S(2)}, u32[]{:S(2)}) %collective-permute-start) | collective-permute-done | bytes 86048 | tf_op jit(solution)/shard_map/ppermute | solution.py:30
  16.1 0.9 broadcast_select_fusion.1
  17.0 0.9 broadcast_in_dim.7
  18.0 7.1 %all-to-all-start = ((bf16[8,176,256]{2,1,0:T(8,128)(2,1)}), bf16[8,176,256]{2,1,0:T(8,128)(2,1)S(1)}, u32[]{:S(2)}, u32[]{:S(2)}) async-start(bf16[8,176,256]{2,1,0:T(8,128)(2,1)} %broadcast_in_dim.7), calls=%async_computation | async-start | bytes 1441792 | tf_op jit(solution)/shard_map/all_to_all | solution.py:36
  25.1 19.9 %all-to-all-done = bf16[8,176,256]{2,1,0:T(8,128)(2,1)S(1)} async-done(((bf16[8,176,256]{2,1,0:T(8,128)(2,1)}), bf16[8,176,256]{2,1,0:T(8,128)(2,1)S(1)}, u32[]{:S(2)}, u32[]{:S(2)}) %all-to-all-start) | async-done | bytes 720928 | tf_op jit(solution)/shard_map/all_to_all | solution.py:36
  45.0 0.9 broadcast_in_dim.6
  45.9 3.5 %all-to-all-start.1 = ((bf16[8,160,256]{2,1,0:T(8,128)(2,1)}), bf16[8,160,256]{2,1,0:T(8,128)(2,1)S(1)}, u32[]{:S(2)}, u32[]{:S(2)}) async-start(bf16[8,160,256]{2,1,0:T(8,128)(2,1)} %broadcast_in_dim.6), calls=%async_computation.1 | async-start | bytes 1310720 | tf_op jit(solution)/shard_map/all_to_all | solution.py:36
  49.5 0.1 stack.19.place_ref.refs_0_
  49.6 0.0 copy-start
  49.6 2.6 %copy-done = bf16[8,1,16,16,1408]{4,3,2,1,0:T(8,128)(2,1)S(1)} copy-done((bf16[8,1,16,16,1408]{4,3,2,1,0:T(8,128)(2,1)S(1)}, bf16[8,1,16,16,1408]{4,3,2,1,0:T(8,128)(2,1)}, u32[]{:S(2)}) %copy-start) | copy-done | bytes 5767192
  52.2 2.5 %teacher_logits.1 = (f32[8,256,256]{2,1,0:T(8,128)S(1)}, f32[8,16,256]{2,1,0:T(8,128)S(1)}, f32[8,16,256]{2,1,0:T(8,128)S(1)}, f32[8,16,256]{2,1,0:T(8,128)S(1)}, f32[8,16,256]{2,1,0:T(8,128)S(1)}) custom-call(s32[5]{0:T(128)S(1)} %stack.19.place_ref.refs_0_, bf16[8,1,16,16,1408]{4,3,2,1,0:T(8,128)(2,1)S(1)} %copy-done, bf16[1408,256]{1,0:T(8,128)(2,1)S(1)} %bitcast.9), custom_call_target="tpu_custom_call" | custom-call | flops 1476395008 | bytes 8585216 | tf_op jit(solution)/shard_map/teacher_logits/pallas_call | solution.py:111
  54.8 7.3 %collective-permute-start.1 = (f32[8,16,256]{2,1,0:T(8,128)S(1)}, f32[8,16,256]{2,1,0:T(8,128)S(1)}, u32[]{:S(2)}, u32[]{:S(2)}) collective-permute-start(f32[8,16,256]{2,1,0:T(8,128)S(1)} %get-tuple-element.22), channel_id=1, source_target_pairs={{0,4},{4,0},{1,5},{5,1},{2,6},{6,2},{3,7},{7,3},{8,12},{12,8},{9,1... | collective-permute-start | bytes 393224 | tf_op jit(solution)/shard_map/ppermute | solution.py:51
  62.1 0.7 collective-permute-start.2
  62.7 6.9 %collective-permute-done.1.column_a.refs_6_ = f32[8,16,256]{2,1,0:T(8,128)S(1)} collective-permute-done((f32[8,16,256]{2,1,0:T(8,128)S(1)}, f32[8,16,256]{2,1,0:T(8,128)S(1)}, u32[]{:S(2)}, u32[]{:S(2)}) %collective-permute-start.1) | collective-permute-done | bytes 131104 | tf_op jit(solution)/shard_map/ppermute | solution.py:51
  69.6 0.0 collective-permute-done.2.column_b.refs_7_
  69.6 1.3 %row_sums.1 = (f32[8,16,256]{2,1,0:T(8,128)}, f32[8,16,256]{2,1,0:T(8,128)S(1)}) custom-call(s32[5]{0:T(128)S(1)} %stack.19.place_ref.refs_0_, f32[8,16,256]{2,1,0:T(8,128)S(1)} %get-tuple-element.20.row_a, f32[8,16,256]{2,1,0:T(8,128)S(1)} %get-tuple-element.21.row_b, f32[8,16,256]{2,1,0:T(8,128)S(1)} %collective-permute-done.1.column_a.refs_6_, ...), custom_call_target="tpu_custom_call" | custom-call | flops 327680 | bytes 786432 | tf_op jit(solution)/shard_map/row_sums/pallas_call | solution.py:149
  70.9 4.6 %collective-permute-start.3 = (f32[8,16,256]{2,1,0:T(8,128)}, f32[8,16,256]{2,1,0:T(8,128)S(1)}, u32[]{:S(2)}, u32[]{:S(2)}) collective-permute-start(f32[8,16,256]{2,1,0:T(8,128)} %get-tuple-element.24), channel_id=1, source_target_pairs={{0,16},{16,0},{1,17},{17,1},{2,18},{18,2},{3,19},{19,3},{4,20},{20... | collective-permute-start | bytes 393224 | tf_op jit(solution)/shard_map/ppermute | solution.py:51
  75.5 0.7 collective-permute-start.4
  76.2 0.0 all-to-all-done.1
  76.2 0.0 copy-start.1
  76.2 2.5 %copy-done.1 = bf16[8,1,16,16,1280]{4,3,2,1,0:T(8,128)(2,1)S(1)} copy-done((bf16[8,1,16,16,1280]{4,3,2,1,0:T(8,128)(2,1)S(1)}, bf16[8,1,16,16,1280]{4,3,2,1,0:T(8,128)(2,1)}, u32[]{:S(2)}) %copy-start.1) | copy-done | bytes 5242904
  78.7 0.0 copy-start.2
  78.7 2.4 %student_logits.1 = (f32[8,256,256]{2,1,0:T(8,128)S(1)}, f32[8,256]{1,0:T(8,128)S(1)}) custom-call(bf16[8,1,16,16,1280]{4,3,2,1,0:T(8,128)(2,1)S(1)} %copy-done.1, bf16[1280,256]{1,0:T(8,128)(2,1)S(1)} %bitcast.10), custom_call_target="tpu_custom_call" | custom-call | flops 1342177280 | bytes 7995392 | tf_op jit(solution)/shard_map/student_logits/pallas_call | solution.py:179
  81.1 0.0 collective-permute-done.3.refs_4_
  81.1 0.0 collective-permute-done.4.refs_5_
  81.1 4.8 %patch_stats.1 = f32[4,24,256]{2,1,0:T(8,128)} custom-call(s32[5]{0:T(128)S(1)} %stack.19.place_ref.refs_0_, f32[8,256,256]{2,1,0:T(8,128)S(1)} %get-tuple-element.16.refs_1_, f32[8,256]{1,0:T(8,128)S(1)} %get-tuple-element.17.refs_2_, f32[8,256,256]{2,1,0:T(8,128)S(1)} %get-tuple-element.19.refs_3_, f32[8,16,256]{2,1,0:T(8,128)S(1)} %collective-permute-done.3.refs_4_, ...), custom_call_target="tpu_custom_call" | custom-call | flops 15728640 | bytes 4194304 | tf_op jit(solution)/shard_map/patch_stats/pallas_call | solution.py:257
  85.9 6.4 %all-to-all-start.2 = ((f32[4,24,256]{2,1,0:T(8,128)}), f32[4,24,256]{2,1,0:T(8,128)S(1)}, u32[]{:S(2)}, u32[]{:S(2)}) async-start(f32[4,24,256]{2,1,0:T(8,128)} %patch_stats.1), calls=%async_computation.2 | async-start | bytes 196608 | tf_op jit(solution)/shard_map/all_to_all | solution.py:20
  92.3 0.0 copy-done.2
  92.3 0.1 reshape.18.refs_1_
  92.4 5.7 %all-to-all-done.2.refs_0_ = f32[4,24,256]{2,1,0:T(8,128)S(1)} async-done(((f32[4,24,256]{2,1,0:T(8,128)}), f32[4,24,256]{2,1,0:T(8,128)S(1)}, u32[]{:S(2)}, u32[]{:S(2)}) %all-to-all-start.2) | async-done | bytes 98336 | tf_op jit(solution)/shard_map/all_to_all | solution.py:20
  98.1 0.7 patch_divergence.1
  98.9 12.4 %all-to-all-start.3 = ((f32[16,1,128]{2,1,0:T(1,128)}), f32[16,1,128]{2,1,0:T(1,128)S(1)}, u32[]{:S(2)}, u32[]{:S(2)}) async-start(f32[16,1,128]{2,1,0:T(1,128)} %get-tuple-element.27), calls=%async_computation.3 | async-start | bytes 16384 | tf_op jit(solution)/shard_map/all_to_all | solution.py:322
  111.2 0.7 reshape.19
  111.9 9.9 %all-to-all-done.3 = f32[16,1,128]{2,1,0:T(1,128)S(1)} async-done(((f32[16,1,128]{2,1,0:T(1,128)}), f32[16,1,128]{2,1,0:T(1,128)S(1)}, u32[]{:S(2)}, u32[]{:S(2)}) %all-to-all-start.3) | async-done | bytes 8224 | tf_op jit(solution)/shard_map/all_to_all | solution.py:322
  121.9 0.6 maximum_divide_fusion
  (7 shorter events, 0.1 us)
Async XLA Ops:
  1.5 14.7 %collective-permute-start = (bf16[168,256]{1,0:T(8,128)(2,1)S(1)}, bf16[168,256]{1,0:T(8,128)(2,1)S(1)}, u32[]{:S(2)}, u32[]{:S(2)}) collective-permute-start(bf16[168,256]{1,0:T(8,128)(2,1)S(1)} %fusion.2), channel_id=1, source_target_pairs={{0,4},{4,0},{8,12},{12,8},{16,20},{20,16},{24,28},{28,24},{32,36},... | collective-permute-start | bytes 258056 | tf_op jit(solution)/shard_map/ppermute | solution.py:30
  18.0 27.1 %all-to-all-start = ((bf16[8,176,256]{2,1,0:T(8,128)(2,1)}), bf16[8,176,256]{2,1,0:T(8,128)(2,1)S(1)}, u32[]{:S(2)}, u32[]{:S(2)}) async-start(bf16[8,176,256]{2,1,0:T(8,128)(2,1)} %broadcast_in_dim.7), calls=%async_computation | async-start | bytes 1441792 | tf_op jit(solution)/shard_map/all_to_all | solution.py:36
  45.9 30.2 %all-to-all-start.1 = ((bf16[8,160,256]{2,1,0:T(8,128)(2,1)}), bf16[8,160,256]{2,1,0:T(8,128)(2,1)S(1)}, u32[]{:S(2)}, u32[]{:S(2)}) async-start(bf16[8,160,256]{2,1,0:T(8,128)(2,1)} %broadcast_in_dim.6), calls=%async_computation.1 | async-start | bytes 1310720 | tf_op jit(solution)/shard_map/all_to_all | solution.py:36
  49.6 2.6 %copy-start = (bf16[8,1,16,16,1408]{4,3,2,1,0:T(8,128)(2,1)S(1)}, bf16[8,1,16,16,1408]{4,3,2,1,0:T(8,128)(2,1)}, u32[]{:S(2)}) copy-start(bf16[8,1,16,16,1408]{4,3,2,1,0:T(8,128)(2,1)} %tokens_ref.1) | copy-start | bytes 17301508
  54.8 14.8 %collective-permute-start.1 = (f32[8,16,256]{2,1,0:T(8,128)S(1)}, f32[8,16,256]{2,1,0:T(8,128)S(1)}, u32[]{:S(2)}, u32[]{:S(2)}) collective-permute-start(f32[8,16,256]{2,1,0:T(8,128)S(1)} %get-tuple-element.22), channel_id=1, source_target_pairs={{0,4},{4,0},{1,5},{5,1},{2,6},{6,2},{3,7},{7,3},{8,12},{12,8},{9,1... | collective-permute-start | bytes 393224 | tf_op jit(solution)/shard_map/ppermute | solution.py:51
  62.1 7.5 %collective-permute-start.2 = (f32[8,16,256]{2,1,0:T(8,128)S(1)}, f32[8,16,256]{2,1,0:T(8,128)S(1)}, u32[]{:S(2)}, u32[]{:S(2)}) collective-permute-start(f32[8,16,256]{2,1,0:T(8,128)S(1)} %get-tuple-element.23), channel_id=1, source_target_pairs={{4,8},{8,4},{5,9},{9,5},{6,10},{10,6},{7,11},{11,7},{20,24},{24,20... | collective-permute-start | bytes 393224 | tf_op jit(solution)/shard_map/ppermute | solution.py:51
  70.9 10.2 %collective-permute-start.3 = (f32[8,16,256]{2,1,0:T(8,128)}, f32[8,16,256]{2,1,0:T(8,128)S(1)}, u32[]{:S(2)}, u32[]{:S(2)}) collective-permute-start(f32[8,16,256]{2,1,0:T(8,128)} %get-tuple-element.24), channel_id=1, source_target_pairs={{0,16},{16,0},{1,17},{17,1},{2,18},{18,2},{3,19},{19,3},{4,20},{20... | collective-permute-start | bytes 393224 | tf_op jit(solution)/shard_map/ppermute | solution.py:51
  75.5 5.6 %collective-permute-start.4 = (f32[8,16,256]{2,1,0:T(8,128)S(1)}, f32[8,16,256]{2,1,0:T(8,128)S(1)}, u32[]{:S(2)}, u32[]{:S(2)}) collective-permute-start(f32[8,16,256]{2,1,0:T(8,128)S(1)} %get-tuple-element.25), channel_id=1, source_target_pairs={{16,32},{32,16},{17,33},{33,17},{18,34},{34,18},{19,35},{35,19},{2... | collective-permute-start | bytes 393224 | tf_op jit(solution)/shard_map/ppermute | solution.py:51
  76.2 2.5 %copy-start.1 = (bf16[8,1,16,16,1280]{4,3,2,1,0:T(8,128)(2,1)S(1)}, bf16[8,1,16,16,1280]{4,3,2,1,0:T(8,128)(2,1)}, u32[]{:S(2)}) copy-start(bf16[8,1,16,16,1280]{4,3,2,1,0:T(8,128)(2,1)} %refs_0_.1) | copy-start | bytes 15728644
  78.7 13.6 %copy-start.2 = (s32[8,1,16,16]{3,2,1,0:T(8,128)S(1)}, s32[8,1,16,16]{3,2,1,0:T(8,128)}, u32[]{:S(2)}) copy-start(s32[8,1,16,16]{3,2,1,0:T(8,128)} %param.9) | copy-start | bytes 24580
  85.9 12.3 %all-to-all-start.2 = ((f32[4,24,256]{2,1,0:T(8,128)}), f32[4,24,256]{2,1,0:T(8,128)S(1)}, u32[]{:S(2)}, u32[]{:S(2)}) async-start(f32[4,24,256]{2,1,0:T(8,128)} %patch_stats.1), calls=%async_computation.2 | async-start | bytes 196608 | tf_op jit(solution)/shard_map/all_to_all | solution.py:20
  98.9 23.0 %all-to-all-start.3 = ((f32[16,1,128]{2,1,0:T(1,128)}), f32[16,1,128]{2,1,0:T(1,128)S(1)}, u32[]{:S(2)}, u32[]{:S(2)}) async-start(f32[16,1,128]{2,1,0:T(1,128)} %get-tuple-element.27), calls=%async_computation.3 | async-start | bytes 16384 | tf_op jit(solution)/shard_map/all_to_all | solution.py:322

commit v7 on v6

--- a/solution.py
+++ b/solution.py
@@ -72,51 +72,34 @@
     return [rows[k : k + 1] for k in range(len(columns))]
 
 
-def whole_spec(shape):
-    return pl.BlockSpec(shape, lambda i: (0,) * len(shape))
-
-
-def image_spec(rows):
-    return pl.BlockSpec((1, rows, LANES), lambda i: (i, 0, 0))
-
-
-def teacher_kernel(place_ref, tokens_ref, head_ref, logits_ref, row_a, row_b, column_a, column_b):
+def teacher_kernel(block, place_ref, tokens_ref, head_ref, logits_ref, row_a, row_b, column_a, column_b):
     edge, width = tokens_ref.shape[2], tokens_ref.shape[-1]
-    block, patches, _ = logits_ref.shape
-    here = pl.ds(pl.program_id(0) * block, block)
-    tokens = tokens_ref[here, 0].reshape(block * patches, width)
-    logits = jnp.dot(tokens, head_ref[...], preferred_element_type=F32)
+    images, patches, _ = logits_ref.shape
     row_even, column_even = place_ref[3] == 1, place_ref[4] == 1
-    for i in range(block):
-        image = logits[i * patches : (i + 1) * patches]
-        logits_ref[i] = image
-        cube = image.reshape(edge, edge, LANES)
-        first, last = cube[0], cube[edge - 1]
-        row_a[i] = jnp.where(row_even, last, first)
-        row_b[i] = jnp.where(row_even, first, last)
-        left, right = cube[:, 0, :], cube[:, edge - 1, :]
-        column_a[i] = jnp.where(column_even, right, left)
-        column_b[i] = jnp.where(column_even, left, right)
+    for start in range(0, images, block):
+        tokens = tokens_ref[start : start + block, 0].reshape(block * patches, width)
+        logits = jnp.dot(tokens, head_ref[...], preferred_element_type=F32)
+        for i in range(block):
+            image = logits[i * patches : (i + 1) * patches]
+            logits_ref[start + i] = image
+            cube = image.reshape(edge, edge, LANES)
+            first, last = cube[0], cube[edge - 1]
+            row_a[start + i] = jnp.where(row_even, last, first)
+            row_b[start + i] = jnp.where(row_even, first, last)
+            left, right = cube[:, 0, :], cube[:, edge - 1, :]
+            column_a[start + i] = jnp.where(column_even, right, left)
+            column_b[start + i] = jnp.where(column_even, left, right)
 
 
 def teacher_logits(place, tokens, head):
     images, _, edge, _, width = tokens.shape
     patches = edge * edge
-    block = math.gcd(images, BLOCK)
     border = jax.ShapeDtypeStruct((images, edge, LANES), F32)
-
-    def spec(rows):
-        return pl.BlockSpec((block, rows, LANES), lambda i: (i, 0, 0))
-
-    return pl.pallas_call(
-        teacher_kernel,
-        grid=(images // block,),
-        in_specs=[
-            pl.BlockSpec(memory_space=pltpu.SMEM),
-            pl.BlockSpec(memory_space=pltpu.VMEM),
-            pl.BlockSpec(memory_space=pltpu.VMEM),
-        ],
-        out_specs=[spec(patches)] + [spec(edge)] * 4,
+    whole = pl.BlockSpec(memory_space=pltpu.VMEM)
+    return pl.pallas_call(
+        lambda *refs: teacher_kernel(math.gcd(images, BLOCK), *refs),
+        in_specs=[pl.BlockSpec(memory_space=pltpu.SMEM), whole, whole],
+        out_specs=[whole] * 5,
         out_shape=[jax.ShapeDtypeStruct((images, patches, LANES), F32)] + [border] * 4,
         compiler_params=pltpu.CompilerParams(vmem_limit_bytes=16 * 2**20),
         cost_estimate=pl.CostEstimate(
@@ -157,30 +140,29 @@
     )(place, row_a, row_b, column_a, column_b)
 
 
-def student_kernel(edge, classes, tokens_ref, head_ref, logits_ref, lse_ref):
-    block, patches, _ = logits_ref.shape
-    start = pl.program_id(0) * block
-    tokens = tokens_ref[pl.ds(start, block), 0].reshape(block * patches, tokens_ref.shape[-1])
-    logits = jnp.dot(tokens, head_ref[...], preferred_element_type=F32)
-    for i in range(block):
-        image = logits[i * patches : (i + 1) * patches]
-        logits_ref[i] = image
-        image = image[:, :classes]
-        top = jnp.max(image, axis=-1, keepdims=True)
-        total = jnp.sum(jnp.exp(image - top), axis=-1, keepdims=True)
-        top, total = in_lanes([top, total])
-        lse_ref[pl.ds(start + i, 1), :] = top + jnp.log(total)
+def student_kernel(block, classes, tokens_ref, head_ref, logits_ref, lse_ref):
+    images, patches, _ = logits_ref.shape
+    for start in range(0, images, block):
+        tokens = tokens_ref[start : start + block, 0].reshape(block * patches, tokens_ref.shape[-1])
+        logits = jnp.dot(tokens, head_ref[...], preferred_element_type=F32)
+        for i in range(block):
+            image = logits[i * patches : (i + 1) * patches]
+            logits_ref[start + i] = image
+            image = image[:, :classes]
+            top = jnp.max(image, axis=-1, keepdims=True)
+            total = jnp.sum(jnp.exp(image - top), axis=-1, keepdims=True)
+            top, total = in_lanes([top, total])
+            lse_ref[start + i : start + i + 1, :] = top + jnp.log(total)
 
 
 def student_logits(tokens, head, classes):
     images, _, edge, _, width = tokens.shape
     patches = edge * edge
-    block = math.gcd(images, BLOCK)
-    return pl.pallas_call(
-        lambda *refs: student_kernel(edge, classes, *refs),
-        grid=(images // block,),
-        in_specs=[pl.BlockSpec(memory_space=pltpu.VMEM), pl.BlockSpec(memory_space=pltpu.VMEM)],
-        out_specs=[pl.BlockSpec((block, patches, LANES), lambda i: (i, 0, 0)), whole_spec((images, patches))],
+    whole = pl.BlockSpec(memory_space=pltpu.VMEM)
+    return pl.pallas_call(
+        lambda *refs: student_kernel(math.gcd(images, BLOCK), classes, *refs),
+        in_specs=[whole, whole],
+        out_specs=[whole, whole],
         out_shape=[
             jax.ShapeDtypeStruct((images, patches, LANES), F32),
             jax.ShapeDtypeStruct((images, patches), F32),
@@ -215,16 +197,16 @@
     shape = (edge, edge, LANES)
     row_even, column_even = place_ref[3] == 1, place_ref[4] == 1
 
-    flat = logits_ref[0]
+    flat = logits_ref[image]
     cube = flat.reshape(shape)
     x = lax.broadcasted_iota(jnp.int32, shape, 1)
-    to_left = jnp.broadcast_to(jnp.where(column_even, column_b[0], column_a[0])[:, None, :], shape)
-    to_right = jnp.broadcast_to(jnp.where(column_even, column_a[0], column_b[0])[:, None, :], shape)
+    to_left = jnp.broadcast_to(jnp.where(column_even, column_b[image], column_a[image])[:, None, :], shape)
+    to_right = jnp.broadcast_to(jnp.where(column_even, column_a[image], column_b[image])[:, None, :], shape)
     before = jnp.where(x == 0, to_left, pltpu.roll(flat, 1, 0).reshape(shape))
     after = jnp.where(x == edge - 1, to_right, pltpu.roll(flat, patches - 1, 0).reshape(shape))
     rows = cube + before + after
-    up = jnp.where(row_even, row_b[0], row_a[0])
-    down = jnp.where(row_even, row_a[0], row_b[0])
+    up = jnp.where(row_even, row_b[image], row_a[image])
+    down = jnp.where(row_even, row_a[image], row_b[image])
     above = jnp.concatenate([up[None], rows[:-1]], axis=0)
     below = jnp.concatenate([rows[1:], down[None]], axis=0)
     total = rows + above + below
@@ -238,7 +220,7 @@
 
     share = 1.0 / (line(place_y) * line(place_x))
     smoothed = (total * share).reshape(patches, LANES)[:, :classes]
-    student = student_ref[0][:, :classes]
+    student = student_ref[image][:, :classes]
 
     top_t = jnp.max(smoothed, axis=-1, keepdims=True)
     expo_t = jnp.exp(smoothed - top_t)
@@ -254,17 +236,12 @@
 def patch_stats(place, student, lse_s, logits, borders, classes, parts):
     images, patches, _ = logits.shape
     edge = borders[0].shape[1]
+    whole = pl.BlockSpec(memory_space=pltpu.VMEM)
     return pl.pallas_call(
         lambda *refs: stats_kernel(edge, classes, parts, images, *refs),
         grid=(images,),
-        in_specs=[
-            pl.BlockSpec(memory_space=pltpu.SMEM),
-            image_spec(patches),
-            whole_spec((images, patches)),
-            image_spec(patches),
-            *[image_spec(edge)] * 4,
-        ],
-        out_specs=whole_spec((parts, 3 * images, patches)),
+        in_specs=[pl.BlockSpec(memory_space=pltpu.SMEM)] + [whole] * 7,
+        out_specs=whole,
         out_shape=jax.ShapeDtypeStruct((parts, 3 * images, patches), F32),
         compiler_params=pltpu.CompilerParams(vmem_limit_bytes=16 * 2**20),
         cost_estimate=pl.CostEstimate(
@@ -338,8 +315,8 @@
 
     head_t, head_s = gathered_heads(teacher_head, student_head, tiles)
     logits, row_a, row_b, column_a, column_b = teacher_logits(place, teacher_tokens, head_t)
+    column_b = swapped(column_b, pairs_of(side, 1, 0, 1), parts, 0)
     column_a = swapped(column_a, pairs_of(side, 0, 0, 1), parts, 0)
-    column_b = swapped(column_b, pairs_of(side, 1, 0, 1), parts, 0)
     row_a, row_b = row_sums(place, row_a, row_b, column_a, column_b)
     row_a = swapped(row_a, pairs_of(side, 0, 1, 0), parts, 0)
     row_b = swapped(row_b, pairs_of(side, 1, 1, 0), parts, 0)

time: 123 us -> 123 us (level)
  no operation moved by 1% of the time
where the time goes in v7:
time: 123 us; the launch traced here: 122 us
  starting transfers between devices  53.5 us (43%)
  waiting for transfers between devices  46.3 us (38%)
  Pallas kernels  11.4 us (9%)
  local copies, waits for them, and re-layouts  7.84 us (6%)
  other arithmetic  2.33 us (2%)
    all_to_all x2, waiting for transfers between devices, along_y(): lax.all_to_all(pair, 'space', split_axis=0, concat_axis=0, tiled=True, ax...  19.9 us
    ppermute x4, starting transfers between devices, swapped(): return lax.ppermute(block, ('space', 'mp'), route)  13.3 us
    all_to_all x1, starting transfers between devices, everywhere_sum(): lax.all_to_all(x, ('space', 'mp'), split_axis=0, concat_axis=0, tiled=Tru...  12.2 us
    ppermute x1, starting transfers between devices, gathered_heads(): other = lax.ppermute(own, 'space', [(t, t ^ 1) for t in range(tiles)])  10.9 us
    all_to_all x2, starting transfers between devices, along_y(): lax.all_to_all(pair, 'space', split_axis=0, concat_axis=0, tiled=True, ax...  10.6 us
    all_to_all x1, waiting for transfers between devices, everywhere_sum(): lax.all_to_all(x, ('space', 'mp'), split_axis=0, concat_axis=0, tiled=Tru...  9.9 us
    ppermute x4, waiting for transfers between devices, swapped(): return lax.ppermute(block, ('space', 'mp'), route)  7.01 us
    all_to_all x1, starting transfers between devices, exchange(): return lax.all_to_all(x, axis, split_axis=0, concat_axis=0, tiled=True)  6.43 us
  transfers between devices with their start and end apart: 9, of which 5 were waited for; matrix products, arithmetic and copies ran while one was open for 1% of the time, Pallas kernels for 5%

profile of v7, /device:TPU:6, one launch (start us, length us, event | category | flops | bytes accessed | tf_op | source)
XLA Modules:
  0.0 122.3 jit_solution(13042321939329715831)
XLA Ops:
  0.6 0.8 fusion.2
  1.5 10.9 %collective-permute-start = (bf16[168,256]{1,0:T(8,128)(2,1)S(1)}, bf16[168,256]{1,0:T(8,128)(2,1)S(1)}, u32[]{:S(2)}, u32[]{:S(2)}) collective-permute-start(bf16[168,256]{1,0:T(8,128)(2,1)S(1)} %fusion.2), channel_id=1, source_target_pairs={{0,4},{4,0},{8,12},{12,8},{16,20},{20,16},{24,28},{28,24},{32,36},... | collective-permute-start | bytes 258056 | tf_op jit(solution)/shard_map/ppermute | solution.py:30
  12.4 3.7 %collective-permute-done = bf16[168,256]{1,0:T(8,128)(2,1)S(1)} collective-permute-done((bf16[168,256]{1,0:T(8,128)(2,1)S(1)}, bf16[168,256]{1,0:T(8,128)(2,1)S(1)}, u32[]{:S(2)}, u32[]{:S(2)}) %collective-permute-start) | collective-permute-done | bytes 86048 | tf_op jit(solution)/shard_map/ppermute | solution.py:30
  16.1 0.9 broadcast_select_fusion.1
  17.0 0.9 broadcast_in_dim.7
  18.0 7.1 %all-to-all-start = ((bf16[8,176,256]{2,1,0:T(8,128)(2,1)}), bf16[8,176,256]{2,1,0:T(8,128)(2,1)S(1)}, u32[]{:S(2)}, u32[]{:S(2)}) async-start(bf16[8,176,256]{2,1,0:T(8,128)(2,1)} %broadcast_in_dim.7), calls=%async_computation | async-start | bytes 1441792 | tf_op jit(solution)/shard_map/all_to_all | solution.py:36
  25.1 19.9 %all-to-all-done = bf16[8,176,256]{2,1,0:T(8,128)(2,1)S(1)} async-done(((bf16[8,176,256]{2,1,0:T(8,128)(2,1)}), bf16[8,176,256]{2,1,0:T(8,128)(2,1)S(1)}, u32[]{:S(2)}, u32[]{:S(2)}) %all-to-all-start) | async-done | bytes 720928 | tf_op jit(solution)/shard_map/all_to_all | solution.py:36
  45.0 0.9 broadcast_in_dim.6
  45.9 3.5 %all-to-all-start.1 = ((bf16[8,160,256]{2,1,0:T(8,128)(2,1)}), bf16[8,160,256]{2,1,0:T(8,128)(2,1)S(1)}, u32[]{:S(2)}, u32[]{:S(2)}) async-start(bf16[8,160,256]{2,1,0:T(8,128)(2,1)} %broadcast_in_dim.6), calls=%async_computation.1 | async-start | bytes 1310720 | tf_op jit(solution)/shard_map/all_to_all | solution.py:36
  49.5 0.1 stack.19.refs_0_.place_ref
  49.6 0.0 copy-start
  49.6 2.6 %copy-done = bf16[8,1,16,16,1408]{4,3,2,1,0:T(8,128)(2,1)S(1)} copy-done((bf16[8,1,16,16,1408]{4,3,2,1,0:T(8,128)(2,1)S(1)}, bf16[8,1,16,16,1408]{4,3,2,1,0:T(8,128)(2,1)}, u32[]{:S(2)}) %copy-start) | copy-done | bytes 5767192
  52.2 2.3 %teacher_logits.1 = (f32[8,256,256]{2,1,0:T(8,128)S(1)}, f32[8,16,256]{2,1,0:T(8,128)S(1)}, f32[8,16,256]{2,1,0:T(8,128)S(1)}, f32[8,16,256]{2,1,0:T(8,128)S(1)}, f32[8,16,256]{2,1,0:T(8,128)S(1)}) custom-call(s32[5]{0:T(128)S(1)} %stack.19.refs_0_.place_ref, bf16[8,1,16,16,1408]{4,3,2,1,0:T(8,128)(2,1)S(1)} %copy-done, bf16[1408,256]{1,0:T(8,128)(2,1)S(1)} %bitcast.9), custom_call_target="tpu_custom_call" | custom-call | flops 1476395008 | bytes 8585216 | tf_op jit(solution)/shard_map/teacher_logits/pallas_call | solution.py:99
  54.6 7.3 %collective-permute-start.1 = (f32[8,16,256]{2,1,0:T(8,128)S(1)}, f32[8,16,256]{2,1,0:T(8,128)S(1)}, u32[]{:S(2)}, u32[]{:S(2)}) collective-permute-start(f32[8,16,256]{2,1,0:T(8,128)S(1)} %get-tuple-element.22), channel_id=1, source_target_pairs={{0,4},{4,0},{1,5},{5,1},{2,6},{6,2},{3,7},{7,3},{8,12},{12,8},{9,1... | collective-permute-start | bytes 393224 | tf_op jit(solution)/shard_map/ppermute | solution.py:51
  61.9 0.7 collective-permute-start.2
  62.5 7.0 %collective-permute-done.1.column_a.refs_6_ = f32[8,16,256]{2,1,0:T(8,128)S(1)} collective-permute-done((f32[8,16,256]{2,1,0:T(8,128)S(1)}, f32[8,16,256]{2,1,0:T(8,128)S(1)}, u32[]{:S(2)}, u32[]{:S(2)}) %collective-permute-start.1) | collective-permute-done | bytes 131104 | tf_op jit(solution)/shard_map/ppermute | solution.py:51
  69.5 0.0 collective-permute-done.2.column_b.refs_7_
  69.5 1.3 %row_sums.1 = (f32[8,16,256]{2,1,0:T(8,128)}, f32[8,16,256]{2,1,0:T(8,128)S(1)}) custom-call(s32[5]{0:T(128)S(1)} %stack.19.refs_0_.place_ref, f32[8,16,256]{2,1,0:T(8,128)S(1)} %get-tuple-element.20.row_a, f32[8,16,256]{2,1,0:T(8,128)S(1)} %get-tuple-element.21.row_b, f32[8,16,256]{2,1,0:T(8,128)S(1)} %collective-permute-done.1.column_a.refs_6_, ...), custom_call_target="tpu_custom_call" | custom-call | flops 327680 | bytes 786432 | tf_op jit(solution)/shard_map/row_sums/pallas_call | solution.py:132
  70.8 4.7 %collective-permute-start.3 = (f32[8,16,256]{2,1,0:T(8,128)}, f32[8,16,256]{2,1,0:T(8,128)S(1)}, u32[]{:S(2)}, u32[]{:S(2)}) collective-permute-start(f32[8,16,256]{2,1,0:T(8,128)} %get-tuple-element.24), channel_id=1, source_target_pairs={{0,16},{16,0},{1,17},{17,1},{2,18},{18,2},{3,19},{19,3},{4,20},{20... | collective-permute-start | bytes 393224 | tf_op jit(solution)/shard_map/ppermute | solution.py:51
  75.5 0.7 collective-permute-start.4
  76.2 0.0 all-to-all-done.1
  76.2 0.0 copy-start.1
  76.2 2.5 %copy-done.1 = bf16[8,1,16,16,1280]{4,3,2,1,0:T(8,128)(2,1)S(1)} copy-done((bf16[8,1,16,16,1280]{4,3,2,1,0:T(8,128)(2,1)S(1)}, bf16[8,1,16,16,1280]{4,3,2,1,0:T(8,128)(2,1)}, u32[]{:S(2)}) %copy-start.1) | copy-done | bytes 5242904
  78.7 0.0 copy-start.2
  78.7 2.4 %student_logits.1 = (f32[8,256,256]{2,1,0:T(8,128)S(1)}, f32[8,256]{1,0:T(8,128)S(1)}) custom-call(bf16[8,1,16,16,1280]{4,3,2,1,0:T(8,128)(2,1)S(1)} %copy-done.1, bf16[1280,256]{1,0:T(8,128)(2,1)S(1)} %bitcast.10), custom_call_target="tpu_custom_call" | custom-call | flops 1342177280 | bytes 7995392 | tf_op jit(solution)/shard_map/student_logits/pallas_call | solution.py:162
  81.0 0.0 collective-permute-done.3.refs_4_
  81.0 0.0 collective-permute-done.4.refs_5_
  81.0 4.8 %patch_stats.1 = f32[4,24,256]{2,1,0:T(8,128)} custom-call(s32[5]{0:T(128)S(1)} %stack.19.refs_0_.place_ref, f32[8,256,256]{2,1,0:T(8,128)S(1)} %get-tuple-element.16.refs_1_, f32[8,256]{1,0:T(8,128)S(1)} %get-tuple-element.17.refs_2_, f32[8,256,256]{2,1,0:T(8,128)S(1)} %get-tuple-element.19.refs_3_, f32[8,16,256]{2,1,0:T(8,128)S(1)} %collective-permute-done.3.refs_4_, ...), custom_call_target="tpu_custom_call" | custom-call | flops 15728640 | bytes 4194304 | tf_op jit(solution)/shard_map/patch_stats/pallas_call | solution.py:240
  85.8 6.4 %all-to-all-start.2 = ((f32[4,24,256]{2,1,0:T(8,128)}), f32[4,24,256]{2,1,0:T(8,128)S(1)}, u32[]{:S(2)}, u32[]{:S(2)}) async-start(f32[4,24,256]{2,1,0:T(8,128)} %patch_stats.1), calls=%async_computation.2 | async-start | bytes 196608 | tf_op jit(solution)/shard_map/all_to_all | solution.py:20
  92.2 0.0 copy-done.2
  92.3 0.1 reshape.18.refs_1_
  92.3 5.7 %all-to-all-done.2.refs_0_ = f32[4,24,256]{2,1,0:T(8,128)S(1)} async-done(((f32[4,24,256]{2,1,0:T(8,128)}), f32[4,24,256]{2,1,0:T(8,128)S(1)}, u32[]{:S(2)}, u32[]{:S(2)}) %all-to-all-start.2) | async-done | bytes 98336 | tf_op jit(solution)/shard_map/all_to_all | solution.py:20
  98.1 0.7 patch_divergence.1
  98.8 12.2 %all-to-all-start.3 = ((f32[16,1,128]{2,1,0:T(1,128)}), f32[16,1,128]{2,1,0:T(1,128)S(1)}, u32[]{:S(2)}, u32[]{:S(2)}) async-start(f32[16,1,128]{2,1,0:T(1,128)} %get-tuple-element.27), calls=%async_computation.3 | async-start | bytes 16384 | tf_op jit(solution)/shard_map/all_to_all | solution.py:299
  111.0 0.7 reshape.19
  111.7 9.9 %all-to-all-done.3 = f32[16,1,128]{2,1,0:T(1,128)S(1)} async-done(((f32[16,1,128]{2,1,0:T(1,128)}), f32[16,1,128]{2,1,0:T(1,128)S(1)}, u32[]{:S(2)}, u32[]{:S(2)}) %all-to-all-start.3) | async-done | bytes 8224 | tf_op jit(solution)/shard_map/all_to_all | solution.py:299
  121.7 0.6 maximum_divide_fusion
  (7 shorter events, 0.1 us)
Async XLA Ops:
  1.5 14.7 %collective-permute-start = (bf16[168,256]{1,0:T(8,128)(2,1)S(1)}, bf16[168,256]{1,0:T(8,128)(2,1)S(1)}, u32[]{:S(2)}, u32[]{:S(2)}) collective-permute-start(bf16[168,256]{1,0:T(8,128)(2,1)S(1)} %fusion.2), channel_id=1, source_target_pairs={{0,4},{4,0},{8,12},{12,8},{16,20},{20,16},{24,28},{28,24},{32,36},... | collective-permute-start | bytes 258056 | tf_op jit(solution)/shard_map/ppermute | solution.py:30
  18.0 27.1 %all-to-all-start = ((bf16[8,176,256]{2,1,0:T(8,128)(2,1)}), bf16[8,176,256]{2,1,0:T(8,128)(2,1)S(1)}, u32[]{:S(2)}, u32[]{:S(2)}) async-start(bf16[8,176,256]{2,1,0:T(8,128)(2,1)} %broadcast_in_dim.7), calls=%async_computation | async-start | bytes 1441792 | tf_op jit(solution)/shard_map/all_to_all | solution.py:36
  45.9 30.2 %all-to-all-start.1 = ((bf16[8,160,256]{2,1,0:T(8,128)(2,1)}), bf16[8,160,256]{2,1,0:T(8,128)(2,1)S(1)}, u32[]{:S(2)}, u32[]{:S(2)}) async-start(bf16[8,160,256]{2,1,0:T(8,128)(2,1)} %broadcast_in_dim.6), calls=%async_computation.1 | async-start | bytes 1310720 | tf_op jit(solution)/shard_map/all_to_all | solution.py:36
  49.6 2.6 %copy-start = (bf16[8,1,16,16,1408]{4,3,2,1,0:T(8,128)(2,1)S(1)}, bf16[8,1,16,16,1408]{4,3,2,1,0:T(8,128)(2,1)}, u32[]{:S(2)}) copy-start(bf16[8,1,16,16,1408]{4,3,2,1,0:T(8,128)(2,1)} %refs_1_.1) | copy-start | bytes 17301508
  54.6 15.0 %collective-permute-start.1 = (f32[8,16,256]{2,1,0:T(8,128)S(1)}, f32[8,16,256]{2,1,0:T(8,128)S(1)}, u32[]{:S(2)}, u32[]{:S(2)}) collective-permute-start(f32[8,16,256]{2,1,0:T(8,128)S(1)} %get-tuple-element.22), channel_id=1, source_target_pairs={{0,4},{4,0},{1,5},{5,1},{2,6},{6,2},{3,7},{7,3},{8,12},{12,8},{9,1... | collective-permute-start | bytes 393224 | tf_op jit(solution)/shard_map/ppermute | solution.py:51
  61.9 7.7 %collective-permute-start.2 = (f32[8,16,256]{2,1,0:T(8,128)S(1)}, f32[8,16,256]{2,1,0:T(8,128)S(1)}, u32[]{:S(2)}, u32[]{:S(2)}) collective-permute-start(f32[8,16,256]{2,1,0:T(8,128)S(1)} %get-tuple-element.23), channel_id=1, source_target_pairs={{4,8},{8,4},{5,9},{9,5},{6,10},{10,6},{7,11},{11,7},{20,24},{24,20... | collective-permute-start | bytes 393224 | tf_op jit(solution)/shard_map/ppermute | solution.py:51
  70.8 10.2 %collective-permute-start.3 = (f32[8,16,256]{2,1,0:T(8,128)}, f32[8,16,256]{2,1,0:T(8,128)S(1)}, u32[]{:S(2)}, u32[]{:S(2)}) collective-permute-start(f32[8,16,256]{2,1,0:T(8,128)} %get-tuple-element.24), channel_id=1, source_target_pairs={{0,16},{16,0},{1,17},{17,1},{2,18},{18,2},{3,19},{19,3},{4,20},{20... | collective-permute-start | bytes 393224 | tf_op jit(solution)/shard_map/ppermute | solution.py:51
  75.5 5.6 %collective-permute-start.4 = (f32[8,16,256]{2,1,0:T(8,128)S(1)}, f32[8,16,256]{2,1,0:T(8,128)S(1)}, u32[]{:S(2)}, u32[]{:S(2)}) collective-permute-start(f32[8,16,256]{2,1,0:T(8,128)S(1)} %get-tuple-element.25), channel_id=1, source_target_pairs={{16,32},{32,16},{17,33},{33,17},{18,34},{34,18},{19,35},{35,19},{2... | collective-permute-start | bytes 393224 | tf_op jit(solution)/shard_map/ppermute | solution.py:51
  76.2 2.5 %copy-start.1 = (bf16[8,1,16,16,1280]{4,3,2,1,0:T(8,128)(2,1)S(1)}, bf16[8,1,16,16,1280]{4,3,2,1,0:T(8,128)(2,1)}, u32[]{:S(2)}) copy-start(bf16[8,1,16,16,1280]{4,3,2,1,0:T(8,128)(2,1)} %refs_0_.1) | copy-start | bytes 15728644
  78.7 13.6 %copy-start.2 = (s32[8,1,16,16]{3,2,1,0:T(8,128)S(1)}, s32[8,1,16,16]{3,2,1,0:T(8,128)}, u32[]{:S(2)}) copy-start(s32[8,1,16,16]{3,2,1,0:T(8,128)} %param.9) | copy-start | bytes 24580
  85.8 12.3 %all-to-all-start.2 = ((f32[4,24,256]{2,1,0:T(8,128)}), f32[4,24,256]{2,1,0:T(8,128)S(1)}, u32[]{:S(2)}, u32[]{:S(2)}) async-start(f32[4,24,256]{2,1,0:T(8,128)} %patch_stats.1), calls=%async_computation.2 | async-start | bytes 196608 | tf_op jit(solution)/shard_map/all_to_all | solution.py:20
  98.8 22.9 %all-to-all-start.3 = ((f32[16,1,128]{2,1,0:T(1,128)}), f32[16,1,128]{2,1,0:T(1,128)S(1)}, u32[]{:S(2)}, u32[]{:S(2)}) async-start(f32[16,1,128]{2,1,0:T(1,128)} %get-tuple-element.27), calls=%async_computation.3 | async-start | bytes 16384 | tf_op jit(solution)/shard_map/all_to_all | solution.py:299

commit v8 on v7

--- a/solution.py
+++ b/solution.py
@@ -191,6 +191,7 @@
     column_a,
     column_b,
     out_ref,
+    share_ref,
 ):
     image = pl.program_id(0)
     patches = edge * edge
@@ -199,11 +200,14 @@
 
     flat = logits_ref[image]
     cube = flat.reshape(shape)
-    x = lax.broadcasted_iota(jnp.int32, shape, 1)
-    to_left = jnp.broadcast_to(jnp.where(column_even, column_b[image], column_a[image])[:, None, :], shape)
-    to_right = jnp.broadcast_to(jnp.where(column_even, column_a[image], column_b[image])[:, None, :], shape)
-    before = jnp.where(x == 0, to_left, pltpu.roll(flat, 1, 0).reshape(shape))
-    after = jnp.where(x == edge - 1, to_right, pltpu.roll(flat, patches - 1, 0).reshape(shape))
+    half = edge // 2
+    x = lax.broadcasted_iota(jnp.int32, (edge, half, LANES), 1)
+    to_left = jnp.where(column_even, column_b[image], column_a[image])[:, None, :]
+    to_right = jnp.where(column_even, column_a[image], column_b[image])[:, None, :]
+    before = pltpu.roll(flat, 1, 0).reshape(shape)
+    before = jnp.concatenate([jnp.where(x == 0, to_left, before[:, :half]), before[:, half:]], axis=1)
+    after = pltpu.roll(flat, patches - 1, 0).reshape(shape)
+    after = jnp.concatenate([after[:, :half], jnp.where(x == half - 1, to_right, after[:, half:])], axis=1)
     rows = cube + before + after
     up = jnp.where(row_even, row_b[image], row_a[image])
     down = jnp.where(row_even, row_a[image], row_b[image])
@@ -211,15 +215,18 @@
     below = jnp.concatenate([rows[1:], down[None]], axis=0)
     total = rows + above + below
 
-    extent = place_ref[2]
-    place_y = place_ref[0] + lax.broadcasted_iota(jnp.int32, (edge, edge, 1), 0)
-    place_x = place_ref[1] + lax.broadcasted_iota(jnp.int32, (edge, edge, 1), 1)
-
-    def line(place):
-        return 1.0 + (place > 0).astype(F32) + (place < extent - 1).astype(F32)
-
-    share = 1.0 / (line(place_y) * line(place_x))
-    smoothed = (total * share).reshape(patches, LANES)[:, :classes]
+    @pl.when(image == 0)
+    def _():
+        extent = place_ref[2]
+        place_y = place_ref[0] + lax.broadcasted_iota(jnp.int32, shape, 0)
+        place_x = place_ref[1] + lax.broadcasted_iota(jnp.int32, shape, 1)
+
+        def line(place):
+            return 1.0 + (place > 0).astype(F32) + (place < extent - 1).astype(F32)
+
+        share_ref[...] = (1.0 / (line(place_y) * line(place_x))).reshape(patches, LANES)
+
+    smoothed = (total.reshape(patches, LANES) * share_ref[...])[:, :classes]
     student = student_ref[image][:, :classes]
 
     top_t = jnp.max(smoothed, axis=-1, keepdims=True)
@@ -243,6 +250,7 @@
         in_specs=[pl.BlockSpec(memory_space=pltpu.SMEM)] + [whole] * 7,
         out_specs=whole,
         out_shape=jax.ShapeDtypeStruct((parts, 3 * images, patches), F32),
+        scratch_shapes=[pltpu.VMEM((patches, LANES), F32)],
         compiler_params=pltpu.CompilerParams(vmem_limit_bytes=16 * 2**20),
         cost_estimate=pl.CostEstimate(
             flops=30 * images * patches * LANES,

time: 123 us -> 123 us (level)
  no operation moved by 1% of the time
where the time goes in v8:
time: 123 us
  starting transfers between devices  53.5 us (43%)
  waiting for transfers between devices  46.3 us (38%)
  Pallas kernels  11.7 us (10%)
  local copies, waits for them, and re-layouts  7.84 us (6%)
  other arithmetic  2.33 us (2%)
    all_to_all x2, waiting for transfers between devices, along_y(): lax.all_to_all(pair, 'space', split_axis=0, concat_axis=0, tiled=True, ax...  19.9 us
    ppermute x4, starting transfers between devices, swapped(): return lax.ppermute(block, ('space', 'mp'), route)  13.3 us
    all_to_all x1, starting transfers between devices, everywhere_sum(): lax.all_to_all(x, ('space', 'mp'), split_axis=0, concat_axis=0, tiled=Tru...  12.2 us
    ppermute x1, starting transfers between devices, gathered_heads(): other = lax.ppermute(own, 'space', [(t, t ^ 1) for t in range(tiles)])  10.9 us
    all_to_all x2, starting transfers between devices, along_y(): lax.all_to_all(pair, 'space', split_axis=0, concat_axis=0, tiled=True, ax...  10.6 us
    all_to_all x1, waiting for transfers between devices, everywhere_sum(): lax.all_to_all(x, ('space', 'mp'), split_axis=0, concat_axis=0, tiled=Tru...  9.9 us
    ppermute x4, waiting for transfers between devices, swapped(): return lax.ppermute(block, ('space', 'mp'), route)  7.01 us
    all_to_all x1, starting transfers between devices, exchange(): return lax.all_to_all(x, axis, split_axis=0, concat_axis=0, tiled=True)  6.43 us
  transfers between devices with their start and end apart: 9, of which 5 were waited for; matrix products, arithmetic and copies ran while one was open for 1% of the time, Pallas kernels for 5%

profile of v8, /device:TPU:6, one launch (start us, length us, event | category | flops | bytes accessed | tf_op | source)
XLA Modules:
  0.0 122.5 jit_solution(12405697995175922317)
XLA Ops:
  0.6 0.8 fusion.2
  1.5 10.9 %collective-permute-start = (bf16[168,256]{1,0:T(8,128)(2,1)S(1)}, bf16[168,256]{1,0:T(8,128)(2,1)S(1)}, u32[]{:S(2)}, u32[]{:S(2)}) collective-permute-start(bf16[168,256]{1,0:T(8,128)(2,1)S(1)} %fusion.2), channel_id=1, source_target_pairs={{0,4},{4,0},{8,12},{12,8},{16,20},{20,16},{24,28},{28,24},{32,36},... | collective-permute-start | bytes 258056 | tf_op jit(solution)/shard_map/ppermute | solution.py:30
  12.4 3.7 %collective-permute-done = bf16[168,256]{1,0:T(8,128)(2,1)S(1)} collective-permute-done((bf16[168,256]{1,0:T(8,128)(2,1)S(1)}, bf16[168,256]{1,0:T(8,128)(2,1)S(1)}, u32[]{:S(2)}, u32[]{:S(2)}) %collective-permute-start) | collective-permute-done | bytes 86048 | tf_op jit(solution)/shard_map/ppermute | solution.py:30
  16.1 0.9 broadcast_select_fusion.1
  17.0 0.9 broadcast_in_dim.7
  18.0 7.1 %all-to-all-start = ((bf16[8,176,256]{2,1,0:T(8,128)(2,1)}), bf16[8,176,256]{2,1,0:T(8,128)(2,1)S(1)}, u32[]{:S(2)}, u32[]{:S(2)}) async-start(bf16[8,176,256]{2,1,0:T(8,128)(2,1)} %broadcast_in_dim.7), calls=%async_computation | async-start | bytes 1441792 | tf_op jit(solution)/shard_map/all_to_all | solution.py:36
  25.1 19.9 %all-to-all-done = bf16[8,176,256]{2,1,0:T(8,128)(2,1)S(1)} async-done(((bf16[8,176,256]{2,1,0:T(8,128)(2,1)}), bf16[8,176,256]{2,1,0:T(8,128)(2,1)S(1)}, u32[]{:S(2)}, u32[]{:S(2)}) %all-to-all-start) | async-done | bytes 720928 | tf_op jit(solution)/shard_map/all_to_all | solution.py:36
  45.0 0.9 broadcast_in_dim.6
  45.9 3.5 %all-to-all-start.1 = ((bf16[8,160,256]{2,1,0:T(8,128)(2,1)}), bf16[8,160,256]{2,1,0:T(8,128)(2,1)S(1)}, u32[]{:S(2)}, u32[]{:S(2)}) async-start(bf16[8,160,256]{2,1,0:T(8,128)(2,1)} %broadcast_in_dim.6), calls=%async_computation.1 | async-start | bytes 1310720 | tf_op jit(solution)/shard_map/all_to_all | solution.py:36
  49.5 0.1 stack.19.refs_0_.place_ref
  49.6 0.0 copy-start
  49.6 2.6 %copy-done = bf16[8,1,16,16,1408]{4,3,2,1,0:T(8,128)(2,1)S(1)} copy-done((bf16[8,1,16,16,1408]{4,3,2,1,0:T(8,128)(2,1)S(1)}, bf16[8,1,16,16,1408]{4,3,2,1,0:T(8,128)(2,1)}, u32[]{:S(2)}) %copy-start) | copy-done | bytes 5767192
  52.2 2.3 %teacher_logits.1 = (f32[8,256,256]{2,1,0:T(8,128)S(1)}, f32[8,16,256]{2,1,0:T(8,128)S(1)}, f32[8,16,256]{2,1,0:T(8,128)S(1)}, f32[8,16,256]{2,1,0:T(8,128)S(1)}, f32[8,16,256]{2,1,0:T(8,128)S(1)}) custom-call(s32[5]{0:T(128)S(1)} %stack.19.refs_0_.place_ref, bf16[8,1,16,16,1408]{4,3,2,1,0:T(8,128)(2,1)S(1)} %copy-done, bf16[1408,256]{1,0:T(8,128)(2,1)S(1)} %bitcast.9), custom_call_target="tpu_custom_call" | custom-call | flops 1476395008 | bytes 8585216 | tf_op jit(solution)/shard_map/teacher_logits/pallas_call | solution.py:99
  54.6 7.3 %collective-permute-start.1 = (f32[8,16,256]{2,1,0:T(8,128)S(1)}, f32[8,16,256]{2,1,0:T(8,128)S(1)}, u32[]{:S(2)}, u32[]{:S(2)}) collective-permute-start(f32[8,16,256]{2,1,0:T(8,128)S(1)} %get-tuple-element.22), channel_id=1, source_target_pairs={{0,4},{4,0},{1,5},{5,1},{2,6},{6,2},{3,7},{7,3},{8,12},{12,8},{9,1... | collective-permute-start | bytes 393224 | tf_op jit(solution)/shard_map/ppermute | solution.py:51
  61.9 0.7 collective-permute-start.2
  62.5 7.0 %collective-permute-done.1.column_a.refs_6_ = f32[8,16,256]{2,1,0:T(8,128)S(1)} collective-permute-done((f32[8,16,256]{2,1,0:T(8,128)S(1)}, f32[8,16,256]{2,1,0:T(8,128)S(1)}, u32[]{:S(2)}, u32[]{:S(2)}) %collective-permute-start.1) | collective-permute-done | bytes 131104 | tf_op jit(solution)/shard_map/ppermute | solution.py:51
  69.5 0.0 collective-permute-done.2.column_b.refs_7_
  69.5 1.3 %row_sums.1 = (f32[8,16,256]{2,1,0:T(8,128)}, f32[8,16,256]{2,1,0:T(8,128)S(1)}) custom-call(s32[5]{0:T(128)S(1)} %stack.19.refs_0_.place_ref, f32[8,16,256]{2,1,0:T(8,128)S(1)} %get-tuple-element.20.row_a, f32[8,16,256]{2,1,0:T(8,128)S(1)} %get-tuple-element.21.row_b, f32[8,16,256]{2,1,0:T(8,128)S(1)} %collective-permute-done.1.column_a.refs_6_, ...), custom_call_target="tpu_custom_call" | custom-call | flops 327680 | bytes 786432 | tf_op jit(solution)/shard_map/row_sums/pallas_call | solution.py:132
  70.8 4.7 %collective-permute-start.3 = (f32[8,16,256]{2,1,0:T(8,128)}, f32[8,16,256]{2,1,0:T(8,128)S(1)}, u32[]{:S(2)}, u32[]{:S(2)}) collective-permute-start(f32[8,16,256]{2,1,0:T(8,128)} %get-tuple-element.24), channel_id=1, source_target_pairs={{0,16},{16,0},{1,17},{17,1},{2,18},{18,2},{3,19},{19,3},{4,20},{20... | collective-permute-start | bytes 393224 | tf_op jit(solution)/shard_map/ppermute | solution.py:51
  75.5 0.7 collective-permute-start.4
  76.2 0.0 all-to-all-done.1
  76.2 0.0 copy-start.1
  76.2 2.5 %copy-done.1 = bf16[8,1,16,16,1280]{4,3,2,1,0:T(8,128)(2,1)S(1)} copy-done((bf16[8,1,16,16,1280]{4,3,2,1,0:T(8,128)(2,1)S(1)}, bf16[8,1,16,16,1280]{4,3,2,1,0:T(8,128)(2,1)}, u32[]{:S(2)}) %copy-start.1) | copy-done | bytes 5242904
  78.7 0.0 copy-start.2
  78.7 2.4 %student_logits.1 = (f32[8,256,256]{2,1,0:T(8,128)S(1)}, f32[8,256]{1,0:T(8,128)S(1)}) custom-call(bf16[8,1,16,16,1280]{4,3,2,1,0:T(8,128)(2,1)S(1)} %copy-done.1, bf16[1280,256]{1,0:T(8,128)(2,1)S(1)} %bitcast.10), custom_call_target="tpu_custom_call" | custom-call | flops 1342177280 | bytes 7995392 | tf_op jit(solution)/shard_map/student_logits/pallas_call | solution.py:162
  81.0 0.0 collective-permute-done.3.refs_4_
  81.0 0.0 collective-permute-done.4.refs_5_
  81.0 5.0 %patch_stats.1 = f32[4,24,256]{2,1,0:T(8,128)} custom-call(s32[5]{0:T(128)S(1)} %stack.19.refs_0_.place_ref, f32[8,256,256]{2,1,0:T(8,128)S(1)} %get-tuple-element.16.refs_1_, f32[8,256]{1,0:T(8,128)S(1)} %get-tuple-element.17.refs_2_, f32[8,256,256]{2,1,0:T(8,128)S(1)} %get-tuple-element.19.refs_3_, f32[8,16,256]{2,1,0:T(8,128)S(1)} %collective-permute-done.3.refs_4_, ...), custom_call_target="tpu_custom_call" | custom-call | flops 15728640 | bytes 4194304 | tf_op jit(solution)/shard_map/patch_stats/pallas_call | solution.py:247
  86.1 6.4 %all-to-all-start.2 = ((f32[4,24,256]{2,1,0:T(8,128)}), f32[4,24,256]{2,1,0:T(8,128)S(1)}, u32[]{:S(2)}, u32[]{:S(2)}) async-start(f32[4,24,256]{2,1,0:T(8,128)} %patch_stats.1), calls=%async_computation.2 | async-start | bytes 196608 | tf_op jit(solution)/shard_map/all_to_all | solution.py:20
  92.5 0.0 copy-done.2
  92.5 0.1 reshape.18.refs_1_
  92.6 5.7 %all-to-all-done.2.refs_0_ = f32[4,24,256]{2,1,0:T(8,128)S(1)} async-done(((f32[4,24,256]{2,1,0:T(8,128)}), f32[4,24,256]{2,1,0:T(8,128)S(1)}, u32[]{:S(2)}, u32[]{:S(2)}) %all-to-all-start.2) | async-done | bytes 98336 | tf_op jit(solution)/shard_map/all_to_all | solution.py:20
  98.3 0.7 patch_divergence.1
  99.0 12.2 %all-to-all-start.3 = ((f32[16,1,128]{2,1,0:T(1,128)}), f32[16,1,128]{2,1,0:T(1,128)S(1)}, u32[]{:S(2)}, u32[]{:S(2)}) async-start(f32[16,1,128]{2,1,0:T(1,128)} %get-tuple-element.27), calls=%async_computation.3 | async-start | bytes 16384 | tf_op jit(solution)/shard_map/all_to_all | solution.py:307
  111.3 0.7 reshape.19
  112.0 9.9 %all-to-all-done.3 = f32[16,1,128]{2,1,0:T(1,128)S(1)} async-done(((f32[16,1,128]{2,1,0:T(1,128)}), f32[16,1,128]{2,1,0:T(1,128)S(1)}, u32[]{:S(2)}, u32[]{:S(2)}) %all-to-all-start.3) | async-done | bytes 8224 | tf_op jit(solution)/shard_map/all_to_all | solution.py:307
  121.9 0.6 maximum_divide_fusion
  (7 shorter events, 0.1 us)
Async XLA Ops:
  1.5 14.7 %collective-permute-start = (bf16[168,256]{1,0:T(8,128)(2,1)S(1)}, bf16[168,256]{1,0:T(8,128)(2,1)S(1)}, u32[]{:S(2)}, u32[]{:S(2)}) collective-permute-start(bf16[168,256]{1,0:T(8,128)(2,1)S(1)} %fusion.2), channel_id=1, source_target_pairs={{0,4},{4,0},{8,12},{12,8},{16,20},{20,16},{24,28},{28,24},{32,36},... | collective-permute-start | bytes 258056 | tf_op jit(solution)/shard_map/ppermute | solution.py:30
  18.0 27.1 %all-to-all-start = ((bf16[8,176,256]{2,1,0:T(8,128)(2,1)}), bf16[8,176,256]{2,1,0:T(8,128)(2,1)S(1)}, u32[]{:S(2)}, u32[]{:S(2)}) async-start(bf16[8,176,256]{2,1,0:T(8,128)(2,1)} %broadcast_in_dim.7), calls=%async_computation | async-start | bytes 1441792 | tf_op jit(solution)/shard_map/all_to_all | solution.py:36
  45.9 30.2 %all-to-all-start.1 = ((bf16[8,160,256]{2,1,0:T(8,128)(2,1)}), bf16[8,160,256]{2,1,0:T(8,128)(2,1)S(1)}, u32[]{:S(2)}, u32[]{:S(2)}) async-start(bf16[8,160,256]{2,1,0:T(8,128)(2,1)} %broadcast_in_dim.6), calls=%async_computation.1 | async-start | bytes 1310720 | tf_op jit(solution)/shard_map/all_to_all | solution.py:36
  49.6 2.6 %copy-start = (bf16[8,1,16,16,1408]{4,3,2,1,0:T(8,128)(2,1)S(1)}, bf16[8,1,16,16,1408]{4,3,2,1,0:T(8,128)(2,1)}, u32[]{:S(2)}) copy-start(bf16[8,1,16,16,1408]{4,3,2,1,0:T(8,128)(2,1)} %refs_1_.1) | copy-start | bytes 17301508
  54.6 15.0 %collective-permute-start.1 = (f32[8,16,256]{2,1,0:T(8,128)S(1)}, f32[8,16,256]{2,1,0:T(8,128)S(1)}, u32[]{:S(2)}, u32[]{:S(2)}) collective-permute-start(f32[8,16,256]{2,1,0:T(8,128)S(1)} %get-tuple-element.22), channel_id=1, source_target_pairs={{0,4},{4,0},{1,5},{5,1},{2,6},{6,2},{3,7},{7,3},{8,12},{12,8},{9,1... | collective-permute-start | bytes 393224 | tf_op jit(solution)/shard_map/ppermute | solution.py:51
  61.9 7.7 %collective-permute-start.2 = (f32[8,16,256]{2,1,0:T(8,128)S(1)}, f32[8,16,256]{2,1,0:T(8,128)S(1)}, u32[]{:S(2)}, u32[]{:S(2)}) collective-permute-start(f32[8,16,256]{2,1,0:T(8,128)S(1)} %get-tuple-element.23), channel_id=1, source_target_pairs={{4,8},{8,4},{5,9},{9,5},{6,10},{10,6},{7,11},{11,7},{20,24},{24,20... | collective-permute-start | bytes 393224 | tf_op jit(solution)/shard_map/ppermute | solution.py:51
  70.8 10.2 %collective-permute-start.3 = (f32[8,16,256]{2,1,0:T(8,128)}, f32[8,16,256]{2,1,0:T(8,128)S(1)}, u32[]{:S(2)}, u32[]{:S(2)}) collective-permute-start(f32[8,16,256]{2,1,0:T(8,128)} %get-tuple-element.24), channel_id=1, source_target_pairs={{0,16},{16,0},{1,17},{17,1},{2,18},{18,2},{3,19},{19,3},{4,20},{20... | collective-permute-start | bytes 393224 | tf_op jit(solution)/shard_map/ppermute | solution.py:51
  75.5 5.6 %collective-permute-start.4 = (f32[8,16,256]{2,1,0:T(8,128)S(1)}, f32[8,16,256]{2,1,0:T(8,128)S(1)}, u32[]{:S(2)}, u32[]{:S(2)}) collective-permute-start(f32[8,16,256]{2,1,0:T(8,128)S(1)} %get-tuple-element.25), channel_id=1, source_target_pairs={{16,32},{32,16},{17,33},{33,17},{18,34},{34,18},{19,35},{35,19},{2... | collective-permute-start | bytes 393224 | tf_op jit(solution)/shard_map/ppermute | solution.py:51
  76.2 2.5 %copy-start.1 = (bf16[8,1,16,16,1280]{4,3,2,1,0:T(8,128)(2,1)S(1)}, bf16[8,1,16,16,1280]{4,3,2,1,0:T(8,128)(2,1)}, u32[]{:S(2)}) copy-start(bf16[8,1,16,16,1280]{4,3,2,1,0:T(8,128)(2,1)} %refs_0_.1) | copy-start | bytes 15728644
  78.7 13.8 %copy-start.2 = (s32[8,1,16,16]{3,2,1,0:T(8,128)S(1)}, s32[8,1,16,16]{3,2,1,0:T(8,128)}, u32[]{:S(2)}) copy-start(s32[8,1,16,16]{3,2,1,0:T(8,128)} %param.9) | copy-start | bytes 24580
  86.1 12.3 %all-to-all-start.2 = ((f32[4,24,256]{2,1,0:T(8,128)}), f32[4,24,256]{2,1,0:T(8,128)S(1)}, u32[]{:S(2)}, u32[]{:S(2)}) async-start(f32[4,24,256]{2,1,0:T(8,128)} %patch_stats.1), calls=%async_computation.2 | async-start | bytes 196608 | tf_op jit(solution)/shard_map/all_to_all | solution.py:20
  99.0 22.9 %all-to-all-start.3 = ((f32[16,1,128]{2,1,0:T(1,128)}), f32[16,1,128]{2,1,0:T(1,128)S(1)}, u32[]{:S(2)}, u32[]{:S(2)}) async-start(f32[16,1,128]{2,1,0:T(1,128)} %get-tuple-element.27), calls=%async_computation.3 | async-start | bytes 16384 | tf_op jit(solution)/shard_map/all_to_all | solution.py:307

commit v9 on v7

--- a/solution.py
+++ b/solution.py
@@ -191,46 +191,51 @@
     column_a,
     column_b,
     out_ref,
+    share_ref,
 ):
-    image = pl.program_id(0)
     patches = edge * edge
     shape = (edge, edge, LANES)
     row_even, column_even = place_ref[3] == 1, place_ref[4] == 1
 
-    flat = logits_ref[image]
-    cube = flat.reshape(shape)
-    x = lax.broadcasted_iota(jnp.int32, shape, 1)
-    to_left = jnp.broadcast_to(jnp.where(column_even, column_b[image], column_a[image])[:, None, :], shape)
-    to_right = jnp.broadcast_to(jnp.where(column_even, column_a[image], column_b[image])[:, None, :], shape)
-    before = jnp.where(x == 0, to_left, pltpu.roll(flat, 1, 0).reshape(shape))
-    after = jnp.where(x == edge - 1, to_right, pltpu.roll(flat, patches - 1, 0).reshape(shape))
-    rows = cube + before + after
-    up = jnp.where(row_even, row_b[image], row_a[image])
-    down = jnp.where(row_even, row_a[image], row_b[image])
-    above = jnp.concatenate([up[None], rows[:-1]], axis=0)
-    below = jnp.concatenate([rows[1:], down[None]], axis=0)
-    total = rows + above + below
-
     extent = place_ref[2]
-    place_y = place_ref[0] + lax.broadcasted_iota(jnp.int32, (edge, edge, 1), 0)
-    place_x = place_ref[1] + lax.broadcasted_iota(jnp.int32, (edge, edge, 1), 1)
+    place_y = place_ref[0] + lax.broadcasted_iota(jnp.int32, shape, 0)
+    place_x = place_ref[1] + lax.broadcasted_iota(jnp.int32, shape, 1)
 
     def line(place):
         return 1.0 + (place > 0).astype(F32) + (place < extent - 1).astype(F32)
 
-    share = 1.0 / (line(place_y) * line(place_x))
-    smoothed = (total * share).reshape(patches, LANES)[:, :classes]
-    student = student_ref[image][:, :classes]
-
-    top_t = jnp.max(smoothed, axis=-1, keepdims=True)
-    expo_t = jnp.exp(smoothed - top_t)
-    sum_t = jnp.sum(expo_t, axis=-1, keepdims=True)
-    gap = jnp.sum(expo_t * (smoothed - student), axis=-1, keepdims=True)
-    top_t, sum_t, gap = in_lanes([top_t, sum_t, gap])
-    lse_s = lse_ref[pl.ds(image, 1), :]
-    for k, stat in enumerate((top_t + jnp.log(sum_t), gap / sum_t, lse_s)):
-        for c in range(parts):
-            out_ref[c, pl.ds(k * images + image, 1), :] = stat
+    share_ref[...] = (1.0 / (line(place_y) * line(place_x))).reshape(patches, LANES)
+
+    half = edge // 2
+    x = lax.broadcasted_iota(jnp.int32, (edge, half, LANES), 1)
+    for image in range(images):
+        flat = logits_ref[image]
+        cube = flat.reshape(shape)
+        to_left = jnp.where(column_even, column_b[image], column_a[image])[:, None, :]
+        to_right = jnp.where(column_even, column_a[image], column_b[image])[:, None, :]
+        before = pltpu.roll(flat, 1, 0).reshape(shape)
+        before = jnp.concatenate([jnp.where(x == 0, to_left, before[:, :half]), before[:, half:]], axis=1)
+        after = pltpu.roll(flat, patches - 1, 0).reshape(shape)
+        after = jnp.concatenate([after[:, :half], jnp.where(x == half - 1, to_right, after[:, half:])], axis=1)
+        rows = cube + before + after
+        up = jnp.where(row_even, row_b[image], row_a[image])
+        down = jnp.where(row_even, row_a[image], row_b[image])
+        above = jnp.concatenate([up[None], rows[:-1]], axis=0)
+        below = jnp.concatenate([rows[1:], down[None]], axis=0)
+        total = rows + above + below
+
+        smoothed = (total.reshape(patches, LANES) * share_ref[...])[:, :classes]
+        student = student_ref[image][:, :classes]
+
+        top_t = jnp.max(smoothed, axis=-1, keepdims=True)
+        expo_t = jnp.exp(smoothed - top_t)
+        sum_t = jnp.sum(expo_t, axis=-1, keepdims=True)
+        gap = jnp.sum(expo_t * (smoothed - student), axis=-1, keepdims=True)
+        top_t, sum_t, gap = in_lanes([top_t, sum_t, gap])
+        lse_s = lse_ref[image : image + 1, :]
+        for k, stat in enumerate((top_t + jnp.log(sum_t), gap / sum_t, lse_s)):
+            for c in range(parts):
+                out_ref[c, k * images + image : k * images + image + 1, :] = stat
 
 
 def patch_stats(place, student, lse_s, logits, borders, classes, parts):
@@ -239,10 +244,10 @@
     whole = pl.BlockSpec(memory_space=pltpu.VMEM)
     return pl.pallas_call(
         lambda *refs: stats_kernel(edge, classes, parts, images, *refs),
-        grid=(images,),
         in_specs=[pl.BlockSpec(memory_space=pltpu.SMEM)] + [whole] * 7,
         out_specs=whole,
         out_shape=jax.ShapeDtypeStruct((parts, 3 * images, patches), F32),
+        scratch_shapes=[pltpu.VMEM((patches, LANES), F32)],
         compiler_params=pltpu.CompilerParams(vmem_limit_bytes=16 * 2**20),
         cost_estimate=pl.CostEstimate(
             flops=30 * images * patches * LANES,

time: 123 us -> 121 us (0.984)
  Pallas kernels: 11.4 us -> 9.82 us
    pallas_call x1, Pallas kernels: 4.77 us -> 3.17 us  [patch_stats(): pl.pallas_call(lambda *refs: stats_kernel(edge, classes, parts, images, *...]
where the time goes in v9:
time: 121 us
  starting transfers between devices  53.5 us (44%)
  waiting for transfers between devices  46.3 us (38%)
  Pallas kernels  9.82 us (8%)
  local copies, waits for them, and re-layouts  7.84 us (6%)
  other arithmetic  2.33 us (2%)
    all_to_all x2, waiting for transfers between devices, along_y(): lax.all_to_all(pair, 'space', split_axis=0, concat_axis=0, tiled=True, ax...  19.9 us
    ppermute x4, starting transfers between devices, swapped(): return lax.ppermute(block, ('space', 'mp'), route)  13.3 us
    all_to_all x1, starting transfers between devices, everywhere_sum(): lax.all_to_all(x, ('space', 'mp'), split_axis=0, concat_axis=0, tiled=Tru...  12.3 us
    ppermute x1, starting transfers between devices, gathered_heads(): other = lax.ppermute(own, 'space', [(t, t ^ 1) for t in range(tiles)])  10.9 us
    all_to_all x2, starting transfers between devices, along_y(): lax.all_to_all(pair, 'space', split_axis=0, concat_axis=0, tiled=True, ax...  10.6 us
    all_to_all x1, waiting for transfers between devices, everywhere_sum(): lax.all_to_all(x, ('space', 'mp'), split_axis=0, concat_axis=0, tiled=Tru...  9.9 us
    ppermute x4, waiting for transfers between devices, swapped(): return lax.ppermute(block, ('space', 'mp'), route)  7.01 us
    all_to_all x1, starting transfers between devices, exchange(): return lax.all_to_all(x, axis, split_axis=0, concat_axis=0, tiled=True)  6.43 us
  transfers between devices with their start and end apart: 9, of which 5 were waited for; matrix products, arithmetic and copies ran while one was open for 1% of the time, Pallas kernels for 5%

profile of v9, /device:TPU:6, one launch (start us, length us, event | category | flops | bytes accessed | tf_op | source)
XLA Modules:
  0.0 120.7 jit_solution(3280356449407802243)
XLA Ops:
  0.6 0.8 fusion.2
  1.5 10.9 %collective-permute-start = (bf16[168,256]{1,0:T(8,128)(2,1)S(1)}, bf16[168,256]{1,0:T(8,128)(2,1)S(1)}, u32[]{:S(2)}, u32[]{:S(2)}) collective-permute-start(bf16[168,256]{1,0:T(8,128)(2,1)S(1)} %fusion.2), channel_id=1, source_target_pairs={{0,4},{4,0},{8,12},{12,8},{16,20},{20,16},{24,28},{28,24},{32,36},... | collective-permute-start | bytes 258056 | tf_op jit(solution)/shard_map/ppermute | solution.py:30
  12.4 3.7 %collective-permute-done = bf16[168,256]{1,0:T(8,128)(2,1)S(1)} collective-permute-done((bf16[168,256]{1,0:T(8,128)(2,1)S(1)}, bf16[168,256]{1,0:T(8,128)(2,1)S(1)}, u32[]{:S(2)}, u32[]{:S(2)}) %collective-permute-start) | collective-permute-done | bytes 86048 | tf_op jit(solution)/shard_map/ppermute | solution.py:30
  16.1 0.9 broadcast_select_fusion.1
  17.0 0.9 broadcast_in_dim.7
  18.0 7.1 %all-to-all-start = ((bf16[8,176,256]{2,1,0:T(8,128)(2,1)}), bf16[8,176,256]{2,1,0:T(8,128)(2,1)S(1)}, u32[]{:S(2)}, u32[]{:S(2)}) async-start(bf16[8,176,256]{2,1,0:T(8,128)(2,1)} %broadcast_in_dim.7), calls=%async_computation | async-start | bytes 1441792 | tf_op jit(solution)/shard_map/all_to_all | solution.py:36
  25.1 19.9 %all-to-all-done = bf16[8,176,256]{2,1,0:T(8,128)(2,1)S(1)} async-done(((bf16[8,176,256]{2,1,0:T(8,128)(2,1)}), bf16[8,176,256]{2,1,0:T(8,128)(2,1)S(1)}, u32[]{:S(2)}, u32[]{:S(2)}) %all-to-all-start) | async-done | bytes 720928 | tf_op jit(solution)/shard_map/all_to_all | solution.py:36
  45.0 0.9 broadcast_in_dim.6
  45.9 3.5 %all-to-all-start.1 = ((bf16[8,160,256]{2,1,0:T(8,128)(2,1)}), bf16[8,160,256]{2,1,0:T(8,128)(2,1)S(1)}, u32[]{:S(2)}, u32[]{:S(2)}) async-start(bf16[8,160,256]{2,1,0:T(8,128)(2,1)} %broadcast_in_dim.6), calls=%async_computation.1 | async-start | bytes 1310720 | tf_op jit(solution)/shard_map/all_to_all | solution.py:36
  49.5 0.1 stack.19.refs_0_.place_ref
  49.6 0.0 copy-start
  49.6 2.6 %copy-done = bf16[8,1,16,16,1408]{4,3,2,1,0:T(8,128)(2,1)S(1)} copy-done((bf16[8,1,16,16,1408]{4,3,2,1,0:T(8,128)(2,1)S(1)}, bf16[8,1,16,16,1408]{4,3,2,1,0:T(8,128)(2,1)}, u32[]{:S(2)}) %copy-start) | copy-done | bytes 5767192
  52.2 2.3 %teacher_logits.1 = (f32[8,256,256]{2,1,0:T(8,128)S(1)}, f32[8,16,256]{2,1,0:T(8,128)S(1)}, f32[8,16,256]{2,1,0:T(8,128)S(1)}, f32[8,16,256]{2,1,0:T(8,128)S(1)}, f32[8,16,256]{2,1,0:T(8,128)S(1)}) custom-call(s32[5]{0:T(128)S(1)} %stack.19.refs_0_.place_ref, bf16[8,1,16,16,1408]{4,3,2,1,0:T(8,128)(2,1)S(1)} %copy-done, bf16[1408,256]{1,0:T(8,128)(2,1)S(1)} %bitcast.9), custom_call_target="tpu_custom_call" | custom-call | flops 1476395008 | bytes 8585216 | tf_op jit(solution)/shard_map/teacher_logits/pallas_call | solution.py:99
  54.6 7.3 %collective-permute-start.1 = (f32[8,16,256]{2,1,0:T(8,128)S(1)}, f32[8,16,256]{2,1,0:T(8,128)S(1)}, u32[]{:S(2)}, u32[]{:S(2)}) collective-permute-start(f32[8,16,256]{2,1,0:T(8,128)S(1)} %get-tuple-element.22), channel_id=1, source_target_pairs={{0,4},{4,0},{1,5},{5,1},{2,6},{6,2},{3,7},{7,3},{8,12},{12,8},{9,1... | collective-permute-start | bytes 393224 | tf_op jit(solution)/shard_map/ppermute | solution.py:51
  61.9 0.7 collective-permute-start.2
  62.5 7.0 %collective-permute-done.1.column_a.refs_6_ = f32[8,16,256]{2,1,0:T(8,128)S(1)} collective-permute-done((f32[8,16,256]{2,1,0:T(8,128)S(1)}, f32[8,16,256]{2,1,0:T(8,128)S(1)}, u32[]{:S(2)}, u32[]{:S(2)}) %collective-permute-start.1) | collective-permute-done | bytes 131104 | tf_op jit(solution)/shard_map/ppermute | solution.py:51
  69.5 0.0 collective-permute-done.2.column_b.refs_7_
  69.5 1.3 %row_sums.1 = (f32[8,16,256]{2,1,0:T(8,128)}, f32[8,16,256]{2,1,0:T(8,128)S(1)}) custom-call(s32[5]{0:T(128)S(1)} %stack.19.refs_0_.place_ref, f32[8,16,256]{2,1,0:T(8,128)S(1)} %get-tuple-element.20.row_a, f32[8,16,256]{2,1,0:T(8,128)S(1)} %get-tuple-element.21.row_b, f32[8,16,256]{2,1,0:T(8,128)S(1)} %collective-permute-done.1.column_a.refs_6_, ...), custom_call_target="tpu_custom_call" | custom-call | flops 327680 | bytes 786432 | tf_op jit(solution)/shard_map/row_sums/pallas_call | solution.py:132
  70.8 4.7 %collective-permute-start.3 = (f32[8,16,256]{2,1,0:T(8,128)}, f32[8,16,256]{2,1,0:T(8,128)S(1)}, u32[]{:S(2)}, u32[]{:S(2)}) collective-permute-start(f32[8,16,256]{2,1,0:T(8,128)} %get-tuple-element.24), channel_id=1, source_target_pairs={{0,16},{16,0},{1,17},{17,1},{2,18},{18,2},{3,19},{19,3},{4,20},{20... | collective-permute-start | bytes 393224 | tf_op jit(solution)/shard_map/ppermute | solution.py:51
  75.5 0.7 collective-permute-start.4
  76.2 0.0 all-to-all-done.1
  76.2 0.0 copy-start.1
  76.2 2.5 %copy-done.1 = bf16[8,1,16,16,1280]{4,3,2,1,0:T(8,128)(2,1)S(1)} copy-done((bf16[8,1,16,16,1280]{4,3,2,1,0:T(8,128)(2,1)S(1)}, bf16[8,1,16,16,1280]{4,3,2,1,0:T(8,128)(2,1)}, u32[]{:S(2)}) %copy-start.1) | copy-done | bytes 5242904
  78.7 0.0 copy-start.2
  78.7 2.4 %student_logits.1 = (f32[8,256,256]{2,1,0:T(8,128)S(1)}, f32[8,256]{1,0:T(8,128)S(1)}) custom-call(bf16[8,1,16,16,1280]{4,3,2,1,0:T(8,128)(2,1)S(1)} %copy-done.1, bf16[1280,256]{1,0:T(8,128)(2,1)S(1)} %bitcast.10), custom_call_target="tpu_custom_call" | custom-call | flops 1342177280 | bytes 7995392 | tf_op jit(solution)/shard_map/student_logits/pallas_call | solution.py:162
  81.0 0.0 collective-permute-done.3.refs_4_
  81.0 0.0 collective-permute-done.4.refs_5_
  81.0 3.2 %patch_stats.1 = f32[4,24,256]{2,1,0:T(8,128)} custom-call(s32[5]{0:T(128)S(1)} %stack.19.refs_0_.place_ref, f32[8,256,256]{2,1,0:T(8,128)S(1)} %get-tuple-element.16.refs_1_, f32[8,256]{1,0:T(8,128)S(1)} %get-tuple-element.17.refs_2_, f32[8,256,256]{2,1,0:T(8,128)S(1)} %get-tuple-element.19.refs_3_, f32[8,16,256]{2,1,0:T(8,128)S(1)} %collective-permute-done.3.refs_4_, ...), custom_call_target="tpu_custom_call" | custom-call | flops 15728640 | bytes 4194304 | tf_op jit(solution)/shard_map/patch_stats/pallas_call | solution.py:245
  84.2 6.4 %all-to-all-start.2 = ((f32[4,24,256]{2,1,0:T(8,128)}), f32[4,24,256]{2,1,0:T(8,128)S(1)}, u32[]{:S(2)}, u32[]{:S(2)}) async-start(f32[4,24,256]{2,1,0:T(8,128)} %patch_stats.1), calls=%async_computation.2 | async-start | bytes 196608 | tf_op jit(solution)/shard_map/all_to_all | solution.py:20
  90.6 0.0 copy-done.2
  90.6 0.1 reshape.18.refs_1_
  90.7 5.7 %all-to-all-done.2.refs_0_ = f32[4,24,256]{2,1,0:T(8,128)S(1)} async-done(((f32[4,24,256]{2,1,0:T(8,128)}), f32[4,24,256]{2,1,0:T(8,128)S(1)}, u32[]{:S(2)}, u32[]{:S(2)}) %all-to-all-start.2) | async-done | bytes 98336 | tf_op jit(solution)/shard_map/all_to_all | solution.py:20
  96.5 0.7 patch_divergence.1
  97.2 12.3 %all-to-all-start.3 = ((f32[16,1,128]{2,1,0:T(1,128)}), f32[16,1,128]{2,1,0:T(1,128)S(1)}, u32[]{:S(2)}, u32[]{:S(2)}) async-start(f32[16,1,128]{2,1,0:T(1,128)} %get-tuple-element.27), calls=%async_computation.3 | async-start | bytes 16384 | tf_op jit(solution)/shard_map/all_to_all | solution.py:304
  109.4 0.7 reshape.19
  110.2 9.9 %all-to-all-done.3 = f32[16,1,128]{2,1,0:T(1,128)S(1)} async-done(((f32[16,1,128]{2,1,0:T(1,128)}), f32[16,1,128]{2,1,0:T(1,128)S(1)}, u32[]{:S(2)}, u32[]{:S(2)}) %all-to-all-start.3) | async-done | bytes 8224 | tf_op jit(solution)/shard_map/all_to_all | solution.py:304
  120.1 0.6 maximum_divide_fusion
  (7 shorter events, 0.1 us)
Async XLA Ops:
  1.5 14.7 %collective-permute-start = (bf16[168,256]{1,0:T(8,128)(2,1)S(1)}, bf16[168,256]{1,0:T(8,128)(2,1)S(1)}, u32[]{:S(2)}, u32[]{:S(2)}) collective-permute-start(bf16[168,256]{1,0:T(8,128)(2,1)S(1)} %fusion.2), channel_id=1, source_target_pairs={{0,4},{4,0},{8,12},{12,8},{16,20},{20,16},{24,28},{28,24},{32,36},... | collective-permute-start | bytes 258056 | tf_op jit(solution)/shard_map/ppermute | solution.py:30
  18.0 27.1 %all-to-all-start = ((bf16[8,176,256]{2,1,0:T(8,128)(2,1)}), bf16[8,176,256]{2,1,0:T(8,128)(2,1)S(1)}, u32[]{:S(2)}, u32[]{:S(2)}) async-start(bf16[8,176,256]{2,1,0:T(8,128)(2,1)} %broadcast_in_dim.7), calls=%async_computation | async-start | bytes 1441792 | tf_op jit(solution)/shard_map/all_to_all | solution.py:36
  45.9 30.2 %all-to-all-start.1 = ((bf16[8,160,256]{2,1,0:T(8,128)(2,1)}), bf16[8,160,256]{2,1,0:T(8,128)(2,1)S(1)}, u32[]{:S(2)}, u32[]{:S(2)}) async-start(bf16[8,160,256]{2,1,0:T(8,128)(2,1)} %broadcast_in_dim.6), calls=%async_computation.1 | async-start | bytes 1310720 | tf_op jit(solution)/shard_map/all_to_all | solution.py:36
  49.6 2.6 %copy-start = (bf16[8,1,16,16,1408]{4,3,2,1,0:T(8,128)(2,1)S(1)}, bf16[8,1,16,16,1408]{4,3,2,1,0:T(8,128)(2,1)}, u32[]{:S(2)}) copy-start(bf16[8,1,16,16,1408]{4,3,2,1,0:T(8,128)(2,1)} %refs_1_.1) | copy-start | bytes 17301508
  54.6 15.0 %collective-permute-start.1 = (f32[8,16,256]{2,1,0:T(8,128)S(1)}, f32[8,16,256]{2,1,0:T(8,128)S(1)}, u32[]{:S(2)}, u32[]{:S(2)}) collective-permute-start(f32[8,16,256]{2,1,0:T(8,128)S(1)} %get-tuple-element.22), channel_id=1, source_target_pairs={{0,4},{4,0},{1,5},{5,1},{2,6},{6,2},{3,7},{7,3},{8,12},{12,8},{9,1... | collective-permute-start | bytes 393224 | tf_op jit(solution)/shard_map/ppermute | solution.py:51
  61.9 7.7 %collective-permute-start.2 = (f32[8,16,256]{2,1,0:T(8,128)S(1)}, f32[8,16,256]{2,1,0:T(8,128)S(1)}, u32[]{:S(2)}, u32[]{:S(2)}) collective-permute-start(f32[8,16,256]{2,1,0:T(8,128)S(1)} %get-tuple-element.23), channel_id=1, source_target_pairs={{4,8},{8,4},{5,9},{9,5},{6,10},{10,6},{7,11},{11,7},{20,24},{24,20... | collective-permute-start | bytes 393224 | tf_op jit(solution)/shard_map/ppermute | solution.py:51
  70.8 10.2 %collective-permute-start.3 = (f32[8,16,256]{2,1,0:T(8,128)}, f32[8,16,256]{2,1,0:T(8,128)S(1)}, u32[]{:S(2)}, u32[]{:S(2)}) collective-permute-start(f32[8,16,256]{2,1,0:T(8,128)} %get-tuple-element.24), channel_id=1, source_target_pairs={{0,16},{16,0},{1,17},{17,1},{2,18},{18,2},{3,19},{19,3},{4,20},{20... | collective-permute-start | bytes 393224 | tf_op jit(solution)/shard_map/ppermute | solution.py:51
  75.5 5.6 %collective-permute-start.4 = (f32[8,16,256]{2,1,0:T(8,128)S(1)}, f32[8,16,256]{2,1,0:T(8,128)S(1)}, u32[]{:S(2)}, u32[]{:S(2)}) collective-permute-start(f32[8,16,256]{2,1,0:T(8,128)S(1)} %get-tuple-element.25), channel_id=1, source_target_pairs={{16,32},{32,16},{17,33},{33,17},{18,34},{34,18},{19,35},{35,19},{2... | collective-permute-start | bytes 393224 | tf_op jit(solution)/shard_map/ppermute | solution.py:51
  76.2 2.5 %copy-start.1 = (bf16[8,1,16,16,1280]{4,3,2,1,0:T(8,128)(2,1)S(1)}, bf16[8,1,16,16,1280]{4,3,2,1,0:T(8,128)(2,1)}, u32[]{:S(2)}) copy-start(bf16[8,1,16,16,1280]{4,3,2,1,0:T(8,128)(2,1)} %refs_0_.1) | copy-start | bytes 15728644
  78.7 12.0 %copy-start.2 = (s32[8,1,16,16]{3,2,1,0:T(8,128)S(1)}, s32[8,1,16,16]{3,2,1,0:T(8,128)}, u32[]{:S(2)}) copy-start(s32[8,1,16,16]{3,2,1,0:T(8,128)} %param.9) | copy-start | bytes 24580
  84.2 12.3 %all-to-all-start.2 = ((f32[4,24,256]{2,1,0:T(8,128)}), f32[4,24,256]{2,1,0:T(8,128)S(1)}, u32[]{:S(2)}, u32[]{:S(2)}) async-start(f32[4,24,256]{2,1,0:T(8,128)} %patch_stats.1), calls=%async_computation.2 | async-start | bytes 196608 | tf_op jit(solution)/shard_map/all_to_all | solution.py:20
  97.2 22.9 %all-to-all-start.3 = ((f32[16,1,128]{2,1,0:T(1,128)}), f32[16,1,128]{2,1,0:T(1,128)S(1)}, u32[]{:S(2)}, u32[]{:S(2)}) async-start(f32[16,1,128]{2,1,0:T(1,128)} %get-tuple-element.27), calls=%async_computation.3 | async-start | bytes 16384 | tf_op jit(solution)/shard_map/all_to_all | solution.py:304
